TPU v7x, 32 devices: a whole 2x2x4 slice. The times are simulated.
32 devices in a mesh: rep: 4 (over y, x), fsdp: 8 (over z, core).
Axes of the slice: x: 2, y: 2, z: 4, core: 2. Of those that a mesh axis runs over, the one named last changes fastest.
Arguments:
- windows: bfloat16 [12544, 768], P(('rep', 'fsdp')), may hold values from -6 to 6
- slot_table: int32 [64], P(('rep', 'fsdp')), may hold values from 0 to 25, as said below
- cotangent: bfloat16 [12544, 768], P(('rep', 'fsdp')), may hold values from -6 to 6
- qkv_weight: bfloat16 [2, 768, 2304], P(None, 'fsdp'), may hold values from -0.21875 to 0.21875
- qv_bias: bfloat16 [2, 1536], P(None, 'fsdp'), may hold values from -1.1953125 to 1.1953125
- proj_weight: bfloat16 [2, 768, 768], P(None, 'fsdp'), may hold values from -0.875 to 0.875
- proj_bias: bfloat16 [2, 768], P(None, 'fsdp'), may hold values from -1.1953125 to 1.1953125
- norm1_gain: bfloat16 [2, 768], P(None, 'fsdp'), may hold values from 0.5 to 1.5
- norm1_bias: bfloat16 [2, 768], P(None, 'fsdp'), may hold values from -1.1953125 to 1.1953125
- norm2_gain: bfloat16 [2, 768], P(None, 'fsdp'), may hold values from 0.5 to 1.5
- norm2_bias: bfloat16 [2, 768], P(None, 'fsdp'), may hold values from -1.1953125 to 1.1953125
- fc1_weight: bfloat16 [2, 768, 3072], P(None, 'fsdp'), may hold values from -0.21875 to 0.21875
- fc1_bias: bfloat16 [2, 3072], P(None, 'fsdp'), may hold values from -1.1953125 to 1.1953125
- fc2_weight: bfloat16 [2, 3072, 768], P(None, 'fsdp'), may hold values from -0.109375 to 0.109375
- fc2_bias: bfloat16 [2, 768], P(None, 'fsdp'), may hold values from -1.1953125 to 1.1953125
- rel_height: bfloat16 [2, 1728], P(None, 'fsdp'), may hold values from -0.59765625 to 0.59765625
- rel_width: bfloat16 [2, 1728], P(None, 'fsdp'), may hold values from -0.59765625 to 0.59765625
Outputs:
- output: bfloat16 [12544, 768], P(('rep', 'fsdp'))
- input_grad: bfloat16 [12544, 768], P(('rep', 'fsdp'))
- qkv_weight_grad: float32 [2, 768, 2304], P(None, 'fsdp')
- qv_bias_grad: float32 [2, 1536], P(None, 'fsdp')
- proj_weight_grad: float32 [2, 768, 768], P(None, 'fsdp')
- proj_bias_grad: float32 [2, 768], P(None, 'fsdp')
- norm1_gain_grad: float32 [2, 768], P(None, 'fsdp')
- norm1_bias_grad: float32 [2, 768], P(None, 'fsdp')
- norm2_gain_grad: float32 [2, 768], P(None, 'fsdp')
- norm2_bias_grad: float32 [2, 768], P(None, 'fsdp')
- fc1_weight_grad: float32 [2, 768, 3072], P(None, 'fsdp')
- fc1_bias_grad: float32 [2, 3072], P(None, 'fsdp')
- fc2_weight_grad: float32 [2, 3072, 768], P(None, 'fsdp')
- fc2_bias_grad: float32 [2, 768], P(None, 'fsdp')
- rel_height_grad: float32 [2, 1728], P(None, 'fsdp')
- rel_width_grad: float32 [2, 1728], P(None, 'fsdp')
Inputs may be any that keep to these rules, and one draw needn't show every extreme that they name: `slot_table`: entries 0 to 24 name a window's place in its image's 5 x 5 grid of windows, row by row; 25 marks an empty slot. Within each replica group the k-th window in order (images one after the other, each with all its windows in order, the last one possibly cut) stands on fsdp index k % 8 in its slot k // 8; each group fills at least half of its 16 slots and leaves at least one empty.
All inputs are finite; a program needn't handle non-finite values.
Results may differ from a plain program's by a relative error of at most 0.025.
Values may be sent and summed in bfloat16 or wider, within the bound.
No kernel may reach another device: no remote copies, remote signals or barrier semaphores. Data moves between devices by JAX's collectives and lax.ppermute only.
A program may use at most 256 MiB of HBM per device.

v0:
```python
import jax
import jax.numpy as jnp
from jax import lax
from jax.sharding import PartitionSpec as P

HEADS = 12
HD = 64
WINDOW = 14
SIDE = 64
LAYERS = 2
GRID = 5


HIGHEST = lax.Precision.HIGHEST
EPSILON = 1e-06


def norm_stats(values):
    centre = jnp.mean(values, -1, keepdims=True)
    centered = values - centre
    spread = jnp.mean(centered * centered, -1, keepdims=True)
    inverse = lax.rsqrt(spread + EPSILON)
    return (centered * inverse, inverse)


def norm_back(grad_normed, normed, inverse, gain):
    scaled = grad_normed * gain
    return inverse * (
        scaled
        - jnp.mean(scaled, -1, keepdims=True)
        - normed * jnp.mean(scaled * normed, -1, keepdims=True)
    )


def relative_rows(table_flat):
    table_rows = table_flat.reshape(2 * WINDOW - 1, HD)
    places = jnp.arange(WINDOW, dtype=jnp.int32)
    offsets = places[:, None] - places[None, :] + WINDOW - 1
    one_hot = (
        offsets[:, :, None] == jnp.arange(2 * WINDOW - 1, dtype=jnp.int32)[None, None, :]
    ).astype(jnp.float32)
    return (jnp.einsum("ikr,re->ike", one_hot, table_rows, precision=HIGHEST), one_hot)


def window_mask(slot_table):
    places = jnp.arange(WINDOW, dtype=jnp.int32)
    rows_inside = slot_table[:, None] // GRID * WINDOW + places[None, :] < SIDE
    cols_inside = slot_table[:, None] % GRID * WINDOW + places[None, :] < SIDE
    both_inside = rows_inside[:, :, None] & cols_inside[:, None, :]
    return both_inside.astype(jnp.float32).reshape(slot_table.shape[0], WINDOW * WINDOW)


def layer_forward(tokens, live_mask, layer_weights):
    (
        qkv_weight,
        qv_bias,
        proj_weight,
        proj_bias,
        norm1_gain,
        norm1_bias,
        norm2_gain,
        norm2_bias,
        fc1_weight,
        fc1_bias,
        fc2_weight,
        fc2_bias,
        rel_height,
        rel_width,
    ) = layer_weights
    slot_count = tokens.shape[0]
    model_width = tokens.shape[2]
    window_span = WINDOW * WINDOW
    total_rows = slot_count * window_span
    live_rows = live_mask[:, :, None]
    first_normed, first_inverse = norm_stats(tokens)
    first_gain = norm1_gain.astype(jnp.float32)
    normed_in = (first_normed * first_gain + norm1_bias.astype(jnp.float32)) * live_rows
    normed_in = normed_in.astype(jnp.bfloat16).reshape(total_rows, model_width)
    projected = jnp.dot(normed_in, qkv_weight, preferred_element_type=jnp.float32)
    bias_pair = qv_bias.astype(jnp.float32)
    query_rows = (projected[:, :model_width] + bias_pair[:model_width]).astype(jnp.bfloat16)
    key_rows = projected[:, model_width : 2 * model_width].astype(jnp.bfloat16)
    value_rows = (projected[:, 2 * model_width :] + bias_pair[model_width:]).astype(jnp.bfloat16)
    query_rows = query_rows.reshape(slot_count, window_span, HEADS, HD)
    key_rows = key_rows.reshape(slot_count, window_span, HEADS, HD)
    value_rows = value_rows.reshape(slot_count, window_span, HEADS, HD)
    heights, one_hot = relative_rows(rel_height.astype(jnp.float32))
    widths, one_hot = relative_rows(rel_width.astype(jnp.float32))
    query_grid = query_rows.astype(jnp.float32).reshape(slot_count, WINDOW, WINDOW, HEADS, HD)
    along_height = jnp.einsum("bijhe,ike->bhijk", query_grid, heights, precision=HIGHEST)
    along_width = jnp.einsum("bijhe,jke->bhijk", query_grid, widths, precision=HIGHEST)
    products = jnp.einsum(
        "bshe,bthe->bhst", query_rows, key_rows, preferred_element_type=jnp.float32
    ) * HD ** (-0.5)
    scores = products.reshape(slot_count, HEADS, WINDOW, WINDOW, WINDOW, WINDOW)
    scores = scores + along_height[..., None] + along_width[..., None, :]
    scores = scores.reshape(slot_count, HEADS, window_span, window_span)
    row_top = jnp.max(scores, -1, keepdims=True)
    shifted = jnp.exp(scores - row_top)
    probabilities = shifted / jnp.sum(shifted, -1, keepdims=True)
    probs_low = probabilities.astype(jnp.bfloat16)
    attended = jnp.einsum(
        "bhst,bthe->bshe", probs_low, value_rows, preferred_element_type=jnp.float32
    )
    attended = attended.astype(jnp.bfloat16).reshape(total_rows, model_width)
    branch = jnp.dot(attended, proj_weight, preferred_element_type=jnp.float32) + proj_bias.astype(
        jnp.float32
    )
    middle = tokens + live_rows * branch.reshape(slot_count, window_span, model_width)
    second_normed, second_inverse = norm_stats(middle)
    second_gain = norm2_gain.astype(jnp.float32)
    hidden_in = (second_normed * second_gain + norm2_bias.astype(jnp.float32)).astype(jnp.bfloat16)
    hidden_in = hidden_in.reshape(total_rows, model_width)
    hidden = jnp.dot(hidden_in, fc1_weight, preferred_element_type=jnp.float32) + fc1_bias.astype(
        jnp.float32
    )
    activated = jax.nn.gelu(hidden, approximate=False).astype(jnp.bfloat16)
    mlp_out = jnp.dot(activated, fc2_weight, preferred_element_type=jnp.float32) + fc2_bias.astype(
        jnp.float32
    )
    result = middle + live_rows * mlp_out.reshape(slot_count, window_span, model_width)
    kept_values = (
        first_normed,
        first_inverse,
        first_gain,
        normed_in,
        query_rows,
        key_rows,
        value_rows,
        query_grid,
        heights,
        widths,
        one_hot,
        probabilities,
        probs_low,
        attended,
        second_normed,
        second_inverse,
        second_gain,
        hidden_in,
        hidden,
        activated,
    )
    return (result, kept_values)


def layer_backward(tokens, live_mask, layer_weights, grad_out):
    (
        qkv_weight,
        qv_bias,
        proj_weight,
        proj_bias,
        norm1_gain,
        norm1_bias,
        norm2_gain,
        norm2_bias,
        fc1_weight,
        fc1_bias,
        fc2_weight,
        fc2_bias,
        rel_height,
        rel_width,
    ) = layer_weights
    unused_result, kept_values = layer_forward(tokens, live_mask, layer_weights)
    (
        first_normed,
        first_inverse,
        first_gain,
        normed_in,
        query_rows,
        key_rows,
        value_rows,
        query_grid,
        heights,
        widths,
        one_hot,
        probabilities,
        probs_low,
        attended,
        second_normed,
        second_inverse,
        second_gain,
        hidden_in,
        hidden,
        activated,
    ) = kept_values
    slot_count = tokens.shape[0]
    model_width = tokens.shape[2]
    window_span = WINDOW * WINDOW
    total_rows = slot_count * window_span
    live_rows = live_mask[:, :, None]
    grad_mlp = (live_rows * grad_out).reshape(total_rows, model_width).astype(jnp.bfloat16)
    grad_fc2 = jnp.einsum("rf,rd->fd", activated, grad_mlp, preferred_element_type=jnp.float32)
    grad_fc2_bias = jnp.sum(grad_mlp.astype(jnp.float32), 0)
    grad_activated = jnp.einsum(
        "rd,fd->rf", grad_mlp, fc2_weight, preferred_element_type=jnp.float32
    )
    unused_gelu, gelu_pull = jax.vjp(
        lambda inner_value: jax.nn.gelu(inner_value, approximate=False), hidden
    )
    grad_hidden = gelu_pull(grad_activated)[0].astype(jnp.bfloat16)
    grad_fc1 = jnp.einsum("rd,rf->df", hidden_in, grad_hidden, preferred_element_type=jnp.float32)
    grad_fc1_bias = jnp.sum(grad_hidden.astype(jnp.float32), 0)
    grad_second = jnp.einsum(
        "rf,df->rd", grad_hidden, fc1_weight, preferred_element_type=jnp.float32
    )
    grad_second = grad_second.reshape(slot_count, window_span, model_width)
    grad_second_gain = jnp.sum(grad_second * second_normed, (0, 1))
    grad_second_shift = jnp.sum(grad_second, (0, 1))
    grad_middle = grad_out + norm_back(grad_second, second_normed, second_inverse, second_gain)
    grad_branch = (live_rows * grad_middle).reshape(total_rows, model_width).astype(jnp.bfloat16)
    grad_proj = jnp.einsum("rd,re->de", attended, grad_branch, preferred_element_type=jnp.float32)
    grad_proj_bias = jnp.sum(grad_branch.astype(jnp.float32), 0)
    grad_attended = jnp.einsum(
        "re,de->rd", grad_branch, proj_weight, preferred_element_type=jnp.float32
    )
    grad_attended = grad_attended.astype(jnp.bfloat16).reshape(slot_count, window_span, HEADS, HD)
    grad_values = jnp.einsum(
        "bhst,bshe->bthe", probs_low, grad_attended, preferred_element_type=jnp.float32
    )
    grad_probs = jnp.einsum(
        "bshe,bthe->bhst", grad_attended, value_rows, preferred_element_type=jnp.float32
    )
    grad_scores = probabilities * (
        grad_probs - jnp.sum(grad_probs * probabilities, -1, keepdims=True)
    )
    grad_scores = grad_scores.astype(jnp.bfloat16)
    grad_queries = jnp.einsum(
        "bhst,bthe->bshe", grad_scores, key_rows, preferred_element_type=jnp.float32
    ) * HD ** (-0.5)
    grad_keys = jnp.einsum(
        "bhst,bshe->bthe", grad_scores, query_rows, preferred_element_type=jnp.float32
    ) * HD ** (-0.5)
    score_grid = grad_scores.astype(jnp.float32).reshape(
        slot_count, HEADS, WINDOW, WINDOW, WINDOW, WINDOW
    )
    grad_along_height = jnp.sum(score_grid, -1)
    grad_along_width = jnp.sum(score_grid, -2)
    relative_part = jnp.einsum(
        "bhijk,ike->bijhe", grad_along_height, heights, precision=HIGHEST
    ) + jnp.einsum("bhijk,jke->bijhe", grad_along_width, widths, precision=HIGHEST)
    grad_queries = grad_queries + relative_part.reshape(slot_count, window_span, HEADS, HD)
    grad_heights = jnp.einsum("bhijk,bijhe->ike", grad_along_height, query_grid, precision=HIGHEST)
    grad_widths = jnp.einsum("bhijk,bijhe->jke", grad_along_width, query_grid, precision=HIGHEST)
    grad_rel_height = jnp.einsum("ikr,ike->re", one_hot, grad_heights, precision=HIGHEST).reshape(
        -1
    )
    grad_rel_width = jnp.einsum("ikr,ike->re", one_hot, grad_widths, precision=HIGHEST).reshape(-1)
    low_queries = grad_queries.reshape(total_rows, model_width).astype(jnp.bfloat16)
    low_keys = grad_keys.reshape(total_rows, model_width).astype(jnp.bfloat16)
    low_values = grad_values.reshape(total_rows, model_width).astype(jnp.bfloat16)
    grad_projected = jnp.concatenate([low_queries, low_keys, low_values], 1)
    grad_qkv = jnp.einsum(
        "rd,re->de", normed_in, grad_projected, preferred_element_type=jnp.float32
    )
    grad_qv_bias = jnp.concatenate(
        [jnp.sum(low_queries.astype(jnp.float32), 0), jnp.sum(low_values.astype(jnp.float32), 0)]
    )
    grad_first = jnp.einsum(
        "re,de->rd", grad_projected, qkv_weight, preferred_element_type=jnp.float32
    )
    grad_first = grad_first.reshape(slot_count, window_span, model_width) * live_rows
    grad_first_gain = jnp.sum(grad_first * first_normed, (0, 1))
    grad_first_shift = jnp.sum(grad_first, (0, 1))
    grad_tokens = grad_middle + norm_back(grad_first, first_normed, first_inverse, first_gain)
    layer_terms = (
        grad_qkv,
        grad_qv_bias,
        grad_proj,
        grad_proj_bias,
        grad_first_gain,
        grad_first_shift,
        grad_second_gain,
        grad_second_shift,
        grad_fc1,
        grad_fc1_bias,
        grad_fc2,
        grad_fc2_bias,
        grad_rel_height,
        grad_rel_width,
    )
    return (layer_terms, grad_tokens)


def on_device(
    windows,
    slot_table,
    cotangent,
    qkv_weight,
    qv_bias,
    proj_weight,
    proj_bias,
    norm1_gain,
    norm1_bias,
    norm2_gain,
    norm2_bias,
    fc1_weight,
    fc1_bias,
    fc2_weight,
    fc2_bias,
    rel_height,
    rel_width,
):
    model_width = windows.shape[1]
    slot_count = slot_table.shape[0]
    window_span = WINDOW * WINDOW
    live_mask = window_mask(slot_table)
    layer_inputs = []
    kept_weights = []
    current = windows.astype(jnp.float32).reshape(slot_count, window_span, model_width)
    for layer_index in range(LAYERS):
        gathered = (
            lax.all_gather(qkv_weight[layer_index], "fsdp", axis=0, tiled=True),
            lax.all_gather(qv_bias[layer_index], "fsdp", axis=0, tiled=True),
            lax.all_gather(proj_weight[layer_index], "fsdp", axis=0, tiled=True),
            lax.all_gather(proj_bias[layer_index], "fsdp", axis=0, tiled=True),
            lax.all_gather(norm1_gain[layer_index], "fsdp", axis=0, tiled=True),
            lax.all_gather(norm1_bias[layer_index], "fsdp", axis=0, tiled=True),
            lax.all_gather(norm2_gain[layer_index], "fsdp", axis=0, tiled=True),
            lax.all_gather(norm2_bias[layer_index], "fsdp", axis=0, tiled=True),
            lax.all_gather(fc1_weight[layer_index], "fsdp", axis=0, tiled=True),
            lax.all_gather(fc1_bias[layer_index], "fsdp", axis=0, tiled=True),
            lax.all_gather(fc2_weight[layer_index], "fsdp", axis=0, tiled=True),
            lax.all_gather(fc2_bias[layer_index], "fsdp", axis=0, tiled=True),
            lax.all_gather(rel_height[layer_index], "fsdp", axis=0, tiled=True),
            lax.all_gather(rel_width[layer_index], "fsdp", axis=0, tiled=True),
        )
        kept_weights.append(gathered)
        layer_inputs.append(current)
        current, unused_kept = layer_forward(current, live_mask, gathered)
    output = current.reshape(slot_count * window_span, model_width).astype(jnp.bfloat16)
    grad_current = cotangent.astype(jnp.float32).reshape(slot_count, window_span, model_width)
    layer_sums = [None] * LAYERS
    for layer_index in reversed(range(LAYERS)):
        gathered = (
            lax.all_gather(qkv_weight[layer_index], "fsdp", axis=0, tiled=True),
            lax.all_gather(qv_bias[layer_index], "fsdp", axis=0, tiled=True),
            lax.all_gather(proj_weight[layer_index], "fsdp", axis=0, tiled=True),
            lax.all_gather(proj_bias[layer_index], "fsdp", axis=0, tiled=True),
            lax.all_gather(norm1_gain[layer_index], "fsdp", axis=0, tiled=True),
            lax.all_gather(norm1_bias[layer_index], "fsdp", axis=0, tiled=True),
            lax.all_gather(norm2_gain[layer_index], "fsdp", axis=0, tiled=True),
            lax.all_gather(norm2_bias[layer_index], "fsdp", axis=0, tiled=True),
            lax.all_gather(fc1_weight[layer_index], "fsdp", axis=0, tiled=True),
            lax.all_gather(fc1_bias[layer_index], "fsdp", axis=0, tiled=True),
            lax.all_gather(fc2_weight[layer_index], "fsdp", axis=0, tiled=True),
            lax.all_gather(fc2_bias[layer_index], "fsdp", axis=0, tiled=True),
            lax.all_gather(rel_height[layer_index], "fsdp", axis=0, tiled=True),
            lax.all_gather(rel_width[layer_index], "fsdp", axis=0, tiled=True),
        )
        terms, grad_current = layer_backward(
            layer_inputs[layer_index], live_mask, gathered, grad_current
        )
        scattered = (
            lax.psum_scatter(
                terms[0].astype(jnp.bfloat16), "fsdp", scatter_dimension=0, tiled=True
            ).astype(jnp.float32),
            lax.psum_scatter(
                terms[1].astype(jnp.bfloat16), "fsdp", scatter_dimension=0, tiled=True
            ).astype(jnp.float32),
            lax.psum_scatter(
                terms[2].astype(jnp.bfloat16), "fsdp", scatter_dimension=0, tiled=True
            ).astype(jnp.float32),
            lax.psum_scatter(
                terms[3].astype(jnp.bfloat16), "fsdp", scatter_dimension=0, tiled=True
            ).astype(jnp.float32),
            lax.psum_scatter(
                terms[4].astype(jnp.bfloat16), "fsdp", scatter_dimension=0, tiled=True
            ).astype(jnp.float32),
            lax.psum_scatter(
                terms[5].astype(jnp.bfloat16), "fsdp", scatter_dimension=0, tiled=True
            ).astype(jnp.float32),
            lax.psum_scatter(
                terms[6].astype(jnp.bfloat16), "fsdp", scatter_dimension=0, tiled=True
            ).astype(jnp.float32),
            lax.psum_scatter(
                terms[7].astype(jnp.bfloat16), "fsdp", scatter_dimension=0, tiled=True
            ).astype(jnp.float32),
            lax.psum_scatter(
                terms[8].astype(jnp.bfloat16), "fsdp", scatter_dimension=0, tiled=True
            ).astype(jnp.float32),
            lax.psum_scatter(
                terms[9].astype(jnp.bfloat16), "fsdp", scatter_dimension=0, tiled=True
            ).astype(jnp.float32),
            lax.psum_scatter(
                terms[10].astype(jnp.bfloat16), "fsdp", scatter_dimension=0, tiled=True
            ).astype(jnp.float32),
            lax.psum_scatter(
                terms[11].astype(jnp.bfloat16), "fsdp", scatter_dimension=0, tiled=True
            ).astype(jnp.float32),
            lax.psum_scatter(
                terms[12].astype(jnp.bfloat16), "fsdp", scatter_dimension=0, tiled=True
            ).astype(jnp.float32),
            lax.psum_scatter(
                terms[13].astype(jnp.bfloat16), "fsdp", scatter_dimension=0, tiled=True
            ).astype(jnp.float32),
        )
        layer_sums[layer_index] = (
            lax.psum(scattered[0].astype(jnp.bfloat16), "rep").astype(jnp.float32),
            lax.psum(scattered[1].astype(jnp.bfloat16), "rep").astype(jnp.float32),
            lax.psum(scattered[2].astype(jnp.bfloat16), "rep").astype(jnp.float32),
            lax.psum(scattered[3].astype(jnp.bfloat16), "rep").astype(jnp.float32),
            lax.psum(scattered[4].astype(jnp.bfloat16), "rep").astype(jnp.float32),
            lax.psum(scattered[5].astype(jnp.bfloat16), "rep").astype(jnp.float32),
            lax.psum(scattered[6].astype(jnp.bfloat16), "rep").astype(jnp.float32),
            lax.psum(scattered[7].astype(jnp.bfloat16), "rep").astype(jnp.float32),
            lax.psum(scattered[8].astype(jnp.bfloat16), "rep").astype(jnp.float32),
            lax.psum(scattered[9].astype(jnp.bfloat16), "rep").astype(jnp.float32),
            lax.psum(scattered[10].astype(jnp.bfloat16), "rep").astype(jnp.float32),
            lax.psum(scattered[11].astype(jnp.bfloat16), "rep").astype(jnp.float32),
            lax.psum(scattered[12].astype(jnp.bfloat16), "rep").astype(jnp.float32),
            lax.psum(scattered[13].astype(jnp.bfloat16), "rep").astype(jnp.float32),
        )
    stacked = [
        jnp.stack([layer_sums[layer_index][member] for layer_index in range(LAYERS)])
        for member in range(14)
    ]
    input_grad = grad_current.reshape(slot_count * window_span, model_width).astype(jnp.bfloat16)
    return (
        output,
        input_grad,
        stacked[0],
        stacked[1],
        stacked[2],
        stacked[3],
        stacked[4],
        stacked[5],
        stacked[6],
        stacked[7],
        stacked[8],
        stacked[9],
        stacked[10],
        stacked[11],
        stacked[12],
        stacked[13],
    )


def solution(mesh):
    placed = (
        P(("rep", "fsdp"), None),
        P(("rep", "fsdp")),
        P(("rep", "fsdp"), None),
        P(None, "fsdp", None),
        P(None, "fsdp"),
        P(None, "fsdp", None),
        P(None, "fsdp"),
        P(None, "fsdp"),
        P(None, "fsdp"),
        P(None, "fsdp"),
        P(None, "fsdp"),
        P(None, "fsdp", None),
        P(None, "fsdp"),
        P(None, "fsdp", None),
        P(None, "fsdp"),
        P(None, "fsdp"),
        P(None, "fsdp"),
    )
    return jax.shard_map(
        on_device,
        mesh=mesh,
        in_specs=placed,
        out_specs=(
            P(("rep", "fsdp"), None),
            P(("rep", "fsdp"), None),
            P(None, "fsdp", None),
            P(None, "fsdp"),
            P(None, "fsdp", None),
            P(None, "fsdp"),
            P(None, "fsdp"),
            P(None, "fsdp"),
            P(None, "fsdp"),
            P(None, "fsdp"),
            P(None, "fsdp", None),
            P(None, "fsdp"),
            P(None, "fsdp", None),
            P(None, "fsdp"),
            P(None, "fsdp"),
            P(None, "fsdp"),
        ),
        check_vma=False,
    )
```

profile of v0, /device:TPU:8, one launch (start us, length us, event | category | flops | bytes accessed | tf_op | source)
XLA Modules:
  0.0 1042.7 jit_solution(16605571947465691046)
XLA Ops:
  24.1 26.8 %all-reduce.39 = (bf16[768]{0:T(1024)(128)(2,1)S(1)}, bf16[768]{0:T(1024)(128)(2,1)S(1)}, bf16[1536]{0:T(1024)(128)(2,1)S(1)}, bf16[1728]{0:T(1024)(128)(2,1)S(1...) all-reduce(bf16[768]{0:T(1024)(128)(2,1)S(1)} %dynamic-update-slice, ...), channel_id=3, replica_groups=mesh['rep'=4,'fsdp'=8] {'fsdp'}, use_global_device_ids=true, to_apply=%add.1 | all-reduce | flops 18432 | bytes 73728
  56.1 13.6 %all-gather.25 = bf16[1,3072]{1,0:T(2,128)(2,1)S(1)} all-gather(bf16[1,384]{1,0:T(2,128)(2,1)S(1)} %get-tuple-element.138), channel_id=27, replica_groups=mesh['rep'=4,'fsdp'=8] {'fsdp'}, dimensions={1}, use_global_device_ids=true | all-gather | bytes 6912 | tf_op jit(solution)/shard_map/all_gather | solution.py:322
  70.4 12.7 %all-gather.11 = bf16[1,3072]{1,0:T(2,128)(2,1)S(1)} all-gather(bf16[1,384]{1,0:T(2,128)(2,1)S(1)} %get-tuple-element.139), channel_id=13, replica_groups=mesh['rep'=4,'fsdp'=8] {'fsdp'}, dimensions={1}, use_global_device_ids=true | all-gather | bytes 6912 | tf_op jit(solution)/shard_map/all_gather | solution.py:322
  109.4 11.3 %convolution_bitcast_fusion.2 = f32[2,12,14,14,14]{2,4,1,0,3:T(8,128)} fusion(f32[14,14,64,1,1]{2,1,4,3,0:T(8,128)S(1)} %copy-done.45, bf16[2,14,14,12,64]{4,3,2,1,0:T(8,128)(2,1)S(1)} %reshape.710), kind=kOutput, calls=%fused_computation.95 | convolution fusion | flops 50577408 | bytes 915712 | tf_op jit(solution)/shard_map/bijhe,jke->bhijk/dot_general | solution.py:91
  141.1 13.2 %add.539 = f32[2,12,14,14,14,14]{5,4,3,2,1,0:T(8,128)} broadcast(f32[2,12,14,14,14]{4,3,2,1,0:T(8,128)S(1)} %copy.135), dimensions={0,1,2,3,4} | broadcast | bytes 3951360 | tf_op jit(solution)/shard_map/add | solution.py:96
  154.3 23.6 %add.540 = f32[2,12,196,196]{3,2,1,0:T(8,128)} reshape(f32[2,12,14,14,14,14]{5,4,3,2,1,0:T(8,128)} %add.539) | data formatting | bytes 7375872 | tf_op jit(solution)/shard_map/add | solution.py:96
  184.0 12.8 %add.542 = f32[2,12,14,14,14,14]{5,4,3,2,1,0:T(8,128)} broadcast(f32[2,12,14,14,14]{4,3,2,1,0:T(8,128)S(1)} %copy-done.10), dimensions={0,1,2,3,5} | broadcast | bytes 3951360 | tf_op jit(solution)/shard_map/add | solution.py:96
  196.8 23.5 %add.543 = f32[2,12,196,196]{3,2,1,0:T(8,128)} reshape(f32[2,12,14,14,14,14]{5,4,3,2,1,0:T(8,128)} %add.542) | data formatting | bytes 7375872 | tf_op jit(solution)/shard_map/add | solution.py:96
  245.4 15.9 %multiply_convert_fusion.3 = (bf16[392,3072]{1,0:T(8,128)(2,1)}, f32[392,3072]{1,0:T(8,128)}, f32[392,3072]{1,0:T(8,128)}) fusion(f32[3072]{0:T(1024)S(1)} %bitcast.328, bf16[1,768,3072]{2,1,0:T(8,128)(2,1)} %all-gather.41.cloned.1.call-done, f32[392,768]{1,0:T(8,128)S(1)} %get-tuple-element.159, f32[768]{0:T(1024)S(1)} %copy-done.102, ...), kind=kOutput, calls=%fused_computation.35 | convolution fusion | flops 1930672128 | bytes 17986624 | tf_op jit(solution)/shard_map/dot_general | solution.py:114
  320.3 13.2 %add.563 = f32[2,12,14,14,14,14]{5,4,3,2,1,0:T(8,128)} broadcast(f32[2,12,14,14,14]{4,3,2,1,0:T(8,128)S(1)} %copy.149), dimensions={0,1,2,3,4} | broadcast | bytes 3951360 | tf_op jit(solution)/shard_map/add | solution.py:96
  333.5 23.4 %add.564 = f32[2,12,196,196]{3,2,1,0:T(8,128)} reshape(f32[2,12,14,14,14,14]{5,4,3,2,1,0:T(8,128)} %add.563) | data formatting | bytes 7375872 | tf_op jit(solution)/shard_map/add | solution.py:96
  363.0 12.7 %add.566 = f32[2,12,14,14,14,14]{5,4,3,2,1,0:T(8,128)} broadcast(f32[2,12,14,14,14]{4,3,2,1,0:T(8,128)S(1)} %copy-done.11), dimensions={0,1,2,3,5} | broadcast | bytes 3951360 | tf_op jit(solution)/shard_map/add | solution.py:96
  375.7 23.3 %add.567 = f32[2,12,196,196]{3,2,1,0:T(8,128)} reshape(f32[2,12,14,14,14,14]{5,4,3,2,1,0:T(8,128)} %add.566) | data formatting | bytes 7375872 | tf_op jit(solution)/shard_map/add | solution.py:96
  425.9 15.8 %multiply_convert_fusion.2 = (bf16[392,3072]{1,0:T(8,128)(2,1)}, f32[392,3072]{1,0:T(8,128)}, f32[392,3072]{1,0:T(8,128)}) fusion(f32[3072]{0:T(1024)S(1)} %bitcast.330, bf16[1,768,3072]{2,1,0:T(8,128)(2,1)} %all-gather.49.cloned.1.call-done, f32[392,768]{1,0:T(8,128)S(1)} %get-tuple-element.166, f32[768]{0:T(1024)S(1)} %copy-done.106, ...), kind=kOutput, calls=%fused_computation.22 | convolution fusion | flops 1930672128 | bytes 17986624 | tf_op jit(solution)/shard_map/dot_general | solution.py:114
  491.6 22.8 %reshape.730 = f32[2,12,14,14,14,14]{5,4,3,2,1,0:T(8,128)} reshape(f32[2,12,196,196]{3,2,1,0:T(8,128)} %copy.162) | data formatting | bytes 7375872 | tf_op jit(solution)/shard_map/reshape | solution.py:234
  514.4 16.5 %fusion.169 = (f32[2,12,14,14,14]{4,3,2,1,0:T(8,128)}, f32[2,12,14,14,14]{4,3,2,1,0:T(8,128)S(1)}) fusion(f32[2,12,14,14,14,14]{5,4,3,2,1,0:T(8,128)} %reshape.730), kind=kLoop, calls=%fused_computation.307 | loop fusion | flops 1712256 | bytes 4214784 | tf_op jit(solution)/shard_map/reduce_sum | solution.py:237
  598.4 22.8 %reshape.732 = f32[2,12,14,14,14,14]{5,4,3,2,1,0:T(8,128)} reshape(f32[2,12,196,196]{3,2,1,0:T(8,128)} %copy.180) | data formatting | bytes 7375872 | tf_op jit(solution)/shard_map/reshape | solution.py:234
  621.2 16.5 %fusion.168 = (f32[2,12,14,14,14]{4,3,2,1,0:T(8,128)}, f32[2,12,14,14,14]{4,3,2,1,0:T(8,128)S(1)}) fusion(f32[2,12,14,14,14,14]{5,4,3,2,1,0:T(8,128)} %reshape.732), kind=kLoop, calls=%fused_computation.306 | loop fusion | flops 1712256 | bytes 4214784 | tf_op jit(solution)/shard_map/reduce_sum | solution.py:237
  722.1 28.0 %all-reduce.38 = (bf16[768]{0:T(1024)(128)(2,1)S(1)}, bf16[1536]{0:T(1024)(128)(2,1)S(1)}, bf16[1536]{0:T(1024)(128)(2,1)S(1)}, bf16[768]{0:T(1024)(128)(2,1)S(1...) all-reduce(bf16[768]{0:T(1024)(128)(2,1)S(1)} %dynamic-update-slice, ...), channel_id=29, replica_groups=mesh['rep'=4,'fsdp'=8] {'fsdp'}, use_global_device_ids=true, to_apply=%add.17 | all-reduce | flops 26112 | bytes 104448
  761.1 55.5 %reduce-scatter.23.cloned.1.call-done = bf16[384,768]{1,0:T(8,128)(2,1)} async-done(((bf16[3072,768]{1,0:T(8,128)(2,1)}), bf16[384,768]{1,0:T(8,128)(2,1)}) %reduce-scatter.23.cloned.1.call-update) | async-done | bytes 589840 | tf_op jit(solution)/shard_map/reduce_scatter | solution.py:385
  816.6 55.5 %reduce-scatter.17.cloned.1.call-done = bf16[96,3072]{1,0:T(8,128)(2,1)} async-done(((bf16[768,3072]{1,0:T(8,128)(2,1)}), bf16[96,3072]{1,0:T(8,128)(2,1)}) %reduce-scatter.17.cloned.1.call-update) | async-done | bytes 589840 | tf_op jit(solution)/shard_map/reduce_scatter | solution.py:379
  872.1 55.5 %reduce-scatter.21.cloned.1.call-done = bf16[384,768]{1,0:T(8,128)(2,1)} async-done(((bf16[3072,768]{1,0:T(8,128)(2,1)}), bf16[384,768]{1,0:T(8,128)(2,1)}) %reduce-scatter.21.cloned.1.call-update) | async-done | bytes 589840 | tf_op jit(solution)/shard_map/reduce_scatter | solution.py:385
  928.4 16.8 %all-reduce.40 = (bf16[1,192]{1,0:T(2,128)(2,1)S(1)}, bf16[1,192]{1,0:T(2,128)(2,1)S(1)}, bf16[1,96]{1,0:T(2,128)(2,1)S(1)}, bf16[1,96]{1,0:T(2,128)(2,1)S(1)}, ...) all-reduce(bf16[1,192]{1,0:T(2,128)(2,1)S(1)} %stack.201, ...), channel_id=1, replica_groups=mesh['rep'=4,'fsdp'=8] {'rep'}, use_global_device_ids=true, to_apply=%region_37.38 | all-reduce | flops 3168 | bytes 12672 | tf_op jit(solution)/shard_map/psum | solution.py:400
  958.8 69.5 %all-reduce.44.cloned.1.call-done = (bf16[1,96,2304]{2,1,0:T(8,128)(2,1)}, bf16[1,96,2304]{2,1,0:T(8,128)(2,1)}, bf16[1,96,768]{2,1,0:T(8,128)(2,1)}, bf16[1,96,...) async-done(((bf16[1,96,2304]{2,1,0:T(8,128)(2,1)}, ...) | async-done | bytes 3538960 | tf_op jit(solution)/shard_map/psum | solution.py:399
  (610 shorter events, 420.5 us)
Async XLA Ops:
  7.2 80.2 %all-gather.37.cloned.1.call-start = ((), (), s32[]{:S(2)}) async-start(), calls=%async_computation.16 | async-start | bytes 3981312 | tf_op jit(solution)/shard_map/all_gather | solution.py:313
  9.5 233.1 %all-gather.39.cloned.1.call-start = ((), (), s32[]{:S(2)}) async-start(), calls=%async_computation.17 | async-start | bytes 1327104 | tf_op jit(solution)/shard_map/all_gather | solution.py:315
  11.4 234.0 %all-gather.41.cloned.1.call-start = ((), (), s32[]{:S(2)}) async-start(), calls=%async_computation.18 | async-start | bytes 5308416 | tf_op jit(solution)/shard_map/all_gather | solution.py:321
  12.6 248.7 %all-gather.43.cloned.1.call-start = ((), (), s32[]{:S(2)}) async-start(), calls=%async_computation.19 | async-start | bytes 5308416 | tf_op jit(solution)/shard_map/all_gather | solution.py:323
  13.8 253.2 %all-gather.45.cloned.1.call-start = ((), (), s32[]{:S(2)}) async-start(), calls=%async_computation.20 | async-start | bytes 3981312 | tf_op jit(solution)/shard_map/all_gather | solution.py:313
  14.4 408.7 %all-gather.47.cloned.1.call-start = ((), (), s32[]{:S(2)}) async-start(), calls=%async_computation.21 | async-start | bytes 1327104 | tf_op jit(solution)/shard_map/all_gather | solution.py:315
  15.0 410.8 %all-gather.49.cloned.1.call-start = ((), (), s32[]{:S(2)}) async-start(), calls=%async_computation.22 | async-start | bytes 5308416 | tf_op jit(solution)/shard_map/all_gather | solution.py:321
  15.7 425.9 %all-gather.51.cloned.1.call-start = ((), (), s32[]{:S(2)}) async-start(), calls=%async_computation.23 | async-start | bytes 5308416 | tf_op jit(solution)/shard_map/all_gather | solution.py:323
  16.5 734.5 %reduce-scatter.15.cloned.1.call-start = ((), (), s32[]{:S(2)}) async-start(), calls=%async_computation.11 | async-start | bytes 1327104 | tf_op jit(solution)/shard_map/reduce_scatter | solution.py:361
  16.6 75.0 %copy-start.55 = (s32[14,14]{1,0:T(8,128)}, s32[14,14]{1,0:T(8,128)S(1)}, u32[]{:S(2)}) copy-start(s32[14,14]{1,0:T(8,128)S(1)} %subtract_add_fusion) | copy-start | bytes 2356
  20.1 71.5 %copy-start.70 = (f32[392]{0:T(512)}, f32[392]{0:T(512)S(1)}, u32[]{:S(2)}) copy-start(f32[392]{0:T(512)S(1)} %broadcast_multiply_fusion.11) | copy-start | bytes 4708
  20.4 71.1 %copy-start.92 = (f32[392]{0:T(512)}, f32[392]{0:T(512)S(1)}, u32[]{:S(2)}) copy-start(f32[392]{0:T(512)S(1)} %add_rsqrt_fusion.3) | copy-start | bytes 4708
  50.9 40.7 %copy-start.104 = (f32[768]{0:T(1024)}, f32[768]{0:T(1024)S(1)}, u32[]{:S(2)}) copy-start(f32[768]{0:T(1024)S(1)} %convert_element_type.558) | copy-start | bytes 9220
  51.0 194.4 %copy-start.78 = (f32[768]{0:T(1024)}, f32[768]{0:T(1024)S(1)}, u32[]{:S(2)}) copy-start(f32[768]{0:T(1024)S(1)} %convert_element_type.561) | copy-start | bytes 9220
  106.2 120.5 %copy-start.18 = (bf16[2,196,12,64]{1,3,2,0:T(8,128)(2,1)}, bf16[2,196,12,64]{1,3,2,0:T(8,128)(2,1)S(1)}, u32[]{:S(2)}) copy-start(bf16[2,196,12,64]{1,3,2,0:T(8,128)(2,1)S(1)} %copy.133) | copy-start | bytes 1806340
  479.0 272.0 %reduce-scatter.13.cloned.1.call-start = ((), (), s32[]{:S(2)}) async-start(), calls=%async_computation.10 | async-start | bytes 1327104 | tf_op jit(solution)/shard_map/reduce_scatter | solution.py:361
  569.8 181.2 %reduce-scatter.11.cloned.1.call-start = ((), (), s32[]{:S(2)}) async-start(), calls=%async_computation.9 | async-start | bytes 3981312 | tf_op jit(solution)/shard_map/reduce_scatter | solution.py:355
  575.8 175.3 %reduce-scatter.9.cloned.1.call-start = ((), (), s32[]{:S(2)}) async-start(), calls=%async_computation.8 | async-start | bytes 3981312 | tf_op jit(solution)/shard_map/reduce_scatter | solution.py:355
  662.6 98.5 %reduce-scatter.19.cloned.1.call-start = ((), (), s32[]{:S(2)}) async-start(), calls=%async_computation.13 | async-start | bytes 5308416 | tf_op jit(solution)/shard_map/reduce_scatter | solution.py:379
  670.2 146.5 %reduce-scatter.23.cloned.1.call-start = ((), (), s32[]{:S(2)}) async-start(), calls=%async_computation.15 | async-start | bytes 5308416 | tf_op jit(solution)/shard_map/reduce_scatter | solution.py:385
  676.7 195.5 %reduce-scatter.17.cloned.1.call-start = ((), (), s32[]{:S(2)}) async-start(), calls=%async_computation.12 | async-start | bytes 5308416 | tf_op jit(solution)/shard_map/reduce_scatter | solution.py:379
  684.2 243.4 %reduce-scatter.21.cloned.1.call-start = ((), (), s32[]{:S(2)}) async-start(), calls=%async_computation.14 | async-start | bytes 5308416 | tf_op jit(solution)/shard_map/reduce_scatter | solution.py:385
  690.5 337.8 %all-reduce.44.cloned.1.call-start = ((), (), s32[]{:S(2)}) async-start(), calls=%async_computation.24 | async-start | bytes 7077888 | tf_op jit(solution)/shard_map/psum | solution.py:399
  722.0 228.9 %copy-start.31 = (f32[392,768]{1,0:T(8,128)S(1)}, f32[392,768]{1,0:T(8,128)}, u32[]{:S(2)}) copy-start(f32[392,768]{1,0:T(8,128)} %get-tuple-element.117) | copy-start | bytes 3612676
  (137 other events, 826.9 us)
Sparse Core Ops, SparseCore 0:
  10.2 42.7 all-gather.36
  54.7 22.5 all-gather.38
  79.5 50.0 all-gather.40
  131.1 50.5 all-gather.42
  183.2 40.7 all-gather.44
  225.4 22.5 all-gather.46
  250.3 49.9 all-gather.48
  301.9 50.5 all-gather.50
  479.1 29.8 reduce-scatter.14
  569.9 29.7 reduce-scatter.12
  602.0 41.3 reduce-scatter.10
  662.8 40.2 reduce-scatter.8
  705.4 55.6 reduce-scatter.18
  763.3 53.3 reduce-scatter.22
  818.8 53.3 reduce-scatter.16
  874.3 53.3 reduce-scatter.20
  931.4 96.8 all-reduce.43
where the time goes:
time: 1060 us; the launch traced here: 1040 us
  local copies, waits for them, and re-layouts  347 us (33%)
  matrix products  255 us (24%)
  waiting for transfers between devices  249 us (23%)
  blocking collectives  97.9 us (9%)
  other arithmetic  71.7 us (7%)
  between operations  21 us (2%)
    add x12, local copies, waits for them, and re-layouts, layer_forward(): scores = scores + along_height[..., None] + along_width[..., None, :]  170 us
    reduce_scatter x2, waiting for transfers between devices, on_device(): lax.psum_scatter(terms[10].astype(jnp.bfloat16), 'fsdp', scatter_dimensio...  111 us
    psum x1, waiting for transfers between devices, on_device(): lax.psum(scattered[0].astype(jnp.bfloat16), 'rep').astype(jnp.float32)  69.5 us
    reduce_scatter x2, waiting for transfers between devices, on_device(): lax.psum_scatter(terms[8].astype(jnp.bfloat16), 'fsdp', scatter_dimension...  65.6 us
    unnamed x2, blocking collectives  54.8 us
    reshape x4, local copies, waits for them, and re-layouts, layer_backward(): grad_scores.astype(jnp.float32)  52 us
    reduce_sum x2, other arithmetic, layer_backward(): grad_along_height = jnp.sum(score_grid, -1)  32.9 us
    dot_general x2, matrix products, layer_forward(): jnp.dot(hidden_in, fc1_weight, preferred_element_type=jnp.float32)  31.6 us
  transfers between devices with their start and end apart: 17, of which 5 were waited for; matrix products, arithmetic and copies ran while one was open for 59% of the time, Pallas kernels for 0%

commit v1 on v0

v1 whole, which is shorter than its diff:
```python
import functools

import jax
import jax.numpy as jnp
import numpy as np
from jax import lax
from jax.experimental import pallas as pl
from jax.experimental.pallas import tpu as pltpu
from jax.sharding import PartitionSpec as P

HEADS = 12
HD = 64
WINDOW = 14
SIDE = 64
LAYERS = 2
GRID = 5
RELS = 2 * WINDOW - 1
EPSILON = 1e-06
PITCH = 16
SPAN = WINDOW * PITCH
PAIRS = HEADS // 2
LANES = 2 * HD
F32 = jnp.float32
BF16 = jnp.bfloat16
CHUNK = 256
ROWS_STEP = 64
VMEM_LIMIT = 56 * 1024 * 1024


def dot_nn(a, b):
    return lax.dot_general(a, b, (((1,), (0,)), ((), ())), preferred_element_type=F32)


def dot_nt(a, b):
    return lax.dot_general(a, b, (((1,), (1,)), ((), ())), preferred_element_type=F32)


def dot_tn(a, b):
    return lax.dot_general(a, b, (((0,), (0,)), ((), ())), preferred_element_type=F32)


def norm_rows(values):
    centre = jnp.mean(values, -1, keepdims=True)
    centered = values - centre
    inverse = lax.rsqrt(jnp.mean(centered * centered, -1, keepdims=True) + EPSILON)
    return centered * inverse, inverse


def norm_back(grad, normed, inverse, gain):
    scaled = grad * gain
    return inverse * (
        scaled
        - jnp.mean(scaled, -1, keepdims=True)
        - normed * jnp.mean(scaled * normed, -1, keepdims=True)
    )


def each(count, step, body):
    def run(index, carry):
        body(pl.multiple_of(index * step, step))
        return carry

    lax.fori_loop(0, count, run, 0)


def each_index(count, body):
    def run(index, carry):
        body(index)
        return carry

    lax.fori_loop(0, count, run, 0)


def half_lane():
    return lax.broadcasted_iota(jnp.int32, (SPAN, LANES), 1)


def split_heads(pair):
    lane = half_lane()
    zero = jnp.zeros_like(pair)
    return jnp.concatenate(
        [jnp.where(lane < HD, pair, zero), jnp.where(lane < HD, zero, pair)], axis=0
    )


def join_heads(stacked):
    return jnp.where(half_lane() < HD, stacked[:SPAN], stacked[SPAN:])


def shift_rows(table):
    by_row = jnp.concatenate(
        [
            pltpu.roll(table[i * PITCH : (i + 1) * PITCH], i, axis=1) if i else table[:PITCH]
            for i in range(WINDOW)
        ],
        axis=0,
    )
    by_col = pltpu.roll(
        table.reshape(WINDOW, PITCH, LANES), 0, axis=2, stride=1, stride_axis=1
    ).reshape(SPAN, LANES)
    return jnp.where(half_lane() < HD, by_row, by_col)


def key_tables():
    ahead = np.zeros((SPAN, LANES), np.float32)
    back = np.zeros((SPAN, LANES), np.float32)
    for k in range(WINDOW):
        for m in range(PITCH):
            row = k * PITCH + m
            ahead[row, WINDOW - 1 + k] = 1.0
            back[row, WINDOW - 1 - k] = 1.0
            if m < WINDOW:
                ahead[row, HD + WINDOW - 1 + m] = 1.0
                back[row, HD + WINDOW - 1 - m] = 1.0
            else:
                ahead[row, LANES - 1] = -1e30
    return jnp.asarray(ahead, BF16), jnp.asarray(back, BF16)


def fetch(copies):
    for copy in copies:
        copy.start()


def attend_kernel(blocks, loader, *refs):
    (x_ref, live_ref, vec_ref, table_ref, keys_ref), refs = refs[:5], refs[5:]
    weight_refs, refs = refs[: blocks], refs[blocks:]
    (mid_ref, h1_ref, q_ref, k_ref, v_ref, p_ref, att_ref), refs = refs[:7], refs[7:]
    w_ref, sem = refs
    ready = loader(weight_refs, w_ref, sem)
    width = x_ref.shape[1]

    def first_norm(start):
        rows = pl.ds(start, ROWS_STEP)
        normed, _ = norm_rows(x_ref[rows, :].astype(F32))
        shaped = (normed * vec_ref[0:1, :] + vec_ref[1:2, :]) * live_ref[rows, :]
        h1_ref[rows, :] = shaped.astype(BF16)

    each(x_ref.shape[0] // ROWS_STEP, ROWS_STEP, first_norm)
    ready()
    for index, (out_ref, bias) in enumerate(((q_ref, 2), (k_ref, None), (v_ref, 3))):

        def project(start, index=index, out_ref=out_ref, bias=bias):
            cols = pl.ds(start, CHUNK)
            made = dot_nn(h1_ref[...], w_ref[index, :, cols])
            if bias is not None:
                made = made + vec_ref[bias : bias + 1, cols]
            out_ref[:, cols] = made.astype(BF16)

        each(width // CHUNK, CHUNK, project)

    def attend(index):
        rows = pl.ds(pl.multiple_of(index // PAIRS * SPAN, SPAN), SPAN)
        cols = pl.ds(pl.multiple_of(index % PAIRS * LANES, LANES), LANES)
        queries = q_ref[rows, cols]
        offsets = dot_nn(queries, table_ref[...])
        lane = half_lane()
        sides = []
        for half in range(2):
            moved = shift_rows(offsets[:, half * LANES : (half + 1) * LANES])
            sides.append(jnp.where(lane == LANES - 1, 1.0, moved).astype(BF16))
        left = jnp.concatenate(
            [split_heads(queries) * HD ** (-0.5), jnp.concatenate(sides, axis=0)], axis=1
        )
        right = jnp.concatenate([k_ref[rows, cols], keys_ref[...]], axis=1)
        scores = dot_nt(left, right)
        shifted = jnp.exp(scores - jnp.max(scores, -1, keepdims=True))
        probs = shifted * (1.0 / jnp.sum(shifted, -1, keepdims=True))
        low = probs.astype(BF16)
        p_ref[index] = low
        att_ref[rows, cols] = join_heads(dot_nn(low, v_ref[rows, cols])).astype(BF16)

    each_index(x_ref.shape[0] // SPAN * PAIRS, attend)

    def finish(start):
        cols = pl.ds(start, CHUNK)
        branch = dot_nn(att_ref[...], w_ref[3, :, cols]) + vec_ref[4:5, cols]
        mid_ref[:, cols] = x_ref[:, cols].astype(F32) + live_ref[...] * branch

    each(width // CHUNK, CHUNK, finish)


def mlp_kernel(blocks, loader, *refs):
    (mid_ref, live_ref, vec_ref, bias_ref), refs = refs[:4], refs[4:]
    weight_refs, refs = refs[: sum(blocks)], refs[sum(blocks) :]
    (out_ref, h2_ref, act_ref, slope_ref), refs = refs[:4], refs[4:]
    w1_ref, w2_ref, sem = refs
    ready1, ready2 = loader(weight_refs, w1_ref, w2_ref, sem)
    width = mid_ref.shape[1]
    hidden_width = act_ref.shape[1]

    def second_norm(start):
        rows = pl.ds(start, ROWS_STEP)
        normed, _ = norm_rows(mid_ref[rows, :])
        h2_ref[rows, :] = (normed * vec_ref[5:6, :] + vec_ref[6:7, :]).astype(BF16)

    each(mid_ref.shape[0] // ROWS_STEP, ROWS_STEP, second_norm)
    ready1()

    def expand(index):
        start = pl.multiple_of(index * CHUNK, CHUNK)
        cols = pl.ds(start, CHUNK)
        inner = pl.ds(pl.multiple_of(start % width, CHUNK), CHUNK)
        hidden = dot_nn(h2_ref[...], w1_ref[start // width, :, inner]) + bias_ref[:, cols]
        below = 0.5 * (1.0 + lax.erf(hidden * (0.5**0.5)))
        bell = jnp.exp(-0.5 * hidden * hidden) * (0.5 / np.pi) ** 0.5
        act_ref[:, cols] = (hidden * below).astype(BF16)
        slope_ref[:, cols] = (below + hidden * bell).astype(BF16)

    each_index(hidden_width // CHUNK, expand)
    ready2()

    def contract(start):
        cols = pl.ds(start, CHUNK)
        made = dot_nn(act_ref[...], w2_ref[:, cols]) + vec_ref[7:8, cols]
        out_ref[:, cols] = mid_ref[:, cols] + live_ref[...] * made

    each(width // CHUNK, CHUNK, contract)


def mlp_back_kernel(blocks, loader, *refs):
    (grad_ref, mid_ref, live_ref, vec_ref, h2_ref, act_ref, slope_ref), refs = refs[:7], refs[7:]
    weight_refs, refs = refs[: sum(blocks)], refs[sum(blocks) :]
    (dmid_ref, g1_ref, g2_ref, sums_ref, hsum_ref), refs = refs[:5], refs[5:]
    w1_ref, w2_ref, dm_ref, dh_ref, ds_ref, sem = refs
    ready1, ready2 = loader(weight_refs, w1_ref, w2_ref, sem)
    width = mid_ref.shape[1]
    hidden_width = act_ref.shape[1]
    count = mid_ref.shape[0] // ROWS_STEP

    dm_ref[...] = (live_ref[...] * grad_ref[...].astype(F32)).astype(BF16)

    def second_weight(start):
        rows = pl.ds(start, CHUNK)
        g2_ref[rows, :] = dot_tn(act_ref[:, rows], dm_ref[...]).astype(BF16)

    each(hidden_width // CHUNK, CHUNK, second_weight)
    sums_ref[...] = jnp.zeros_like(sums_ref)
    sums_ref[0:1, :] = jnp.sum(dm_ref[...].astype(F32), 0, keepdims=True)
    ready2()

    def inner_grad(start):
        cols = pl.ds(start, CHUNK)
        made = (dot_nt(dm_ref[...], w2_ref[cols, :]) * slope_ref[:, cols].astype(F32)).astype(BF16)
        dh_ref[:, cols] = made
        hsum_ref[:, cols] = jnp.sum(made.astype(F32), 0, keepdims=True)

    each(hidden_width // CHUNK, CHUNK, inner_grad)
    ready1()

    def first_weight(index):
        start = pl.multiple_of(index * CHUNK, CHUNK)
        inner = pl.ds(pl.multiple_of(start % width, CHUNK), CHUNK)
        g1_ref[start // width, :, inner] = dot_tn(
            h2_ref[...], dh_ref[:, pl.ds(start, CHUNK)]
        ).astype(BF16)

    each_index(hidden_width // CHUNK, first_weight)

    def back_in(start):
        rows = pl.ds(start, CHUNK)
        made = dot_nt(dh_ref[:, 0:width], w1_ref[0, rows, :])
        for block in range(1, hidden_width // width):
            made += dot_nt(
                dh_ref[:, block * width : (block + 1) * width], w1_ref[block, rows, :]
            )
        ds_ref[:, rows] = made

    each(width // CHUNK, CHUNK, back_in)

    def back_norm(start):
        rows = pl.ds(start, ROWS_STEP)
        normed, inverse = norm_rows(mid_ref[rows, :])
        grad = ds_ref[rows, :]
        sums_ref[1:2, :] += jnp.sum(grad * normed, 0, keepdims=True)
        sums_ref[2:3, :] += jnp.sum(grad, 0, keepdims=True)
        dmid_ref[rows, :] = grad_ref[rows, :].astype(F32) + norm_back(
            grad, normed, inverse, vec_ref[5:6, :]
        )

    each(count, ROWS_STEP, back_norm)


def attend_back_kernel(blocks, loader, *refs):
    (
        dmid_ref,
        x_ref,
        live_ref,
        vec_ref,
        table_ref,
        keys_ref,
        h1_ref,
        q_ref,
        k_ref,
        v_ref,
        p_ref,
        att_ref,
    ), refs = refs[:12], refs[12:]
    weight_refs, refs = refs[:blocks], refs[blocks:]
    (next_ref, g_ref, sums_ref, rel_ref), refs = refs[:4], refs[4:]
    w_ref, db_ref, da_ref, dq_ref, dk_ref, dv_ref, dh_ref, sem = refs
    ready = loader(weight_refs, w_ref, sem)
    width = x_ref.shape[1]
    count = x_ref.shape[0] // ROWS_STEP

    db_ref[...] = (live_ref[...] * dmid_ref[...]).astype(BF16)
    sums_ref[...] = jnp.zeros_like(sums_ref)
    sums_ref[0:1, :] = jnp.sum(db_ref[...].astype(F32), 0, keepdims=True)
    rel_ref[...] = jnp.zeros_like(rel_ref)

    def out_weight(start):
        cols = pl.ds(start, CHUNK)
        g_ref[3, :, cols] = dot_tn(att_ref[...], db_ref[:, cols]).astype(BF16)

    each(width // CHUNK, CHUNK, out_weight)
    ready()

    def back_out(start):
        rows = pl.ds(start, CHUNK)
        da_ref[:, rows] = dot_nt(db_ref[...], w_ref[3, rows, :]).astype(BF16)

    each(width // CHUNK, CHUNK, back_out)

    def attend(index):
        rows = pl.ds(pl.multiple_of(index // PAIRS * SPAN, SPAN), SPAN)
        cols = pl.ds(pl.multiple_of(index % PAIRS * LANES, LANES), LANES)
        low = p_ref[index]
        probs = low.astype(F32)
        outer = split_heads(da_ref[rows, cols])
        queries = split_heads(q_ref[rows, cols])
        d_probs = dot_nt(outer, v_ref[rows, cols])
        dv_ref[rows, cols] = dot_tn(low, outer).astype(BF16)
        mean = jnp.sum(d_probs * probs, -1, keepdims=True)
        d_scores = (probs * (d_probs - mean)).astype(BF16)
        both = dot_nn(d_scores, jnp.concatenate([k_ref[rows, cols], keys_ref[...]], axis=1))
        moved = [
            shift_rows(both[half * SPAN : (half + 1) * SPAN, LANES:]).astype(BF16)
            for half in range(2)
        ]
        rel_part = dot_nt(jnp.concatenate(moved, axis=1), table_ref[...])
        direct = join_heads(both[:, :LANES]) * HD ** (-0.5)
        dq_ref[rows, cols] = (direct + rel_part).astype(BF16)
        dk_ref[rows, cols] = (dot_tn(d_scores, queries) * HD ** (-0.5)).astype(BF16)
        rel_ref[...] += dot_tn(jnp.concatenate(moved, axis=0), queries)

    each_index(x_ref.shape[0] // SPAN * PAIRS, attend)
    sums_ref[1:2, :] = jnp.sum(dq_ref[...].astype(F32), 0, keepdims=True)
    sums_ref[2:3, :] = jnp.sum(dv_ref[...].astype(F32), 0, keepdims=True)
    for index, part_ref in enumerate((dq_ref, dk_ref, dv_ref)):

        def in_weight(start, index=index, part_ref=part_ref):
            cols = pl.ds(start, CHUNK)
            g_ref[index, :, cols] = dot_tn(h1_ref[...], part_ref[:, cols]).astype(BF16)

        each(width // CHUNK, CHUNK, in_weight)

    def back_in(start):
        rows = pl.ds(start, CHUNK)
        made = dot_nt(dq_ref[...], w_ref[0, rows, :])
        made += dot_nt(dk_ref[...], w_ref[1, rows, :])
        made += dot_nt(dv_ref[...], w_ref[2, rows, :])
        dh_ref[:, rows] = made * live_ref[...]

    each(width // CHUNK, CHUNK, back_in)

    def back_norm(start):
        rows = pl.ds(start, ROWS_STEP)
        normed, inverse = norm_rows(x_ref[rows, :].astype(F32))
        grad = dh_ref[rows, :]
        sums_ref[3:4, :] += jnp.sum(grad * normed, 0, keepdims=True)
        sums_ref[4:5, :] += jnp.sum(grad, 0, keepdims=True)
        next_ref[rows, :] = dmid_ref[rows, :] + norm_back(grad, normed, inverse, vec_ref[0:1, :])

    each(count, ROWS_STEP, back_norm)


VM = pl.BlockSpec(memory_space=pltpu.VMEM)
ANY = pl.BlockSpec(memory_space=pl.ANY)


def call(kernel, resident, pieces, outs, scratch, flops):
    moved = sum(a.size * a.dtype.itemsize for a in (*resident, *pieces, *outs))
    return pl.pallas_call(
        kernel,
        out_shape=tuple(outs),
        in_specs=[VM] * len(resident) + [ANY] * len(pieces),
        out_specs=tuple([VM] * len(outs)),
        scratch_shapes=scratch,
        compiler_params=pltpu.CompilerParams(vmem_limit_bytes=VMEM_LIMIT),
        cost_estimate=pl.CostEstimate(flops=int(flops), bytes_accessed=int(moved), transcendentals=0),
    )(*resident, *pieces)


def shape(dims, kind):
    return jax.ShapeDtypeStruct(tuple(dims), kind)


def whole_attention(weight_refs, w_ref, sem):
    qkv_ref, proj_ref = weight_refs
    width = w_ref.shape[1]
    copies = [
        pltpu.make_async_copy(qkv_ref.at[:, pl.ds(i * width, width)], w_ref.at[i], sem.at[i])
        for i in range(3)
    ]
    copies.append(pltpu.make_async_copy(proj_ref, w_ref.at[3], sem.at[3]))
    fetch(copies)

    def ready():
        for copy in copies:
            copy.wait()

    return ready


def whole_mlp(weight_refs, w1_ref, w2_ref, sem):
    fc1_ref, fc2_ref = weight_refs
    width = w1_ref.shape[1]
    first = [
        pltpu.make_async_copy(fc1_ref.at[:, pl.ds(i * width, width)], w1_ref.at[i], sem.at[i])
        for i in range(w1_ref.shape[0])
    ]
    second = [pltpu.make_async_copy(fc2_ref, w2_ref, sem.at[w1_ref.shape[0]])]
    fetch(first)
    fetch(second)

    def ready1():
        for copy in first:
            copy.wait()

    def ready2():
        for copy in second:
            copy.wait()

    return ready1, ready2


def attend_forward(x, live, vec, table, keys, pieces, loader):
    rows, width = x.shape
    outs = (
        shape((rows, width), F32),
        *[shape((rows, width), BF16)] * 4,
        shape((rows // SPAN * PAIRS, 2 * SPAN, SPAN), BF16),
        shape((rows, width), BF16),
    )
    scratch = [pltpu.VMEM((4, width, width), BF16), pltpu.SemaphoreType.DMA((len(pieces) + 2,))]
    return call(
        functools.partial(attend_kernel, len(pieces), loader),
        (x, live, vec, table, keys),
        pieces,
        outs,
        scratch,
        2 * rows * width * 4 * width,
    )


def mlp_forward(mid, live, vec, bias, pieces, loader, counts):
    rows, width = mid.shape
    hidden = bias.shape[1]
    outs = (
        shape((rows, width), F32),
        shape((rows, width), BF16),
        shape((rows, hidden), BF16),
        shape((rows, hidden), BF16),
    )
    scratch = [
        pltpu.VMEM((hidden // width, width, width), BF16),
        pltpu.VMEM((hidden, width), BF16),
        pltpu.SemaphoreType.DMA((8,)),
    ]
    return call(
        functools.partial(mlp_kernel, counts, loader),
        (mid, live, vec, bias),
        pieces,
        outs,
        scratch,
        4 * rows * width * hidden,
    )


def mlp_backward(grad, mid, live, vec, h2, act, slope, pieces, loader, counts):
    rows, width = mid.shape
    hidden = act.shape[1]
    outs = (
        shape((rows, width), F32),
        shape((hidden // width, width, width), BF16),
        shape((hidden, width), BF16),
        shape((8, width), F32),
        shape((1, hidden), F32),
    )
    scratch = [
        pltpu.VMEM((hidden // width, width, width), BF16),
        pltpu.VMEM((hidden, width), BF16),
        pltpu.VMEM((rows, width), BF16),
        pltpu.VMEM((rows, hidden), BF16),
        pltpu.VMEM((rows, width), F32),
        pltpu.SemaphoreType.DMA((8,)),
    ]
    return call(
        functools.partial(mlp_back_kernel, counts, loader),
        (grad, mid, live, vec, h2, act, slope),
        pieces,
        outs,
        scratch,
        8 * rows * width * hidden,
    )


def attend_backward(dmid, x, live, vec, table, keys, h1, q, k, v, p, att, pieces, loader):
    rows, width = x.shape
    outs = (
        shape((rows, width), F32),
        shape((4, width, width), BF16),
        shape((8, width), F32),
        shape((LANES, LANES), F32),
    )
    scratch = [
        pltpu.VMEM((4, width, width), BF16),
        *[pltpu.VMEM((rows, width), BF16)] * 5,
        pltpu.VMEM((rows, width), F32),
        pltpu.SemaphoreType.DMA((len(pieces) + 2,)),
    ]
    return call(
        functools.partial(attend_back_kernel, len(pieces), loader),
        (dmid, x, live, vec, table, keys, h1, q, k, v, p, att),
        pieces,
        outs,
        scratch,
        4 * rows * width * 4 * width,
    )


def live_rows(slot_table):
    places = jnp.arange(PITCH, dtype=jnp.int32)
    rows_inside = slot_table[:, None] // GRID * WINDOW + places[None, :WINDOW] < SIDE
    cols_inside = slot_table[:, None] % GRID * WINDOW + places[None, :] < SIDE
    cols_inside = cols_inside & (places < WINDOW)[None, :]
    both_inside = rows_inside[:, :, None] & cols_inside[:, None, :]
    return both_inside.astype(F32).reshape(slot_table.shape[0] * SPAN, 1)


def spread(values):
    width = values.shape[1]
    grid = values.reshape(-1, WINDOW, width)
    return jnp.pad(grid, ((0, 0), (0, PITCH - WINDOW), (0, 0))).reshape(-1, width)


def gather_back(values):
    width = values.shape[1]
    return values.reshape(-1, PITCH, width)[:, :WINDOW].reshape(-1, width)


def relative_tables(rel_height, rel_width):
    stacked = jnp.stack([rel_height, rel_width], 1).reshape(LAYERS, 2, RELS, HD)

    def spread_table(rows):
        padded = jnp.pad(rows, ((0, 0), (0, 0), (0, HD - RELS), (0, 0)))
        one = padded.reshape(LAYERS, LANES, HD).transpose(0, 2, 1)
        none = jnp.zeros_like(one)
        return jnp.concatenate(
            [jnp.concatenate([one, none], 2), jnp.concatenate([none, one], 2)], 1
        )

    return spread_table(stacked[:, :, ::-1]), spread_table(stacked)


SMALL = (
    "qv_bias", "proj_bias", "norm1_gain", "norm1_bias", "norm2_gain", "norm2_bias",
    "fc1_bias", "fc2_bias", "rel_height", "rel_width",
)


def gather_small(parts):
    packed = jnp.concatenate(parts, axis=1)
    whole = lax.all_gather(packed, "fsdp", axis=0, tiled=False)
    found = []
    start = 0
    for part in parts:
        size = part.shape[1]
        cut = whole[:, :, start : start + size]
        found.append(cut.transpose(1, 0, 2).reshape(LAYERS, -1))
        start += size
    return found


def on_device(
    windows, slot_table, cotangent, qkv_weight, qv_bias, proj_weight, proj_bias, norm1_gain,
    norm1_bias, norm2_gain, norm2_bias, fc1_weight, fc1_bias, fc2_weight, fc2_bias, rel_height,
    rel_width,
):
    width = windows.shape[1]
    live = live_rows(slot_table)
    (
        qv_bias_w, proj_bias_w, norm1_gain_w, norm1_bias_w, norm2_gain_w, norm2_bias_w,
        fc1_bias_w, fc2_bias_w, rel_height_w, rel_width_w,
    ) = gather_small((
        qv_bias, proj_bias, norm1_gain, norm1_bias, norm2_gain, norm2_bias, fc1_bias, fc2_bias,
        rel_height, rel_width,
    ))
    vec = jnp.stack(
        [norm1_gain_w, norm1_bias_w, qv_bias_w[:, :width], qv_bias_w[:, width:], proj_bias_w,
         norm2_gain_w, norm2_bias_w, fc2_bias_w], 1
    ).astype(F32)
    hidden_bias = fc1_bias_w.astype(F32)[:, None, :]
    ahead, back = relative_tables(rel_height_w, rel_width_w)
    keys_ahead, keys_back = key_tables()
    current = spread(windows).astype(F32)
    gathered = [
        tuple(
            lax.all_gather(w[layer], "fsdp", axis=0, tiled=True)
            for w in (qkv_weight, proj_weight, fc1_weight, fc2_weight)
        )
        for layer in range(LAYERS)
    ]
    kept = []
    for layer in range(LAYERS):
        qkv, proj, fc1, fc2 = gathered[layer]
        mid, h1, q, k, v, p, att = attend_forward(
            current, live, vec[layer], ahead[layer], keys_ahead, (qkv, proj), whole_attention
        )
        following, h2, act, slope = mlp_forward(
            mid, live, vec[layer], hidden_bias[layer], (fc1, fc2), whole_mlp, (1, 1)
        )
        kept.append((current, mid, h1, q, k, v, p, att, h2, act, slope))
        current = following
    output = gather_back(current).astype(BF16)
    grad = spread(cotangent).astype(F32)
    big = [None] * LAYERS
    small = [None] * LAYERS
    for layer in reversed(range(LAYERS)):
        qkv, proj, fc1, fc2 = gathered[layer]
        x, mid, h1, q, k, v, p, att, h2, act, slope = kept[layer]
        dmid, g1, g2, sums2, hsum = mlp_backward(
            grad, mid, live, vec[layer], h2, act, slope, (fc1, fc2), whole_mlp, (1, 1)
        )
        grad, g, sums1, rel = attend_backward(
            dmid, x, live, vec[layer], back[layer], keys_back, h1, q, k, v, p, att, (qkv, proj),
            whole_attention,
        )
        rel = rel[:, :HD] + rel[:, HD:]
        small[layer] = (
            jnp.concatenate([sums1[1], sums1[2]]), sums1[0], sums1[3], sums1[4], sums2[1],
            sums2[2], hsum[0], sums2[0], rel[:RELS].reshape(-1), rel[HD : HD + RELS].reshape(-1),
        )
        shards = lax.axis_size("fsdp")

        def reduce(value, axis):
            return lax.psum(
                lax.psum_scatter(value, "fsdp", scatter_dimension=axis, tiled=True), "rep"
            ).astype(F32)

        g = reduce(g, 1)
        g1 = reduce(g1, 1)
        big[layer] = (
            jnp.concatenate([g[0], g[1], g[2]], 1), g[3], jnp.concatenate(list(g1), 1),
            reduce(g2, 0),
        )
    shards = lax.axis_size("fsdp")
    packed = jnp.concatenate(
        [
            jnp.stack([small[layer][i] for layer in range(LAYERS)]).reshape(LAYERS, shards, -1)
            for i in range(len(SMALL))
        ],
        2,
    ).astype(BF16)
    mine = lax.psum(
        lax.psum_scatter(packed, "fsdp", scatter_dimension=1, tiled=True), "rep"
    ).astype(F32)[:, 0]
    cuts = np.cumsum([0] + [small[0][i].shape[0] // shards for i in range(len(SMALL))])
    tiny = [mine[:, cuts[i] : cuts[i + 1]] for i in range(len(SMALL))]
    qv, pb, n1g, n1b, n2g, n2b, f1b, f2b, rh, rw = tiny
    stacked = [jnp.stack([big[layer][i] for layer in range(LAYERS)]) for i in range(4)]
    input_grad = gather_back(grad).astype(BF16)
    return (
        output, input_grad, stacked[0], qv, stacked[1], pb, n1g, n1b, n2g, n2b, stacked[2], f1b,
        stacked[3], f2b, rh, rw,
    )


def solution(mesh):
    rows = P(("rep", "fsdp"), None)
    cube = P(None, "fsdp", None)
    flat = P(None, "fsdp")
    return jax.shard_map(
        on_device,
        mesh=mesh,
        in_specs=(
            rows, P(("rep", "fsdp")), rows, cube, flat, cube, flat, flat, flat, flat, flat, cube,
            flat, cube, flat, flat, flat,
        ),
        out_specs=(
            rows, rows, cube, flat, cube, flat, flat, flat, flat, flat, cube, flat, cube, flat,
            flat, flat,
        ),
        check_vma=False,
    )
```

time: 1060 us -> 872 us (0.82); the launches traced: 1040 us -> 870 us
  waiting for transfers between devices: 249 us -> 590 us
  local copies, waits for them, and re-layouts: 347 us -> 23.3 us
  matrix products: 255 us -> 0 us
  Pallas kernels: 0 us -> 181 us
  other arithmetic: 71.7 us -> 10.5 us
  blocking collectives: 97.9 us -> 50.3 us
    all_gather x8, waiting for transfers between devices: 0.11 us -> 258 us  [on_device(): lax.all_gather(w[layer], 'fsdp', axis=0, tiled=True)]
    dot_general x56 -> x0, matrix products: 255 us -> none  [the longest x2 31.6 us: layer_forward(): jnp.dot(hidden_in, fc1_weight, preferred_element_type=jnp.float32)]
    pallas_call x0 -> x8, Pallas kernels: none -> 181 us  [call(): pl.pallas_call(kernel, out_shape=tuple(outs), in_specs=[VM] * len(residen...]
    add x14 -> x0, local copies, waits for them, and re-layouts: 177 us -> none  [the longest x12 170 us: layer_forward(): scores = scores + along_height[..., None] + along_width[..., None, :]]
    reshape x30 -> x17, local copies, waits for them, and re-layouts: 98.8 us -> 1.2 us  [the longest x12 0.57 us: on_device(): jnp.stack([small[layer][i] for layer in range(LAYERS)])]
    reduce_scatter x8 -> x6, waiting for transfers between devices: 177 us -> 271 us  [reduce(): lax.psum_scatter(value, 'fsdp', scatter_dimension=axis, tiled=True)]
    reduce_sum x10 -> x0, other arithmetic: 38.6 us -> none  [the longest x2 32.9 us: layer_backward(): grad_along_height = jnp.sum(score_grid, -1)]
    unnamed x2 -> x1, blocking collectives: 54.8 us -> 26.1 us
  transfers between devices with their start and end apart: 17 -> 15, of which waited for: 5 -> 13; matrix products, arithmetic and copies ran while one was open for 59% -> 2% of each run, Pallas kernels for 0% -> 13%
where the time goes in v1:
time: 872 us; the launch traced here: 870 us
  waiting for transfers between devices  590 us (68%)
  Pallas kernels  181 us (21%)
  blocking collectives  50.3 us (6%)
  local copies, waits for them, and re-layouts  23.3 us (3%)
  between operations  14.8 us (2%)
  other arithmetic  10.5 us (1%)
    reduce_scatter x6, waiting for transfers between devices, reduce(): lax.psum_scatter(value, 'fsdp', scatter_dimension=axis, tiled=True)  271 us
    all_gather x8, waiting for transfers between devices, on_device(): lax.all_gather(w[layer], 'fsdp', axis=0, tiled=True)  258 us
    pallas_call x8, Pallas kernels, call(): pl.pallas_call(kernel, out_shape=tuple(outs), in_specs=[VM] * len(residen...  181 us
    psum x1, waiting for transfers between devices, reduce(): lax.psum(lax.psum_scatter(value, 'fsdp', scatter_dimension=axis, tiled=Tr...  55.5 us
    unnamed x1, blocking collectives  26.1 us
  transfers between devices with their start and end apart: 15, of which 13 were waited for; matrix products, arithmetic and copies ran while one was open for 2% of the time, Pallas kernels for 13%

profile of v1, /device:TPU:8, one launch (start us, length us, event | category | flops | bytes accessed | tf_op | source)
XLA Modules:
  0.0 870.3 jit_solution(7458556358260128314)
XLA Ops:
  17.1 14.2 %all-gather.9 = bf16[8,2,1584]{2,1,0:T(2,128)(2,1)S(1)} all-gather(bf16[1,2,1584]{2,1,0:T(2,128)(2,1)S(1)} %bitcast.113), channel_id=2, replica_groups=mesh['rep'=4,'fsdp'=8] {'fsdp'}, dimensions={0}, use_global_device_ids=true | all-gather | bytes 57024 | tf_op jit(solution)/shard_map/all_gather | solution.py:574
  40.0 36.1 %all-gather.19.cloned.1.call-done = bf16[1,768,2304]{2,1,0:T(8,128)(2,1)} async-done(((bf16[1,96,2304]{2,1,0:T(8,128)(2,1)}), bf16[1,768,2304]{2,1,0:T(8,128)(2,1)}) %all-gather.19.cloned.1.call-update) | async-done | bytes 3538960 | tf_op jit(solution)/shard_map/all_gather | solution.py:609
  76.1 19.9 %shard_map.306 = (f32[448,768]{1,0:T(8,128)}, bf16[448,768]{1,0:T(8,128)(2,1)}, bf16[448,768]{1,0:T(8,128)(2,1)}, bf16[448,768]{1,0:T(8,128)(2,1)}, bf16[448,768...) custom-call(f32[448,768]{1,0:T(8,128)} %bitcast_convert_fusion.1.refs_0_.refs_1_, ...), custom_call_target="tpu_custom_call" | custom-call | flops 2113929216 | bytes 13469440 | tf_op jit(solution)/shard_map/pallas_call | solution.py:383
  96.1 32.5 %all-gather.23.cloned.1.call-done = bf16[1,768,3072]{2,1,0:T(8,128)(2,1)} async-done(((bf16[1,96,3072]{2,1,0:T(8,128)(2,1)}), bf16[1,768,3072]{2,1,0:T(8,128)(2,1)}) %all-gather.23.cloned.1.call-update) | async-done | bytes 4718608 | tf_op jit(solution)/shard_map/all_gather | solution.py:609
  128.6 52.6 %all-gather.25.cloned.1.call-done = bf16[1,3072,768]{2,1,0:T(8,128)(2,1)} async-done(((bf16[1,384,768]{2,1,0:T(8,128)(2,1)}), bf16[1,3072,768]{2,1,0:T(8,128)(2,1)}) %all-gather.25.cloned.1.call-update) | async-done | bytes 4718608 | tf_op jit(solution)/shard_map/all_gather | solution.py:609
  181.2 14.4 %shard_map.307 = (f32[448,768]{1,0:T(8,128)}, bf16[448,768]{1,0:T(8,128)(2,1)}, bf16[448,3072]{1,0:T(8,128)(2,1)}, bf16[448,3072]{1,0:T(8,128)(2,1)}) custom-call(f32[448,768]{1,0:T(8,128)} %get-tuple-element.56.refs_0_.refs_1_, f32[448,1]{1,0:T(8,128)} %reshape.263.refs_1_.refs_2_, f32[8,768]{1,0:T(8,128)} %get-tuple-element.141.refs_2_.refs_3_, ...), custom_call_target="tpu_custom_call" | custom-call | flops 4227858432 | bytes 18421504 | tf_op jit(solution)/shard_map/pallas_call | solution.py:383
  195.5 10.1 %all-gather.29.cloned.1.call-done = bf16[1,768,768]{2,1,0:T(8,128)(2,1)} async-done(((bf16[1,96,768]{2,1,0:T(8,128)(2,1)}), bf16[1,768,768]{2,1,0:T(8,128)(2,1)}) %all-gather.29.cloned.1.call-update) | async-done | bytes 1179664 | tf_op jit(solution)/shard_map/all_gather | solution.py:609
  205.6 41.8 %all-gather.27.cloned.1.call-done = bf16[1,768,2304]{2,1,0:T(8,128)(2,1)} async-done(((bf16[1,96,2304]{2,1,0:T(8,128)(2,1)}), bf16[1,768,2304]{2,1,0:T(8,128)(2,1)}) %all-gather.27.cloned.1.call-update) | async-done | bytes 3538960 | tf_op jit(solution)/shard_map/all_gather | solution.py:609
  247.4 19.9 %shard_map.308 = (f32[448,768]{1,0:T(8,128)}, bf16[448,768]{1,0:T(8,128)(2,1)}, bf16[448,768]{1,0:T(8,128)(2,1)}, bf16[448,768]{1,0:T(8,128)(2,1)}, bf16[448,768...) custom-call(f32[448,768]{1,0:T(8,128)} %get-tuple-element.57.refs_0_.refs_1_, ...), custom_call_target="tpu_custom_call" | custom-call | flops 2113929216 | bytes 13469440 | tf_op jit(solution)/shard_map/pallas_call | solution.py:383
  267.3 32.5 %all-gather.31.cloned.1.call-done = bf16[1,768,3072]{2,1,0:T(8,128)(2,1)} async-done(((bf16[1,96,3072]{2,1,0:T(8,128)(2,1)}), bf16[1,768,3072]{2,1,0:T(8,128)(2,1)}) %all-gather.31.cloned.1.call-update) | async-done | bytes 4718608 | tf_op jit(solution)/shard_map/all_gather | solution.py:609
  299.8 52.7 %all-gather.33.cloned.1.call-done = bf16[1,3072,768]{2,1,0:T(8,128)(2,1)} async-done(((bf16[1,384,768]{2,1,0:T(8,128)(2,1)}), bf16[1,3072,768]{2,1,0:T(8,128)(2,1)}) %all-gather.33.cloned.1.call-update) | async-done | bytes 4718608 | tf_op jit(solution)/shard_map/all_gather | solution.py:609
  352.6 14.3 %shard_map.309 = (f32[448,768]{1,0:T(8,128)}, bf16[448,768]{1,0:T(8,128)(2,1)}, bf16[448,3072]{1,0:T(8,128)(2,1)}, bf16[448,3072]{1,0:T(8,128)(2,1)}) custom-call(f32[448,768]{1,0:T(8,128)} %get-tuple-element.58.refs_0_.refs_1_, f32[448,1]{1,0:T(8,128)} %reshape.263.refs_1_.refs_2_, f32[8,768]{1,0:T(8,128)} %get-tuple-element.140.refs_2_.refs_3_, ...), custom_call_target="tpu_custom_call" | custom-call | flops 4227858432 | bytes 18421504 | tf_op jit(solution)/shard_map/pallas_call | solution.py:383
  366.9 28.1 %shard_map.310 = (f32[448,768]{1,0:T(8,128)}, bf16[4,768,768]{2,1,0:T(8,128)(2,1)}, bf16[3072,768]{1,0:T(8,128)(2,1)}, f32[8,768]{1,0:T(8,128)}, f32[1,3072]{1,0:T(1,128)}) custom-call(f32[448,768]{1,0:T(8,128)} %bitcast_convert_fusion.refs_0_, f32[448,768]{1,0:T(8,128)} %get-tuple-element.58.refs_0_.refs_1_, f32[448,1]{1,0:T(8,128)} %reshape.263.refs_1_.refs_2_, ...), custom_call_target="tpu_custom_call" | custom-call | flops 8455716864 | bytes 29259520 | tf_op jit(solution)/shard_map/pallas_call | solution.py:383
  395.0 27.8 %shard_map.311 = (f32[448,768]{1,0:T(8,128)}, bf16[4,768,768]{2,1,0:T(8,128)(2,1)}, f32[8,768]{1,0:T(8,128)}, f32[128,128]{1,0:T(8,128)}) custom-call(f32[448,768]{1,0:T(8,128)} %get-tuple-element.63.refs_0_, f32[448,768]{1,0:T(8,128)} %get-tuple-element.57.refs_0_.refs_1_, f32[448,1]{1,0:T(8,128)} %reshape.263.refs_1_.refs_2_, ...), custom_call_target="tpu_custom_call" | custom-call | flops 4227858432 | bytes 19654400 | tf_op jit(solution)/shard_map/pallas_call | solution.py:383
  422.9 28.4 %shard_map.312 = (f32[448,768]{1,0:T(8,128)}, bf16[4,768,768]{2,1,0:T(8,128)(2,1)}, bf16[3072,768]{1,0:T(8,128)(2,1)}, f32[8,768]{1,0:T(8,128)}, f32[1,3072]{1,0:T(1,128)}) custom-call(f32[448,768]{1,0:T(8,128)} %get-tuple-element.70.refs_0_, f32[448,768]{1,0:T(8,128)} %get-tuple-element.56.refs_0_.refs_1_, f32[448,1]{1,0:T(8,128)} %reshape.263.refs_1_.refs_2_, ...), custom_call_target="tpu_custom_call" | custom-call | flops 8455716864 | bytes 29259520 | tf_op jit(solution)/shard_map/pallas_call | solution.py:383
  451.3 28.0 %shard_map.313 = (f32[448,768]{1,0:T(8,128)}, bf16[4,768,768]{2,1,0:T(8,128)(2,1)}, f32[8,768]{1,0:T(8,128)}, f32[128,128]{1,0:T(8,128)}) custom-call(f32[448,768]{1,0:T(8,128)} %get-tuple-element.74.refs_0_, f32[448,768]{1,0:T(8,128)} %bitcast_convert_fusion.1.refs_0_.refs_1_, f32[448,1]{1,0:T(8,128)} %reshape.263.refs_1_.refs_2_, ...), custom_call_target="tpu_custom_call" | custom-call | flops 4227858432 | bytes 19654400 | tf_op jit(solution)/shard_map/pallas_call | solution.py:383
  482.8 48.7 %reduce-scatter.7.cloned.1.call-done = bf16[4,96,768]{2,1,0:T(8,128)(2,1)} async-done(((bf16[4,768,768]{2,1,0:T(8,128)(2,1)}), bf16[4,96,768]{2,1,0:T(8,128)(2,1)}) %reduce-scatter.7.cloned.1.call-update) | async-done | bytes 589840 | tf_op jit(solution)/shard_map/reduce_scatter | solution.py:648
  531.5 55.7 %reduce-scatter.13.cloned.1.call-done = bf16[4,96,768]{2,1,0:T(8,128)(2,1)} async-done(((bf16[4,768,768]{2,1,0:T(8,128)(2,1)}), bf16[4,96,768]{2,1,0:T(8,128)(2,1)}) %reduce-scatter.13.cloned.1.call-update) | async-done | bytes 589840 | tf_op jit(solution)/shard_map/reduce_scatter | solution.py:648
  587.2 55.5 %reduce-scatter.11.cloned.1.call-done = bf16[4,96,768]{2,1,0:T(8,128)(2,1)} async-done(((bf16[4,768,768]{2,1,0:T(8,128)(2,1)}), bf16[4,96,768]{2,1,0:T(8,128)(2,1)}) %reduce-scatter.11.cloned.1.call-update) | async-done | bytes 589840 | tf_op jit(solution)/shard_map/reduce_scatter | solution.py:648
  642.7 55.7 %reduce-scatter.17.cloned.1.call-done = bf16[384,768]{1,0:T(8,128)(2,1)} async-done(((bf16[3072,768]{1,0:T(8,128)(2,1)}), bf16[384,768]{1,0:T(8,128)(2,1)}) %reduce-scatter.17.cloned.1.call-update) | async-done | bytes 589840 | tf_op jit(solution)/shard_map/reduce_scatter | solution.py:648
  698.3 55.5 %reduce-scatter.15.cloned.1.call-done = bf16[384,768]{1,0:T(8,128)(2,1)} async-done(((bf16[3072,768]{1,0:T(8,128)(2,1)}), bf16[384,768]{1,0:T(8,128)(2,1)}) %reduce-scatter.15.cloned.1.call-update) | async-done | bytes 589840 | tf_op jit(solution)/shard_map/reduce_scatter | solution.py:648
  756.5 26.1 %all-reduce.8 = bf16[2,8,1584]{2,0,1:T(2,128)(2,1)S(1)} all-reduce(bf16[2,8,1584]{2,0,1:T(2,128)(2,1)S(1)} %concatenate.63), channel_id=13, replica_groups=mesh['rep'=4,'fsdp'=8] {'fsdp'}, use_global_device_ids=true, to_apply=%region_4.5.clone | all-reduce | flops 25344 | bytes 101376
  783.3 10.0 %psum.51 = bf16[2,1584]{1,0:T(2,128)(2,1)S(1)} all-reduce(bf16[2,1584]{1,0:T(2,128)(2,1)S(1)} %dynamic-slice_bitcast_fusion), channel_id=1, replica_groups=mesh['rep'=4,'fsdp'=8] {'rep'}, use_global_device_ids=true, to_apply=%region_5.6 | all-reduce | flops 3168 | bytes 12672 | tf_op jit(solution)/shard_map/psum | solution.py:665
  798.5 55.5 %all-reduce.12.cloned.1.call-done = (bf16[4,96,768]{2,1,0:T(8,128)(2,1)}, bf16[4,96,768]{2,1,0:T(8,128)(2,1)}, bf16[4,96,768]{2,1,0:T(8,128)(2,1)}, bf16[4,96,76...) async-done(((bf16[4,96,768]{2,1,0:T(8,128)(2,1)}, bf16[4,96,768]{2,1,0:T(8,128)(2,1)}, bf16[4,96,768]{2,1,0:T(8,128)(2,1)}, ...) | async-done | bytes 3538960 | tf_op jit(solution)/shard_map/psum | solution.py:647
  (225 shorter events, 39.4 us)
Async XLA Ops:
  7.2 4.1 copy-start.4
  7.2 32.8 %all-gather.21.cloned.1.call-start = ((), (), s32[]{:S(2)}) async-start(), calls=%async_computation.13 | async-start | bytes 1327104 | tf_op jit(solution)/shard_map/all_gather | solution.py:609
  9.1 67.1 %all-gather.19.cloned.1.call-start = ((), (), s32[]{:S(2)}) async-start(), calls=%async_computation.12 | async-start | bytes 3981312 | tf_op jit(solution)/shard_map/all_gather | solution.py:609
  11.3 117.3 %all-gather.23.cloned.1.call-start = ((), (), s32[]{:S(2)}) async-start(), calls=%async_computation.14 | async-start | bytes 5308416 | tf_op jit(solution)/shard_map/all_gather | solution.py:609
  12.4 168.7 %all-gather.25.cloned.1.call-start = ((), (), s32[]{:S(2)}) async-start(), calls=%async_computation.15 | async-start | bytes 5308416 | tf_op jit(solution)/shard_map/all_gather | solution.py:609
  14.0 2.9 copy-start.23
  14.0 2.9 copy-start.24
  14.1 2.9 copy-start.25
  14.1 2.9 copy-start.26
  14.1 2.9 copy-start.27
  14.1 17.7 %copy-start.6 = (bf16[392,768]{1,0:T(8,128)(2,1)S(1)}, bf16[392,768]{1,0:T(8,128)(2,1)}, u32[]{:S(2)}) copy-start(bf16[392,768]{1,0:T(8,128)(2,1)} %param.19) | copy-start | bytes 1806340
  14.1 191.5 %all-gather.29.cloned.1.call-start = ((), (), s32[]{:S(2)}) async-start(), calls=%async_computation.17 | async-start | bytes 1327104 | tf_op jit(solution)/shard_map/all_gather | solution.py:609
  14.7 232.7 %all-gather.27.cloned.1.call-start = ((), (), s32[]{:S(2)}) async-start(), calls=%async_computation.16 | async-start | bytes 3981312 | tf_op jit(solution)/shard_map/all_gather | solution.py:609
  15.3 284.5 %all-gather.31.cloned.1.call-start = ((), (), s32[]{:S(2)}) async-start(), calls=%async_computation.18 | async-start | bytes 5308416 | tf_op jit(solution)/shard_map/all_gather | solution.py:609
  15.4 16.7 %copy-start.30 = (s32[2]{0:T(128)S(1)}, s32[2]{0:T(128)}, u32[]{:S(2)}) copy-start(s32[2]{0:T(128)} %param.20) | copy-start | bytes 28
  16.1 336.5 %all-gather.33.cloned.1.call-start = ((), (), s32[]{:S(2)}) async-start(), calls=%async_computation.19 | async-start | bytes 5308416 | tf_op jit(solution)/shard_map/all_gather | solution.py:609
  16.8 465.9 %reduce-scatter.9.cloned.1.call-start = ((), (), s32[]{:S(2)}) async-start(), calls=%async_computation.7 | async-start | bytes 5308416 | tf_op jit(solution)/shard_map/reduce_scatter | solution.py:648
  422.9 108.6 %reduce-scatter.7.cloned.1.call-start = ((), (), s32[]{:S(2)}) async-start(), calls=%async_computation.6 | async-start | bytes 5308416 | tf_op jit(solution)/shard_map/reduce_scatter | solution.py:648
  479.3 107.8 %reduce-scatter.13.cloned.1.call-start = ((), (), s32[]{:S(2)}) async-start(), calls=%async_computation.9 | async-start | bytes 5308416 | tf_op jit(solution)/shard_map/reduce_scatter | solution.py:648
  480.1 162.6 %reduce-scatter.11.cloned.1.call-start = ((), (), s32[]{:S(2)}) async-start(), calls=%async_computation.8 | async-start | bytes 5308416 | tf_op jit(solution)/shard_map/reduce_scatter | solution.py:648
  480.6 217.7 %reduce-scatter.17.cloned.1.call-start = ((), (), s32[]{:S(2)}) async-start(), calls=%async_computation.11 | async-start | bytes 5308416 | tf_op jit(solution)/shard_map/reduce_scatter | solution.py:648
  481.4 272.4 %reduce-scatter.15.cloned.1.call-start = ((), (), s32[]{:S(2)}) async-start(), calls=%async_computation.10 | async-start | bytes 5308416 | tf_op jit(solution)/shard_map/reduce_scatter | solution.py:648
  482.0 372.0 %all-reduce.12.cloned.1.call-start = ((), (), s32[]{:S(2)}) async-start(), calls=%async_computation.20 | async-start | bytes 7077888 | tf_op jit(solution)/shard_map/psum | solution.py:647
  753.9 40.7 %copy-start = (f32[448,768]{1,0:T(8,128)S(1)}, f32[448,768]{1,0:T(8,128)}, u32[]{:S(2)}) copy-start(f32[448,768]{1,0:T(8,128)} %get-tuple-element.59) | copy-start | bytes 4128772
  (23 other events, 39.8 us)
Sparse Core Ops, SparseCore 0:
  9.7 23.9 all-gather.20
  35.9 40.1 all-gather.18
  78.3 50.1 all-gather.22
  130.6 50.4 all-gather.24
  182.6 22.9 all-gather.28
  207.1 40.2 all-gather.26
  249.6 50.1 all-gather.30
  302.1 50.4 all-gather.32
  423.0 52.0 reduce-scatter.8
  479.5 51.9 reduce-scatter.6
  533.8 53.3 reduce-scatter.12
  589.3 53.3 reduce-scatter.10
  645.0 53.3 reduce-scatter.16
  700.5 53.3 reduce-scatter.14
  757.5 96.4 all-reduce.11

commit v2 on v1

v2 whole, which is shorter than its diff:
```python
import functools

import jax
import jax.numpy as jnp
import numpy as np
from jax import lax
from jax.experimental import pallas as pl
from jax.experimental.pallas import tpu as pltpu
from jax.sharding import PartitionSpec as P

HEADS = 12
HD = 64
WINDOW = 14
SIDE = 64
LAYERS = 2
GRID = 5
RELS = 2 * WINDOW - 1
EPSILON = 1e-06
PITCH = 16
SPAN = WINDOW * PITCH
PAIRS = HEADS // 2
LANES = 2 * HD
F32 = jnp.float32
BF16 = jnp.bfloat16
CHUNK = 256
ROWS_STEP = 64
VMEM_LIMIT = 56 * 1024 * 1024
SLAB = 384
RIDERS = 8


def dot_nn(a, b):
    return lax.dot_general(a, b, (((1,), (0,)), ((), ())), preferred_element_type=F32)


def dot_nt(a, b):
    return lax.dot_general(a, b, (((1,), (1,)), ((), ())), preferred_element_type=F32)


def dot_tn(a, b):
    return lax.dot_general(a, b, (((0,), (0,)), ((), ())), preferred_element_type=F32)


def norm_rows(values):
    centre = jnp.mean(values, -1, keepdims=True)
    centered = values - centre
    inverse = lax.rsqrt(jnp.mean(centered * centered, -1, keepdims=True) + EPSILON)
    return centered * inverse, inverse


def norm_back(grad, normed, inverse, gain):
    scaled = grad * gain
    return inverse * (
        scaled
        - jnp.mean(scaled, -1, keepdims=True)
        - normed * jnp.mean(scaled * normed, -1, keepdims=True)
    )


def each(count, step, body):
    def run(index, carry):
        body(pl.multiple_of(index * step, step))
        return carry

    lax.fori_loop(0, count, run, 0)


def each_index(count, body):
    def run(index, carry):
        body(index)
        return carry

    lax.fori_loop(0, count, run, 0)


def half_lane():
    return lax.broadcasted_iota(jnp.int32, (SPAN, LANES), 1)


def split_heads(pair):
    lane = half_lane()
    zero = jnp.zeros_like(pair)
    return jnp.concatenate(
        [jnp.where(lane < HD, pair, zero), jnp.where(lane < HD, zero, pair)], axis=0
    )


def join_heads(stacked):
    return jnp.where(half_lane() < HD, stacked[:SPAN], stacked[SPAN:])


def shift_rows(table):
    by_row = jnp.concatenate(
        [
            pltpu.roll(table[i * PITCH : (i + 1) * PITCH], i, axis=1) if i else table[:PITCH]
            for i in range(WINDOW)
        ],
        axis=0,
    )
    by_col = pltpu.roll(
        table.reshape(WINDOW, PITCH, LANES), 0, axis=2, stride=1, stride_axis=1
    ).reshape(SPAN, LANES)
    return jnp.where(half_lane() < HD, by_row, by_col)


def key_tables():
    ahead = np.zeros((SPAN, LANES), np.float32)
    back = np.zeros((SPAN, LANES), np.float32)
    for k in range(WINDOW):
        for m in range(PITCH):
            row = k * PITCH + m
            ahead[row, WINDOW - 1 + k] = 1.0
            back[row, WINDOW - 1 - k] = 1.0
            if m < WINDOW:
                ahead[row, HD + WINDOW - 1 + m] = 1.0
                back[row, HD + WINDOW - 1 - m] = 1.0
            else:
                ahead[row, LANES - 1] = -1e30
    return jnp.asarray(ahead, BF16), jnp.asarray(back, BF16)


def fetch(copies):
    for copy in copies:
        copy.start()


def attend_kernel(source, *refs):
    (x_ref, live_ref, vec_ref, table_ref, keys_ref), refs = refs[:5], refs[5:]
    weight_refs, refs = refs[: source.count], refs[source.count :]
    (mid_ref, h1_ref, q_ref, k_ref, v_ref, p_ref, att_ref), refs = refs[:7], refs[7:]
    token_ref, w_ref, sem = refs
    token_ref[...] = jnp.zeros_like(token_ref)
    ready = source.load("attend", weight_refs, w_ref, sem)
    width = x_ref.shape[1]

    def first_norm(start):
        rows = pl.ds(start, ROWS_STEP)
        normed, _ = norm_rows(x_ref[rows, :].astype(F32))
        shaped = (normed * vec_ref[0:1, :] + vec_ref[1:2, :]) * live_ref[rows, :]
        h1_ref[rows, :] = shaped.astype(BF16)

    each(x_ref.shape[0] // ROWS_STEP, ROWS_STEP, first_norm)
    ready()
    for index, (out_ref, bias) in enumerate(((q_ref, 2), (k_ref, None), (v_ref, 3))):

        def project(start, index=index, out_ref=out_ref, bias=bias):
            cols = pl.ds(start, CHUNK)
            made = dot_nn(h1_ref[...], w_ref[index, :, cols])
            if bias is not None:
                made = made + vec_ref[bias : bias + 1, cols]
            out_ref[:, cols] = made.astype(BF16)

        each(width // CHUNK, CHUNK, project)

    def attend(index):
        rows = pl.ds(pl.multiple_of(index // PAIRS * SPAN, SPAN), SPAN)
        cols = pl.ds(pl.multiple_of(index % PAIRS * LANES, LANES), LANES)
        queries = q_ref[rows, cols]
        offsets = dot_nn(queries, table_ref[...])
        lane = half_lane()
        sides = []
        for half in range(2):
            moved = shift_rows(offsets[:, half * LANES : (half + 1) * LANES])
            sides.append(jnp.where(lane == LANES - 1, 1.0, moved).astype(BF16))
        left = jnp.concatenate(
            [split_heads(queries) * HD ** (-0.5), jnp.concatenate(sides, axis=0)], axis=1
        )
        right = jnp.concatenate([k_ref[rows, cols], keys_ref[...]], axis=1)
        scores = dot_nt(left, right)
        shifted = jnp.exp(scores - jnp.max(scores, -1, keepdims=True))
        probs = shifted * (1.0 / jnp.sum(shifted, -1, keepdims=True))
        low = probs.astype(BF16)
        p_ref[index] = low
        att_ref[rows, cols] = join_heads(dot_nn(low, v_ref[rows, cols])).astype(BF16)

    each_index(x_ref.shape[0] // SPAN * PAIRS, attend)

    def finish(start):
        cols = pl.ds(start, CHUNK)
        branch = dot_nn(att_ref[...], w_ref[3, :, cols]) + vec_ref[4:5, cols]
        mid_ref[:, cols] = x_ref[:, cols].astype(F32) + live_ref[...] * branch

    each(width // CHUNK, CHUNK, finish)


def mlp_kernel(plan, source, top, *refs):
    (mid_ref, live_ref, vec_ref, bias_ref), refs = refs[:4], refs[4:]
    if top:
        (grad_ref,), refs = refs[:1], refs[1:]
    weight_refs, refs = refs[: source.count], refs[source.count :]
    if top:
        (h2_ref, act_ref, slope_ref, sums_ref), refs = refs[:4], refs[4:]
        sink_refs, refs = refs[: plan.sinks], refs[plan.sinks :]
        (w1_ref, dm_ref, sem), refs = refs[:3], refs[3:]
        sink = plan.sink(sink_refs, refs)
    else:
        out_ref, h2_ref, act_ref, slope_ref, token_ref, w1_ref, w2_ref, sem, sem2 = refs
        token_ref[...] = jnp.zeros_like(token_ref)
    ready1 = source.load("fc1", weight_refs, w1_ref, sem)
    if not top:
        ready2 = source.load("fc2", weight_refs, w2_ref, sem2)
    width = mid_ref.shape[1]
    hidden_width = act_ref.shape[1]

    def second_norm(start):
        rows = pl.ds(start, ROWS_STEP)
        normed, _ = norm_rows(mid_ref[rows, :])
        h2_ref[rows, :] = (normed * vec_ref[5:6, :] + vec_ref[6:7, :]).astype(BF16)

    each(mid_ref.shape[0] // ROWS_STEP, ROWS_STEP, second_norm)
    ready1()

    def expand(index):
        start = pl.multiple_of(index * CHUNK, CHUNK)
        cols = pl.ds(start, CHUNK)
        inner = pl.ds(pl.multiple_of(start % width, CHUNK), CHUNK)
        hidden = dot_nn(h2_ref[...], w1_ref[start // width, :, inner]) + bias_ref[:, cols]
        below = 0.5 * (1.0 + lax.erf(hidden * (0.5**0.5)))
        bell = jnp.exp(-0.5 * hidden * hidden) * (0.5 / np.pi) ** 0.5
        act_ref[:, cols] = (hidden * below).astype(BF16)
        slope_ref[:, cols] = (below + hidden * bell).astype(BF16)

    each_index(hidden_width // CHUNK, expand)
    if top:
        sums_ref[...] = jnp.zeros_like(sums_ref)
        second_weight(grad_ref, live_ref, act_ref, dm_ref, sums_ref, sink)
        sink.start()
        sink.wait()
    else:
        ready2()
        contract(act_ref, w2_ref, vec_ref, mid_ref, live_ref, out_ref)


def contract(act_ref, w2_ref, vec_ref, mid_ref, live_ref, out_ref):
    def run(start):
        cols = pl.ds(start, CHUNK)
        made = dot_nn(act_ref[...], w2_ref[:, cols]) + vec_ref[7:8, cols]
        out_ref[:, cols] = mid_ref[:, cols] + live_ref[...] * made

    each(out_ref.shape[1] // CHUNK, CHUNK, run)


def out_kernel(source, act_ref, vec_ref, mid_ref, live_ref, *refs):
    weight_refs, (out_ref, w2_ref, sem) = refs[: source.count], refs[source.count :]
    source.load("fc2", weight_refs, w2_ref, sem)()
    contract(act_ref, w2_ref, vec_ref, mid_ref, live_ref, out_ref)


def second_weight(grad_ref, live_ref, act_ref, dm_ref, sums_ref, sink):
    dm_ref[...] = (live_ref[...] * grad_ref[...].astype(F32)).astype(BF16)
    sums_ref[0:1, :] = jnp.sum(dm_ref[...].astype(F32), 0, keepdims=True)

    def run(index):
        rows = pl.ds(pl.multiple_of(index * SLAB, SLAB), SLAB)
        sink.rows(index, dot_tn(act_ref[:, rows], dm_ref[...]).astype(BF16))

    each_index(act_ref.shape[1] // SLAB, run)


def hidden_back_kernel(plan, source, top, *refs):
    (grad_ref, live_ref, h2_ref, act_ref, slope_ref), refs = refs[:5], refs[5:]
    weight_refs, refs = refs[: source.count], refs[source.count :]
    (dh_ref, sums_ref, hsum_ref), refs = refs[:3], refs[3:]
    sink_refs, refs = refs[: plan.sinks], refs[plan.sinks :]
    if not top:
        more_refs, refs = refs[: plan.sinks], refs[plan.sinks :]
    (w2_ref, dm_ref, sem), refs = refs[:3], refs[3:]
    sink = plan.sink(sink_refs, refs)
    if not top:
        more = plan.sink(more_refs, refs[plan.sink_scratch :])
    ready = source.load("fc2", weight_refs, w2_ref, sem)
    width = h2_ref.shape[1]
    hidden_width = act_ref.shape[1]
    sums_ref[...] = jnp.zeros_like(sums_ref)
    if top:
        dm_ref[...] = (live_ref[...] * grad_ref[...].astype(F32)).astype(BF16)
    else:
        second_weight(grad_ref, live_ref, act_ref, dm_ref, sums_ref, more)
        more.start()
    ready()

    def inner_grad(start):
        cols = pl.ds(start, CHUNK)
        made = (dot_nt(dm_ref[...], w2_ref[cols, :]) * slope_ref[:, cols].astype(F32)).astype(BF16)
        dh_ref[:, cols] = made
        hsum_ref[:, cols] = jnp.sum(made.astype(F32), 0, keepdims=True)

    each(hidden_width // CHUNK, CHUNK, inner_grad)

    def first_weight(index):
        start = pl.multiple_of(index * CHUNK, CHUNK)
        inner = pl.ds(pl.multiple_of(start % width, CHUNK), CHUNK)
        sink.cols(
            start // width, inner, dot_tn(h2_ref[...], dh_ref[:, pl.ds(start, CHUNK)]).astype(BF16)
        )

    each_index(hidden_width // CHUNK, first_weight)
    sink.start()
    if not top:
        more.wait()
    sink.wait()


def middle_back_kernel(source, *refs):
    (grad_ref, mid_ref, vec_ref, dh_ref), refs = refs[:4], refs[4:]
    weight_refs, refs = refs[: source.count], refs[source.count :]
    dmid_ref, sums_ref, w1_ref, ds_ref, sem = refs
    source.load("fc1", weight_refs, w1_ref, sem)()
    width = mid_ref.shape[1]
    hidden_width = dh_ref.shape[1]

    def back_in(start):
        rows = pl.ds(start, CHUNK)
        made = dot_nt(dh_ref[:, 0:width], w1_ref[0, rows, :])
        for block in range(1, hidden_width // width):
            made += dot_nt(
                dh_ref[:, block * width : (block + 1) * width], w1_ref[block, rows, :]
            )
        ds_ref[:, rows] = made

    each(width // CHUNK, CHUNK, back_in)
    sums_ref[...] = jnp.zeros_like(sums_ref)

    def back_norm(start):
        rows = pl.ds(start, ROWS_STEP)
        normed, inverse = norm_rows(mid_ref[rows, :])
        grad = ds_ref[rows, :]
        sums_ref[1:2, :] += jnp.sum(grad * normed, 0, keepdims=True)
        sums_ref[2:3, :] += jnp.sum(grad, 0, keepdims=True)
        dmid_ref[rows, :] = grad_ref[rows, :].astype(F32) + norm_back(
            grad, normed, inverse, vec_ref[5:6, :]
        )

    each(mid_ref.shape[0] // ROWS_STEP, ROWS_STEP, back_norm)


def scores_back_kernel(source, *refs):
    (
        dmid_ref, live_ref, table_ref, keys_ref, q_ref, k_ref, v_ref, p_ref,
    ), refs = refs[:8], refs[8:]
    weight_refs, refs = refs[: source.count], refs[source.count :]
    db_ref, dq_ref, dk_ref, dv_ref, sums_ref, rel_ref, w_ref, da_ref, sem = refs
    ready = source.load("attend", weight_refs, w_ref, sem)
    width = dmid_ref.shape[1]
    db_ref[...] = (live_ref[...] * dmid_ref[...]).astype(BF16)
    sums_ref[...] = jnp.zeros_like(sums_ref)
    sums_ref[0:1, :] = jnp.sum(db_ref[...].astype(F32), 0, keepdims=True)
    rel_ref[...] = jnp.zeros_like(rel_ref)
    ready()

    def back_out(start):
        rows = pl.ds(start, CHUNK)
        da_ref[:, rows] = dot_nt(db_ref[...], w_ref[3, rows, :]).astype(BF16)

    each(width // CHUNK, CHUNK, back_out)

    def attend(index):
        rows = pl.ds(pl.multiple_of(index // PAIRS * SPAN, SPAN), SPAN)
        cols = pl.ds(pl.multiple_of(index % PAIRS * LANES, LANES), LANES)
        low = p_ref[index]
        probs = low.astype(F32)
        outer = split_heads(da_ref[rows, cols])
        queries = split_heads(q_ref[rows, cols])
        d_probs = dot_nt(outer, v_ref[rows, cols])
        dv_ref[rows, cols] = dot_tn(low, outer).astype(BF16)
        mean = jnp.sum(d_probs * probs, -1, keepdims=True)
        d_scores = (probs * (d_probs - mean)).astype(BF16)
        both = dot_nn(d_scores, jnp.concatenate([k_ref[rows, cols], keys_ref[...]], axis=1))
        moved = [
            shift_rows(both[half * SPAN : (half + 1) * SPAN, LANES:]).astype(BF16)
            for half in range(2)
        ]
        rel_part = dot_nt(jnp.concatenate(moved, axis=1), table_ref[...])
        direct = join_heads(both[:, :LANES]) * HD ** (-0.5)
        dq_ref[rows, cols] = (direct + rel_part).astype(BF16)
        dk_ref[rows, cols] = (dot_tn(d_scores, queries) * HD ** (-0.5)).astype(BF16)
        rel_ref[...] += dot_tn(jnp.concatenate(moved, axis=0), queries)

    each_index(dmid_ref.shape[0] // SPAN * PAIRS, attend)
    sums_ref[1:2, :] = jnp.sum(dq_ref[...].astype(F32), 0, keepdims=True)
    sums_ref[2:3, :] = jnp.sum(dv_ref[...].astype(F32), 0, keepdims=True)


def first_weights_kernel(plan, rotated, *refs):
    (h1_ref, att_ref, db_ref, dq_ref, dk_ref, dv_ref), refs = refs[:6], refs[6:]
    sink = plan.sink(refs[: plan.sinks], refs[plan.sinks :], rotated)
    pairs = ((h1_ref, dq_ref), (h1_ref, dk_ref), (h1_ref, dv_ref), (att_ref, db_ref))
    for index, (left_ref, right_ref) in enumerate(pairs):

        def weight(start, index=index, left_ref=left_ref, right_ref=right_ref):
            cols = pl.ds(start, CHUNK)
            sink.cols(index, cols, dot_tn(left_ref[...], right_ref[:, cols]).astype(BF16))

        each(h1_ref.shape[1] // CHUNK, CHUNK, weight)
    sink.start()
    sink.wait()


def first_back_kernel(source, *refs):
    (dmid_ref, x_ref, live_ref, vec_ref, dq_ref, dk_ref, dv_ref), refs = refs[:7], refs[7:]
    weight_refs, refs = refs[: source.count], refs[source.count :]
    next_ref, sums_ref, w_ref, dh_ref, sem = refs
    source.load("attend", weight_refs, w_ref, sem)()
    width = x_ref.shape[1]

    def back_in(start):
        rows = pl.ds(start, CHUNK)
        made = dot_nt(dq_ref[...], w_ref[0, rows, :])
        made += dot_nt(dk_ref[...], w_ref[1, rows, :])
        made += dot_nt(dv_ref[...], w_ref[2, rows, :])
        dh_ref[:, rows] = made * live_ref[...]

    each(width // CHUNK, CHUNK, back_in)
    sums_ref[...] = jnp.zeros_like(sums_ref)

    def back_norm(start):
        rows = pl.ds(start, ROWS_STEP)
        normed, inverse = norm_rows(x_ref[rows, :].astype(F32))
        grad = dh_ref[rows, :]
        sums_ref[3:4, :] += jnp.sum(grad * normed, 0, keepdims=True)
        sums_ref[4:5, :] += jnp.sum(grad, 0, keepdims=True)
        next_ref[rows, :] = dmid_ref[rows, :] + norm_back(grad, normed, inverse, vec_ref[0:1, :])

    each(x_ref.shape[0] // ROWS_STEP, ROWS_STEP, back_norm)


VM = pl.BlockSpec(memory_space=pltpu.VMEM)
ANY = pl.BlockSpec(memory_space=pl.ANY)


def shape(dims, kind):
    return jax.ShapeDtypeStruct(tuple(dims), kind)


class Source:
    def __init__(self, **parts):
        self.parts = parts
        self.arrays = []
        self.places = {}
        for name, (arrays, _, _) in parts.items():
            found = []
            for array in arrays:
                known = [i for i, other in enumerate(self.arrays) if other is array]
                if not known:
                    known = [len(self.arrays)]
                    self.arrays.append(array)
                found.append(known[0])
            self.places[name] = found
        self.count = len(self.arrays)

    def semaphores(self, name):
        whole = self.parts[name][1] is None
        return pltpu.SemaphoreType.DMA((4 if whole else 32,))

    def load(self, name, refs, target, sem):
        arrays, block, rotated = self.parts[name]
        refs = [refs[i] for i in self.places[name]]
        if block is None:
            pairs = whole_pairs(name, refs, target)
        else:
            pairs = piece_pairs(name, refs, target, block, rotated)
        copies = [
            pltpu.make_async_copy(given, taken, sem.at[i])
            for i, (given, taken) in enumerate(pairs)
        ]
        for copy in copies:
            copy.start()

        def ready():
            for copy in copies:
                copy.wait()

        return ready


def whole_pairs(name, refs, target):
    if name == "fc2":
        return [(refs[0], target)]
    width = target.shape[1]
    pairs = []
    for ref in refs:
        for start in range(0, ref.shape[1], width):
            pairs.append((ref.at[:, pl.ds(start, width)], target.at[len(pairs)]))
    return pairs


def position():
    shard = lax.axis_index("fsdp")
    return lax.axis_index("rep"), shard >> 1, shard & 1


def piece_pairs(name, refs, target, block, rotated):
    rep, level, core = position()
    pairs = []
    for parity in range(2):
        for part, (away, levels) in enumerate(
            ((0, range(4)), (1, range(4)), (2, range(4)), (3, range(2)), (3, range(2, 4)))
        ):
            ref = refs[parity * 5 + part]
            for place, step in enumerate(levels):
                source_level = (level - step) & 3 if rotated else step
                shard = source_level * 2 + (core ^ parity)
                kind = rep ^ away
                rows = target.shape[-2] // 8
                if name == "fc2":
                    span = rows // 4
                    start = shard * rows + kind * span
                    taken = target.at[pl.ds(pl.multiple_of(start, 16), span), :]
                else:
                    span = rows
                    start = pl.multiple_of(shard * span, 16)
                    taken = target.at[kind, pl.ds(start, span), :]
                pairs.append((ref.at[place, block, pl.ds(0, span), :], taken))
    return pairs


class WholeSink:
    def __init__(self, refs):
        self.ref = refs[0]

    def rows(self, index, value):
        self.ref[pl.ds(pl.multiple_of(index * SLAB, SLAB), SLAB), :] = value

    def cols(self, block, cols, value):
        self.ref[block, :, cols] = value

    def start(self):
        pass

    def wait(self):
        pass


class PieceSink:
    def __init__(self, refs, scratch, rotated):
        self.held, sem = scratch[:2]
        rep, level, core = position()
        self.copies = []
        for parity in range(2):
            for away in range(4):
                given = self.held.at[core ^ parity, rep ^ away]
                taken = refs[parity].at[away]
                moves = [(given, taken)]
                if rotated:
                    moves = [(given.at[(level + step) & 3], taken.at[step]) for step in range(4)]
                for move in moves:
                    self.copies.append(pltpu.make_async_copy(*move, sem.at[len(self.copies)]))

    def rows(self, index, value):
        span = self.held.shape[3]
        for block in range(4):
            self.held[index & 1, block, index >> 1] = value[block * span : (block + 1) * span]

    def cols(self, block, cols, value):
        span = self.held.shape[3]
        for shard in range(8):
            self.held[shard & 1, block, shard >> 1, :, cols] = value[
                shard * span : (shard + 1) * span
            ]

    def start(self):
        for copy in self.copies:
            copy.start()

    def wait(self):
        for copy in self.copies:
            copy.wait()


class WholePlan:
    sinks = 1
    sink_scratch = 0

    def sink(self, refs, scratch, rotated=False):
        return WholeSink(refs)

    def sink_outs(self, dims):
        return [shape(dims, BF16)], [VM], []


class PiecePlan:
    sinks = 2
    sink_scratch = 2

    def sink(self, refs, scratch, rotated=False):
        return PieceSink(refs, scratch, rotated)

    def sink_outs(self, dims):
        width = dims[-1]
        span = int(np.prod(dims)) // width // 32
        outs = [shape((4, 4, span, width), BF16)] * 2
        scratch = [pltpu.VMEM((2, 4, 4, span, width), BF16), pltpu.SemaphoreType.DMA((32,))]
        return outs, [ANY] * 2, scratch


def call(kernel, resident, source, outs, scratch, micros, sinks=(), after=()):
    specs = [VM] * len(outs)
    outs = list(outs)
    scratch = list(scratch)
    for more_outs, more_specs, more_scratch in sinks:
        outs += more_outs
        specs += more_specs
        scratch += more_scratch
    first = len(resident) + source.count

    def body(*refs):
        kernel(*refs[:first], *refs[first + len(after) :])

    return pl.pallas_call(
        body,
        out_shape=tuple(outs),
        in_specs=[VM] * len(resident) + [ANY] * (source.count + len(after)),
        out_specs=tuple(specs),
        scratch_shapes=scratch,
        compiler_params=pltpu.CompilerParams(vmem_limit_bytes=VMEM_LIMIT),
        cost_estimate=pl.CostEstimate(
            flops=int(micros * 1e9), bytes_accessed=1 << 20, transcendentals=0
        ),
    )(*resident, *source.arrays, *after)


def attend_forward(x, live, vec, table, keys, source, after):
    rows, width = x.shape
    outs = (
        shape((rows, width), F32),
        *[shape((rows, width), BF16)] * 4,
        shape((rows // SPAN * PAIRS, 2 * SPAN, SPAN), BF16),
        shape((rows, width), BF16),
        shape((8, LANES), F32),
    )
    scratch = [pltpu.VMEM((4, width, width), BF16), source.semaphores("attend")]
    return call(
        functools.partial(attend_kernel, source),
        (x, live, vec, table, keys), source, outs, scratch, 20, (), after,
    )


def mlp_forward(plan, top, mid, live, vec, bias, grad, source, after):
    rows, width = mid.shape
    hidden = bias.shape[1]
    outs = [
        shape((rows, width), BF16), shape((rows, hidden), BF16), shape((rows, hidden), BF16),
    ]
    scratch = [pltpu.VMEM((hidden // width, width, width), BF16)]
    resident = [mid, live, vec, bias]
    sinks = []
    if top:
        resident.append(grad)
        outs.append(shape((8, width), F32))
        scratch += [pltpu.VMEM((rows, width), BF16), source.semaphores("fc1")]
        sinks.append(plan.sink_outs((hidden, width)))
    else:
        outs.insert(0, shape((rows, width), F32))
        outs.append(shape((8, LANES), F32))
        scratch += [
            pltpu.VMEM((hidden, width), BF16), source.semaphores("fc1"),
            source.semaphores("fc2"),
        ]
    return call(
        functools.partial(mlp_kernel, plan, source, top),
        resident, source, outs, scratch, 16, sinks, after,
    )


def mlp_output(act, vec, mid, live, source, after):
    hidden, width = act.shape[1], mid.shape[1]
    scratch = [pltpu.VMEM((hidden, width), BF16), source.semaphores("fc2")]
    return call(
        functools.partial(out_kernel, source), (act, vec, mid, live), source,
        [shape(mid.shape, F32)], scratch, 5, (), after,
    )[0]


def hidden_backward(plan, top, grad, live, h2, act, slope, source, after):
    rows, width = h2.shape
    hidden = act.shape[1]
    outs = [shape((rows, hidden), BF16), shape((8, width), F32), shape((1, hidden), F32)]
    sinks = [plan.sink_outs((hidden // width, width, width))]
    if not top:
        sinks.append(plan.sink_outs((hidden, width)))
    scratch = [
        pltpu.VMEM((hidden, width), BF16), pltpu.VMEM((rows, width), BF16),
        source.semaphores("fc2"),
    ]
    return call(
        functools.partial(hidden_back_kernel, plan, source, top),
        (grad, live, h2, act, slope), source, outs, scratch, 15, sinks, after,
    )


def middle_backward(grad, mid, vec, dh, source, after):
    rows, width = mid.shape
    hidden = dh.shape[1]
    outs = [shape((rows, width), F32), shape((8, width), F32)]
    scratch = [
        pltpu.VMEM((hidden // width, width, width), BF16), pltpu.VMEM((rows, width), F32),
        source.semaphores("fc1"),
    ]
    return call(
        functools.partial(middle_back_kernel, source),
        (grad, mid, vec, dh), source, outs, scratch, 10, (), after,
    )


def scores_backward(dmid, live, table, keys, q, k, v, p, source, after):
    rows, width = dmid.shape
    outs = [*[shape((rows, width), BF16)] * 4, shape((8, width), F32), shape((LANES, LANES), F32)]
    scratch = [
        pltpu.VMEM((4, width, width), BF16), pltpu.VMEM((rows, width), BF16),
        source.semaphores("attend"),
    ]
    return call(
        functools.partial(scores_back_kernel, source),
        (dmid, live, table, keys, q, k, v, p), source, outs, scratch, 15, (), after,
    )


def first_weights(plan, rotated, h1, att, db, dq, dk, dv, after):
    width = h1.shape[1]
    return call(
        functools.partial(first_weights_kernel, plan, rotated), (h1, att, db, dq, dk, dv),
        Source(), [], [], 8, [plan.sink_outs((4, width, width))], after,
    )


def first_backward(dmid, x, live, vec, dq, dk, dv, source, after):
    rows, width = x.shape
    outs = [shape((rows, width), F32), shape((8, width), F32)]
    scratch = [
        pltpu.VMEM((4, width, width), BF16), pltpu.VMEM((rows, width), F32),
        source.semaphores("attend"),
    ]
    return call(
        functools.partial(first_back_kernel, source),
        (dmid, x, live, vec, dq, dk, dv), source, outs, scratch, 8, (), after,
    )


def live_rows(slot_table):
    places = jnp.arange(PITCH, dtype=jnp.int32)
    rows_inside = slot_table[:, None] // GRID * WINDOW + places[None, :WINDOW] < SIDE
    cols_inside = slot_table[:, None] % GRID * WINDOW + places[None, :] < SIDE
    cols_inside = cols_inside & (places < WINDOW)[None, :]
    both_inside = rows_inside[:, :, None] & cols_inside[:, None, :]
    return both_inside.astype(F32).reshape(slot_table.shape[0] * SPAN, 1)


def spread(values):
    width = values.shape[1]
    grid = values.reshape(-1, WINDOW, width)
    return jnp.pad(grid, ((0, 0), (0, PITCH - WINDOW), (0, 0))).reshape(-1, width)


def gather_back(values):
    width = values.shape[1]
    return values.reshape(-1, PITCH, width)[:, :WINDOW].reshape(-1, width)


def relative_tables(rel_height, rel_width):
    stacked = jnp.stack([rel_height, rel_width], 1).reshape(LAYERS, 2, RELS, HD)

    def spread_table(rows):
        padded = jnp.pad(rows, ((0, 0), (0, 0), (0, HD - RELS), (0, 0)))
        one = padded.reshape(LAYERS, LANES, HD).transpose(0, 2, 1)
        none = jnp.zeros_like(one)
        return jnp.concatenate(
            [jnp.concatenate([one, none], 2), jnp.concatenate([none, one], 2)], 1
        )

    return spread_table(stacked[:, :, ::-1]), spread_table(stacked)


def whole_weights(weights):
    qkv, proj, fc1, fc2 = weights
    layers = []
    for layer in range(LAYERS):
        q, p, a, b = (
            lax.all_gather(w[layer], "fsdp", axis=0, tiled=True) for w in (qkv, proj, fc1, fc2)
        )
        layers.append(
            dict(attend=((q, p), None, False), fc1=((a,), None, False), fc2=((b,), None, False))
        )
    return layers


def whole_small(parts):
    packed = jnp.concatenate(parts, axis=1)
    return lax.all_gather(packed, "fsdp", axis=0, tiled=False)


def whole_reduce(value, axis):
    return lax.psum(
        lax.psum_scatter(value, "fsdp", scatter_dimension=axis, tiled=True), "rep"
    ).astype(F32)


def whole_sums(grads, small):
    big = []
    for (g,), (g1,), (g2,) in grads:
        g, g1, g2 = whole_reduce(g, 1), whole_reduce(g1, 1), whole_reduce(g2, 0)
        big.append(
            (jnp.concatenate([g[0], g[1], g[2]], 1), g[3], jnp.concatenate(list(g1), 1), g2)
        )
    mine = whole_reduce(small.astype(BF16), 1)[:, 0]
    return big, mine


def permute(value, axis, move):
    return lax.ppermute(value, axis, [(i, move(i)) for i in range({"rep": 4, "fsdp": 8}[axis])])


def to_x(value):
    return permute(value, "rep", lambda i: i ^ 1)


def to_y(value):
    return permute(value, "rep", lambda i: i ^ 2)


def to_xy(value):
    return permute(value, "rep", lambda i: i ^ 3)


def to_core(value):
    return permute(value, "fsdp", lambda i: i ^ 1)


def to_level(value, step):
    return permute(value, "fsdp", lambda i: (i + 2 * step) % 8)


LEVELS = [[0, 2, 4, 6], [1, 3, 5, 7]]


def swap(value, flag, axis):
    first = lax.slice_in_dim(value, 0, 1, axis=axis)
    second = lax.slice_in_dim(value, 1, 2, axis=axis)
    return jnp.where(flag == 1, jnp.concatenate([second, first], axis), value)


def by_replica(value, rep):
    rest = value.shape[1:]
    value = value.reshape(2, 2, *rest)
    value = swap(swap(value, rep & 1, 1), rep >> 1, 0)
    return value.reshape(4, *rest)


def turn(value, start, axis):
    size = value.shape[axis]
    return lax.dynamic_slice_in_dim(
        jnp.concatenate([value, value], axis), start, size, axis
    )


def own_blocks(weights, layer, rep):
    qkv, proj, fc1, fc2 = (w[layer] for w in weights)
    width = proj.shape[1]
    span = proj.shape[0]
    first = lax.dynamic_slice_in_dim(jnp.concatenate([qkv, proj], 1), rep * width, width, 1)
    second = lax.dynamic_slice_in_dim(fc1, rep * width, width, 1)
    third = lax.dynamic_slice_in_dim(fc2, rep * span, span, 0)
    return first, second, third


class Across:
    def __init__(self, held):
        self.held = held
        self.x, self.y = to_x(held), to_y(held)

    def finish(self, token=None):
        low, high = self.y[:2], self.x[2:]
        if token is not None:
            low, high = low + token, high + token
        pieces = (self.held, self.x, self.y, to_x(low), to_y(high))
        return pieces + tuple(to_core(piece) for piece in pieces)


class PieceWeights:
    def __init__(self, weights, small):
        rep, level, core = position()
        blocks = [own_blocks(weights, layer, rep) for layer in range(LAYERS)]
        self.width = blocks[0][0].shape[1]
        self.size = small.shape[0] // 4
        rider = lax.dynamic_slice_in_dim(small, rep * self.size, self.size, 0)
        rider = jnp.pad(rider, (0, RIDERS * self.width - self.size)).reshape(RIDERS, self.width)
        first = jnp.concatenate([blocks[0][0], rider], 0)[None, None]
        held = jnp.concatenate([first] + [to_level(first, step) for step in (1, 2, 3)], 0)
        self.rest0 = self.levels(blocks[0][1:])
        self.rest1 = self.levels(blocks[1][:2])
        self.last = lax.all_gather(weights[3][1], "fsdp", axis=0, tiled=True)
        self.group_a = Across(held).finish()
        self.next_b = Across(self.rest0)
        span = blocks[0][0].shape[0]
        riders = jnp.stack(
            [
                jnp.concatenate(
                    [t[:, 0, span:] for t in self.group_a[5 * p : 5 * p + 5]], 0
                ).reshape(4, 4, RIDERS * self.width)[:, :, : self.size]
                for p in range(2)
            ]
        )
        riders = by_replica(swap(riders, core, 0).transpose(1, 0, 2, 3), rep)
        turned = jnp.concatenate([riders[:, :, i : i + 1] for i in (3, 2, 1, 0)], 2)
        riders = turn(turned, 3 - level, 2)
        self.small = riders.transpose(2, 1, 0, 3).reshape(8, LAYERS, -1)

    def levels(self, parts):
        span, width = parts[0].shape
        joined = lax.all_gather(
            jnp.concatenate(parts, 0), "fsdp", axis=0, tiled=True, axis_index_groups=LEVELS
        )
        return joined.reshape(4, len(parts), span, width)

    def before(self, name):
        if name == "attend_0":
            return (self.rest0,)
        if name == "mlp_0":
            return (self.next_c.held,)
        return ()

    def passed(self, name, token):
        if name == "attend_0":
            token = token[0, 0].astype(BF16)
            self.group_b = self.next_b.finish(token)
            self.next_c = Across(self.rest1 + token)
        if name == "mlp_0":
            self.group_c = self.next_c.finish(token[0, 0].astype(BF16))

    def source(self, layer, *names):
        if layer == 0:
            parts = dict(
                attend=lambda: (self.group_a, 0, True),
                fc1=lambda: (self.group_b, 0, False),
                fc2=lambda: (self.group_b, 1, False),
            )
        else:
            parts = dict(
                attend=lambda: (self.group_c, 0, False),
                fc1=lambda: (self.group_c, 1, False),
                fc2=lambda: ((self.last,), None, False),
            )
        return Source(**{name: parts[name]() for name in names})


class WholeWeights:
    def __init__(self, weights, small):
        self.small = whole_small(small)
        self.layers = whole_weights(weights)

    def before(self, name):
        return ()

    def passed(self, name, token):
        pass

    def source(self, layer, *names):
        return Source(**{name: self.layers[layer][name] for name in names})


class ReplicaSum:
    def __init__(self, pair):
        self.keep, send = pair
        self.got = to_core(send)
        self.step = 0

    def both(self, away, part):
        return self.keep[away, part].astype(F32) + self.got[away, part].astype(F32)

    def advance(self):
        low, high = slice(0, 2), slice(2, 4)
        self.step += 1
        if self.step == 1:
            send_x = jnp.stack([self.both(1, low), self.both(3, low)]).astype(BF16)
            send_y = jnp.stack([self.both(2, high), self.both(3, high)]).astype(BF16)
            self.x, self.y = to_x(send_x), to_y(send_y)
            return [send_x, send_y]
        if self.step == 2:
            send_y = (self.both(2, low) + self.x[1].astype(F32)).astype(BF16)
            send_x = (self.both(1, high) + self.y[1].astype(F32)).astype(BF16)
            self.last_y, self.last_x = to_y(send_y), to_x(send_x)
            return [send_x, send_y]
        self.result = jnp.concatenate(
            [
                self.both(0, low) + self.x[0].astype(F32) + self.last_y.astype(F32),
                self.both(0, high) + self.y[0].astype(F32) + self.last_x.astype(F32),
            ],
            0,
        ).astype(BF16)
        return [self.result]


def sum_levels(parts):
    joined = jnp.stack(parts, 1)
    _, count, span, width = joined.shape
    mine = lax.psum_scatter(
        joined.reshape(-1, width), "fsdp", scatter_dimension=0, tiled=True,
        axis_index_groups=LEVELS,
    )
    return lax.all_gather(mine, "rep", axis=0, tiled=True).reshape(4, count, span, width)


def ride_along(small, width, rep, level, core):
    size = small.shape[0] * small.shape[2] // 4
    flat = small.transpose(1, 0, 2).reshape(4, 2, 4, size)
    flat = jnp.pad(flat, ((0, 0), (0, 0), (0, 0), (0, RIDERS * width - size)))
    flat = turn(flat, level, 0).transpose(1, 2, 0, 3)
    flat = swap(flat, core, 0).transpose(1, 0, 2, 3)
    flat = by_replica(flat, rep).transpose(1, 0, 2, 3)
    return flat.reshape(2, 4, 4, RIDERS, width).astype(BF16)


class PieceSums:
    def __init__(self):
        self.open = []
        self.sums = {}
        self.top = None

    def add(self, name, pair):
        self.sums[name] = ReplicaSum(pair)

    def sum_top(self):
        self.top = sum_levels([self.sums[f"{n}_1"].result for n in ("fc2", "fc1", "attend")])

    def advance(self, *names):
        found = []
        for name in names:
            found += self.sums[name].advance()
        return found

    def finish(self, pair, small):
        rep, level, core = position()
        span, width = pair[0].shape[2:]
        riders = ride_along(small, width, rep, level, core)
        keep, send = pair
        self.add(
            "last",
            (jnp.concatenate([keep, riders[0]], 2), jnp.concatenate([send, riders[1]], 2)),
        )
        rest = sum_levels([self.sums[f"{n}_0"].result for n in ("fc2", "fc1")])
        self.advance("last")
        self.advance("last")
        self.advance("last")
        mine = self.sums["last"].result
        total = mine[0].astype(F32)
        for step in (1, 2, 3):
            total = total + to_level(mine[step], step).astype(F32)
        total = total.astype(BF16)
        last = jnp.stack([total, to_x(total), to_y(total), to_xy(total)])
        last = by_replica(last, rep).astype(F32)

        def named(first, second, third):
            first, second, third = (t.astype(F32) for t in (first, second, third))
            return (
                jnp.concatenate([first[0], first[1], first[2]], 1),
                first[3],
                jnp.concatenate(list(second), 1),
                third.reshape(-1, width),
            )

        size = small.shape[0] * small.shape[2] // 4
        tiny = last[:, span:].reshape(4, -1)[:, :size].reshape(LAYERS, -1)
        top = self.top
        return [
            named(last[:, :span], rest[:, 1], rest[:, 0]),
            named(top[:, 2], top[:, 1], top[:, 0]),
        ], tiny


class WholeSums:
    def __init__(self):
        self.pairs = {}

    def add(self, name, pair):
        self.pairs[name] = pair

    def advance(self, *names):
        return ()

    def sum_top(self):
        pass

    def finish(self, pair, small):
        grads = [
            (pair, self.pairs["fc1_0"], self.pairs["fc2_0"]),
            tuple(self.pairs[f"{name}_1"] for name in ("attend", "fc1", "fc2")),
        ]
        return whole_sums(grads, small)


def on_device(
    ring, windows, slot_table, cotangent, qkv_weight, qv_bias, proj_weight, proj_bias,
    norm1_gain, norm1_bias, norm2_gain, norm2_bias, fc1_weight, fc1_bias, fc2_weight, fc2_bias,
    rel_height, rel_width,
):
    width = windows.shape[1]
    weights = (qkv_weight, proj_weight, fc1_weight, fc2_weight)
    parts = (
        qv_bias, proj_bias, norm1_gain, norm1_bias, norm2_gain, norm2_bias, fc1_bias, fc2_bias,
        rel_height, rel_width,
    )
    cuts = np.cumsum([0] + [part.shape[1] for part in parts])
    if ring:
        plan, pending = PiecePlan(), PieceSums()
        held = PieceWeights(weights, jnp.concatenate(parts, 1).reshape(-1))
    else:
        plan, pending = WholePlan(), WholeSums()
        held = WholeWeights(weights, parts)
    small = held.small
    (
        qv_bias_w, proj_bias_w, norm1_gain_w, norm1_bias_w, norm2_gain_w, norm2_bias_w,
        fc1_bias_w, fc2_bias_w, rel_height_w, rel_width_w,
    ) = [
        small[:, :, a:b].transpose(1, 0, 2).reshape(LAYERS, -1) for a, b in zip(cuts, cuts[1:])
    ]
    vec = jnp.stack(
        [norm1_gain_w, norm1_bias_w, qv_bias_w[:, :width], qv_bias_w[:, width:], proj_bias_w,
         norm2_gain_w, norm2_bias_w, fc2_bias_w], 1
    ).astype(F32)
    hidden_bias = fc1_bias_w.astype(F32)[:, None, :]
    ahead, back = relative_tables(rel_height_w, rel_width_w)
    keys_ahead, keys_back = key_tables()
    live = live_rows(slot_table)
    current = spread(windows)
    grad = spread(cotangent)
    kept = []
    for layer in range(LAYERS):
        top = layer == LAYERS - 1
        mid, h1, q, k, v, p, att, token = attend_forward(
            current, live, vec[layer], ahead[layer], keys_ahead, held.source(layer, "attend"),
            held.before(f"attend_{layer}"),
        )
        held.passed(f"attend_{layer}", token)
        used = ("fc1",) if top else ("fc1", "fc2")
        made = mlp_forward(
            plan, top, mid, live, vec[layer], hidden_bias[layer], grad,
            held.source(layer, *used), held.before(f"mlp_{layer}"),
        )
        if top:
            h2, act, slope, top_sums = made[:4]
            pending.add("fc2_1", made[4:])
        else:
            following, h2, act, slope, token = made
            held.passed(f"mlp_{layer}", token)
        kept.append((current, mid, h1, q, k, v, p, att, h2, act, slope))
        current = following
    sums = [None] * LAYERS
    steps = {
        "hidden_1": (),
        "middle_1": ("fc2_1",),
        "scores_1": ("fc2_1", "fc1_1"),
        "weights_1": ("fc2_1", "fc1_1"),
        "first_1": ("fc1_1",),
        "hidden_0": ("attend_1",),
        "middle_0": ("attend_1",),
        "scores_0": ("attend_1", "fc2_0", "fc1_0"),
        "weights_0": ("fc2_0", "fc1_0"),
        "first_0": ("fc2_0", "fc1_0"),
    }
    for layer in reversed(range(LAYERS)):
        top = layer == LAYERS - 1
        x, mid, h1, q, k, v, p, att, h2, act, slope = kept[layer]
        made = hidden_backward(
            plan, top, grad, live, h2, act, slope, held.source(layer, "fc2"),
            pending.advance(*steps[f"hidden_{layer}"]),
        )
        dh, sums3, hsum = made[:3]
        pending.add(f"fc1_{layer}", made[3 : 3 + plan.sinks])
        if top:
            sums3 = top_sums
        else:
            pending.add("fc2_0", made[3 + plan.sinks :])
        dmid, sums2 = middle_backward(
            grad, mid, vec[layer], dh, held.source(layer, "fc1"),
            pending.advance(*steps[f"middle_{layer}"]),
        )
        db, dq, dk, dv, sums1, rel = scores_backward(
            dmid, live, back[layer], keys_back, q, k, v, p, held.source(layer, "attend"),
            pending.advance(*steps[f"scores_{layer}"]),
        )
        pair = first_weights(
            plan, ring and layer == 0, h1, att, db, dq, dk, dv,
            pending.advance(*steps[f"weights_{layer}"]),
        )
        if top:
            pending.add("attend_1", pair)
        grad, sums4 = first_backward(
            dmid, x, live, vec[layer], dq, dk, dv, held.source(layer, "attend"),
            pending.advance(*steps[f"first_{layer}"]),
        )
        if not top:
            pending.sum_top()
        rel = rel[:, :HD] + rel[:, HD:]
        sums[layer] = (
            jnp.concatenate([sums1[1], sums1[2]]), sums1[0], sums4[3], sums4[4], sums2[1],
            sums2[2], hsum[0], sums3[0], rel[:RELS].reshape(-1), rel[HD : HD + RELS].reshape(-1),
        )
    output = gather_back(
        mlp_output(
            kept[-1][9], vec[-1], kept[-1][1], live, held.source(LAYERS - 1, "fc2"), (grad,)
        )
    ).astype(BF16)
    input_grad = gather_back(grad).astype(BF16)
    shards = lax.axis_size("fsdp")
    packed = jnp.concatenate(
        [
            jnp.stack([sums[layer][i] for layer in range(LAYERS)]).reshape(LAYERS, shards, -1)
            for i in range(len(parts))
        ],
        2,
    )
    big, mine = pending.finish(pair, packed)
    qv, pb, n1g, n1b, n2g, n2b, f1b, f2b, rh, rw = [
        mine[:, a:b] for a, b in zip(cuts, cuts[1:])
    ]
    stacked = [jnp.stack([big[layer][i] for layer in range(LAYERS)]) for i in range(4)]
    return (
        output, input_grad, stacked[0], qv, stacked[1], pb, n1g, n1b, n2g, n2b, stacked[2], f1b,
        stacked[3], f2b, rh, rw,
    )


def solution(mesh):
    rows = P(("rep", "fsdp"), None)
    cube = P(None, "fsdp", None)
    flat = P(None, "fsdp")
    ring = mesh.shape["rep"] == 4 and mesh.shape["fsdp"] == 8
    return jax.shard_map(
        functools.partial(on_device, ring),
        mesh=mesh,
        in_specs=(
            rows, P(("rep", "fsdp")), rows, cube, flat, cube, flat, flat, flat, flat, flat, cube,
            flat, cube, flat, flat, flat,
        ),
        out_specs=(
            rows, rows, cube, flat, cube, flat, flat, flat, flat, flat, cube, flat, cube, flat,
            flat, flat,
        ),
        check_vma=False,
    )
```

time: 872 us -> 616 us (0.71); the launches traced: 870 us -> 605 us
  waiting for transfers between devices: 590 us -> 163 us
  other arithmetic: 10.5 us -> 82.3 us
  starting transfers between devices: 0.59 us -> 56.9 us
  blocking collectives: 50.3 us -> 0 us
  Pallas kernels: 181 us -> 227 us
  local copies, waits for them, and re-layouts: 23.3 us -> 58.4 us
    reduce_scatter x6 -> x2, waiting for transfers between devices: 271 us -> 0.02 us  [sum_levels(): lax.psum_scatter(joined.reshape(-1, width), 'fsdp', scatter_dimension=0,...]
    all_gather x8 -> x5, waiting for transfers between devices: 258 us -> 10.3 us  [the longest x2 10.3 us: sum_levels(): lax.all_gather(mine, 'rep', axis=0, tiled=True)]
    ppermute x0 -> x66, waiting for transfers between devices: none -> 152 us  [permute(): lax.ppermute(value, axis, [(i, move(i)) for i in range({'rep': 4, 'fsdp':...]
    ppermute x0 -> x66, starting transfers between devices: none -> 56.6 us  [permute(): lax.ppermute(value, axis, [(i, move(i)) for i in range({'rep': 4, 'fsdp':...]
    psum x1 -> x0, waiting for transfers between devices: 55.5 us -> none  [reduce(): lax.psum(lax.psum_scatter(value, 'fsdp', scatter_dimension=axis, tiled=Tr...]
    pallas_call x8 -> x15, Pallas kernels: 181 us -> 227 us  [call(): pl.pallas_call(body, out_shape=tuple(outs), in_specs=[VM] * len(resident)...]
    another operation x17 -> x41, other arithmetic: 0.5 us -> 35.8 us
    unnamed x1 -> x0, blocking collectives: 26.1 us -> none
  transfers between devices with their start and end apart: 15 -> 73, of which waited for: 13 -> 29; matrix products, arithmetic and copies ran while one was open for 2% -> 20% of each run, Pallas kernels for 13% -> 33%
where the time goes in v2:
time: 616 us; the launch traced here: 605 us
  Pallas kernels  227 us (37%)
  waiting for transfers between devices  163 us (26%)
  other arithmetic  82.3 us (13%)
  local copies, waits for them, and re-layouts  58.4 us (9%)
  starting transfers between devices  56.9 us (9%)
  between operations  17.4 us (3%)
    pallas_call x15, Pallas kernels, call(): pl.pallas_call(body, out_shape=tuple(outs), in_specs=[VM] * len(resident)...  227 us
    ppermute x66, waiting for transfers between devices, permute(): lax.ppermute(value, axis, [(i, move(i)) for i in range({'rep': 4, 'fsdp':...  152 us
    ppermute x66, starting transfers between devices, permute(): lax.ppermute(value, axis, [(i, move(i)) for i in range({'rep': 4, 'fsdp':...  56.6 us
    another operation x16, other arithmetic  21.8 us
  transfers between devices with their start and end apart: 73, of which 29 were waited for; matrix products, arithmetic and copies ran while one was open for 20% of the time, Pallas kernels for 33%

profile of v2, /device:TPU:8, one launch (start us, length us, event | category | flops | bytes accessed | tf_op | source)
XLA Modules:
  0.0 604.7 jit_solution(7846027983041730652)
XLA Ops:
  18.8 13.7 %collective-permute-done.1 = bf16[1,1,104,768]{3,2,0,1:T(8,128)(2,1)S(1)} collective-permute-done((bf16[1,1,104,768]{3,2,0,1:T(8,128)(2,1)S(1)}, bf16[1,1,104,768]{3,2,0,1:T(8,128)(2,1)S(1)}, u32[]{:S(2)}, u32[]{:S(2)}) %collective-permute-start.1) | collective-permute-done | bytes 159776 | tf_op jit(solution)/shard_map/ppermute | solution.py:809
  32.5 11.3 %collective-permute-done = bf16[1,1,104,768]{3,2,0,1:T(8,128)(2,1)S(1)} collective-permute-done((bf16[1,1,104,768]{3,2,0,1:T(8,128)(2,1)S(1)}, bf16[1,1,104,768]{3,2,0,1:T(8,128)(2,1)S(1)}, u32[]{:S(2)}, u32[]{:S(2)}) %collective-permute-start) | collective-permute-done | bytes 159776 | tf_op jit(solution)/shard_map/ppermute | solution.py:809
  81.9 20.0 %shard_map.306 = (f32[448,768]{1,0:T(8,128)}, bf16[448,768]{1,0:T(8,128)(2,1)}, bf16[448,768]{1,0:T(8,128)(2,1)}, bf16[448,768]{1,0:T(8,128)(2,1)}, bf16[448,768...) custom-call(bf16[448,768]{1,0:T(8,128)(2,1)} %bitcast.345, ...), custom_call_target="tpu_custom_call" | custom-call | flops 20000000000 | bytes 1048576 | tf_op jit(solution)/shard_map/pallas_call | solution.py:609
  113.5 20.7 %collective-permute-done.22.refs_7_.refs_6_.refs_10_.refs_9_ = bf16[4,2,96,768]{3,2,1,0:T(8,128)(2,1)S(1)} collective-permute-done((bf16[4,2,96,768]{3,2,1,0:T(8,128)(2,1)S(1)}, bf16[4,2,96,768]{3,2,1,0:T(8,128)(2,1)S(1)}, u32[]{:S(2)}, u32[]{:S(2)}) %collective-permute-start.22) | collective-permute-done | bytes 1179680 | tf_op jit(solution)/shard_map/ppermute | solution.py:809
  134.2 12.7 %collective-permute-done.14.refs_7_.refs_8_ = bf16[2,2,96,768]{3,2,1,0:T(8,128)(2,1)} collective-permute-done((bf16[2,2,96,768]{3,2,1,0:T(8,128)(2,1)S(1)}, bf16[2,2,96,768]{3,2,1,0:T(8,128)(2,1)}, u32[]{:S(2)}, u32[]{:S(2)}) %collective-permute-start.14) | collective-permute-done | bytes 589856 | tf_op jit(solution)/shard_map/ppermute | solution.py:809
  150.2 16.3 %shard_map.307 = (f32[448,768]{1,0:T(8,128)}, bf16[448,768]{1,0:T(8,128)(2,1)}, bf16[448,3072]{1,0:T(8,128)(2,1)}, bf16[448,3072]{1,0:T(8,128)(2,1)}, f32[8,128]{1,0:T(8,128)}) custom-call(f32[448,768]{1,0:T(8,128)} %get-tuple-element.77.refs_0_.refs_1_, f32[448,1]{1,0:T(8,128)} %reshape.665.refs_1_.refs_2_.refs_3_, ...), custom_call_target="tpu_custom_call" | custom-call | flops 16000000000 | bytes 1048576 | tf_op jit(solution)/shard_map/pallas_call | solution.py:609
  173.2 11.1 %collective-permute-done.23.refs_8_.refs_7_.refs_11_.refs_10_ = bf16[2,2,96,768]{3,2,1,0:T(8,128)(2,1)S(1)} collective-permute-done((bf16[2,2,96,768]{3,2,1,0:T(8,128)(2,1)S(1)}, bf16[2,2,96,768]{3,2,1,0:T(8,128)(2,1)S(1)}, u32[]{:S(2)}, u32[]{:S(2)}) %collective-permute-start.23) | collective-permute-done | bytes 589856 | tf_op jit(solution)/shard_map/ppermute | solution.py:809
  189.5 20.3 %shard_map.308 = (f32[448,768]{1,0:T(8,128)}, bf16[448,768]{1,0:T(8,128)(2,1)}, bf16[448,768]{1,0:T(8,128)(2,1)}, bf16[448,768]{1,0:T(8,128)(2,1)}, bf16[448,768...) custom-call(f32[448,768]{1,0:T(8,128)} %get-tuple-element.79.refs_0_.refs_1_, ...), custom_call_target="tpu_custom_call" | custom-call | flops 20000000000 | bytes 1048576 | tf_op jit(solution)/shard_map/pallas_call | solution.py:609
  209.8 19.7 %shard_map.309 = (bf16[448,768]{1,0:T(8,128)(2,1)}, bf16[448,3072]{1,0:T(8,128)(2,1)}, bf16[448,3072]{1,0:T(8,128)(2,1)}, f32[8,768]{1,0:T(8,128)}, bf16[4,4,96,...) custom-call(f32[448,768]{1,0:T(8,128)} %get-tuple-element.81.refs_0_.refs_1_.refs_2_, ...), custom_call_target="tpu_custom_call" | custom-call | flops 16000000000 | bytes 1048576 | tf_op jit(solution)/shard_map/pallas_call | solution.py:609
  236.8 19.9 %shard_map.310 = (bf16[448,3072]{1,0:T(8,128)(2,1)}, f32[8,768]{1,0:T(8,128)}, f32[1,3072]{1,0:T(1,128)}, bf16[4,4,96,768]{3,2,1,0:T(8,128)(2,1)}, bf16[4,4,96,768]{3,2,1,0:T(8,128)(2,1)}) custom-call(bf16[448,768]{1,0:T(8,128)(2,1)} %bitcast.348, f32[448,1]{1,0:T(8,128)} %reshape.665.refs_1_.refs_2_.refs_3_, bf16[448,768]{1,0:T(8,128)(2,1)} %get-tuple-element.83.refs_2_, ...), custom_call_target="tpu_custom_call" | custom-call | flops 15000000512 | bytes 1048576 | tf_op jit(solution)/shard_map/pallas_call | solution.py:609
  266.8 6.8 %collective-permute-done.32 = bf16[2,2,96,768]{3,2,1,0:T(8,128)(2,1)S(1)} collective-permute-done((bf16[2,2,96,768]{3,2,1,0:T(8,128)(2,1)}, bf16[2,2,96,768]{3,2,1,0:T(8,128)(2,1)S(1)}, u32[]{:S(2)}, u32[]{:S(2)}) %collective-permute-start.32) | collective-permute-done | bytes 589856 | tf_op jit(solution)/shard_map/ppermute | solution.py:809
  279.3 11.0 %shard_map.311 = (f32[448,768]{1,0:T(8,128)}, f32[8,768]{1,0:T(8,128)}) custom-call(bf16[448,768]{1,0:T(8,128)(2,1)} %bitcast.349, f32[448,768]{1,0:T(8,128)} %get-tuple-element.81.refs_0_.refs_1_.refs_2_, f32[8,768]{1,0:T(8,128)} %get-tuple-element.257.refs_2_.refs_3_.refs_1_, bf16[448,3072]{1,0:T(8,128)(2,1)} %get-tuple-element.85.refs_3_, ...), custom_call_target="tpu_custom_call" | custom-call | flops 10000000000 | bytes 1048576 | tf_op jit(solution)/shard_map/pallas_call | solution.py:609
  296.3 18.1 %shard_map.312 = (bf16[448,768]{1,0:T(8,128)(2,1)}, bf16[448,768]{1,0:T(8,128)(2,1)}, bf16[448,768]{1,0:T(8,128)(2,1)}, bf16[448,768]{1,0:T(8,128)(2,1)}, f32[8,768]{1,0:T(8,128)}, /*index=5*/f32[128,128]{1,0:T(8,128)}) custom-call(f32[448,768]{1,0:T(8,128)} %get-tuple-element.88.refs_0_, f32[448,1]{1,0:T(8,128)} %reshape.665.refs_1_.refs_2_.refs_3_, ...), custom_call_target="tpu_custom_call" | custom-call | flops 15000000512 | bytes 1048576 | tf_op jit(solution)/shard_map/pallas_call | solution.py:609
  316.9 10.1 %shard_map.314 = (bf16[4,4,96,768]{3,2,1,0:T(8,128)(2,1)}, bf16[4,4,96,768]{3,2,1,0:T(8,128)(2,1)}) custom-call(bf16[448,768]{1,0:T(8,128)(2,1)} %get-tuple-element.102.refs_0_, bf16[448,768]{1,0:T(8,128)(2,1)} %get-tuple-element.103.refs_1_, bf16[448,768]{1,0:T(8,128)(2,1)} %get-tuple-element.104.refs_2_, ...), custom_call_target="tpu_custom_call" | custom-call | flops 8000000000 | bytes 1048576 | tf_op jit(solution)/shard_map/pallas_call | solution.py:609
  345.7 10.6 %shard_map.313 = (f32[448,768]{1,0:T(8,128)}, f32[8,768]{1,0:T(8,128)}) custom-call(f32[448,768]{1,0:T(8,128)} %get-tuple-element.88.refs_0_, f32[448,768]{1,0:T(8,128)} %get-tuple-element.79.refs_0_.refs_1_, f32[448,1]{1,0:T(8,128)} %reshape.665.refs_1_.refs_2_.refs_3_, f32[8,768]{1,0:T(8,128)} %get-tuple-element.257.refs_2_.refs_3_.refs_1_, ...), custom_call_target="tpu_custom_call" | custom-call | flops 8000000000 | bytes 1048576 | tf_op jit(solution)/shard_map/pallas_call | solution.py:609
  363.4 22.9 %shard_map.315 = (bf16[448,3072]{1,0:T(8,128)(2,1)}, f32[8,768]{1,0:T(8,128)}, f32[1,3072]{1,0:T(1,128)}, bf16[4,4,96,768]{3,2,1,0:T(8,128)(2,1)}, bf16[4,4,96,7...) custom-call(f32[448,768]{1,0:T(8,128)} %get-tuple-element.98.refs_0_, ...), custom_call_target="tpu_custom_call" | custom-call | flops 15000000512 | bytes 1048576 | tf_op jit(solution)/shard_map/pallas_call | solution.py:609
  392.4 11.2 %shard_map.316 = (f32[448,768]{1,0:T(8,128)}, f32[8,768]{1,0:T(8,128)}) custom-call(f32[448,768]{1,0:T(8,128)} %get-tuple-element.98.refs_0_, f32[448,768]{1,0:T(8,128)} %get-tuple-element.77.refs_0_.refs_1_, f32[8,768]{1,0:T(8,128)} %get-tuple-element.258.refs_2_.refs_3_, bf16[448,3072]{1,0:T(8,128)(2,1)} %get-tuple-element.107.refs_3_, ...), custom_call_target="tpu_custom_call" | custom-call | flops 10000000000 | bytes 1048576 | tf_op jit(solution)/shard_map/pallas_call | solution.py:609
  419.5 18.1 %shard_map.317 = (bf16[448,768]{1,0:T(8,128)(2,1)}, bf16[448,768]{1,0:T(8,128)(2,1)}, bf16[448,768]{1,0:T(8,128)(2,1)}, bf16[448,768]{1,0:T(8,128)(2,1)}, f32[8,768]{1,0:T(8,128)}, /*index=5*/f32[128,128]{1,0:T(8,128)}) custom-call(f32[448,768]{1,0:T(8,128)} %get-tuple-element.108.refs_0_, f32[448,1]{1,0:T(8,128)} %reshape.665.refs_1_.refs_2_.refs_3_, ...), custom_call_target="tpu_custom_call" | custom-call | flops 15000000512 | bytes 1048576 | tf_op jit(solution)/shard_map/pallas_call | solution.py:609
  463.0 9.7 %shard_map.320 = (bf16[4,4,96,768]{3,2,1,0:T(8,128)(2,1)}, bf16[4,4,96,768]{3,2,1,0:T(8,128)(2,1)}) custom-call(bf16[448,768]{1,0:T(8,128)(2,1)} %get-tuple-element.121.refs_0_, bf16[448,768]{1,0:T(8,128)(2,1)} %get-tuple-element.122.refs_1_, bf16[448,768]{1,0:T(8,128)(2,1)} %get-tuple-element.123.refs_2_, ...), custom_call_target="tpu_custom_call" | custom-call | flops 8000000000 | bytes 1048576 | tf_op jit(solution)/shard_map/pallas_call | solution.py:609
  477.6 10.5 %shard_map.318 = (f32[448,768]{1,0:T(8,128)}, f32[8,768]{1,0:T(8,128)}) custom-call(f32[448,768]{1,0:T(8,128)} %get-tuple-element.108.refs_0_, bf16[448,768]{1,0:T(8,128)(2,1)} %bitcast.346, f32[448,1]{1,0:T(8,128)} %reshape.665.refs_1_.refs_2_.refs_3_, f32[8,768]{1,0:T(8,128)} %get-tuple-element.258.refs_2_.refs_3_, ...), custom_call_target="tpu_custom_call" | custom-call | flops 8000000000 | bytes 1048576 | tf_op jit(solution)/shard_map/pallas_call | solution.py:609
  508.7 18.5 %collective-permute-done.59 = bf16[2,2,104,768]{3,2,1,0:T(8,128)(2,1)S(1)} collective-permute-done((bf16[2,2,104,768]{3,2,1,0:T(8,128)(2,1)S(1)}, bf16[2,2,104,768]{3,2,1,0:T(8,128)(2,1)S(1)}, u32[]{:S(2)}, u32[]{:S(2)}) %collective-permute-start.59) | collective-permute-done | bytes 639008 | tf_op jit(solution)/shard_map/ppermute | solution.py:809
  532.0 13.9 %collective-permute-done.57 = bf16[2,104,768]{2,1,0:T(8,128)(2,1)S(1)} collective-permute-done((bf16[2,104,768]{2,1,0:T(8,128)(2,1)S(1)}, bf16[2,104,768]{2,1,0:T(8,128)(2,1)S(1)}, u32[]{:S(2)}, u32[]{:S(2)}) %collective-permute-start.57) | collective-permute-done | bytes 319520 | tf_op jit(solution)/shard_map/ppermute | solution.py:809
  551.9 8.6 %shard_map.319 = f32[448,768]{1,0:T(8,128)} custom-call(bf16[448,3072]{1,0:T(8,128)(2,1)} %get-tuple-element.82.refs_3_.refs_0_, f32[8,768]{1,0:T(8,128)} %get-tuple-element.257.refs_2_.refs_3_.refs_1_, f32[448,768]{1,0:T(8,128)} %get-tuple-element.81.refs_0_.refs_1_.refs_2_, f32[448,1]{1,0:T(8,128)} %reshape.665.refs_1_.refs_2_.refs_3_, ...), custom_call_target="tpu_custom_call" | custom-call | flops 5000000000 | bytes 1048576 | tf_op jit(solution)/shard_map/pallas_call | solution.py:609
  581.1 10.3 %all-gather.13.cloned.1.call-done = bf16[768,768]{1,0:T(8,128)(2,1)} async-done(((bf16[192,768]{1,0:T(8,128)(2,1)}), bf16[768,768]{1,0:T(8,128)(2,1)}) %all-gather.13.cloned.1.call-update) | async-done | bytes 1179664 | tf_op jit(solution)/shard_map/all_gather | solution.py:999
  (526 shorter events, 241.2 us)
Async XLA Ops:
  8.0 71.8 %all-gather.7.cloned.1.call-start = ((), (), s32[]{:S(2)}) async-start(), calls=%async_computation.2 | async-start | bytes 1474560 | tf_op jit(solution)/shard_map/all_gather | solution.py:909
  11.4 91.7 %all-gather.9.cloned.1.call-start = ((), (), s32[]{:S(2)}) async-start(), calls=%async_computation.3 | async-start | bytes 1474560 | tf_op jit(solution)/shard_map/all_gather | solution.py:909
  15.2 28.6 %collective-permute-start = (bf16[1,1,104,768]{3,2,0,1:T(8,128)(2,1)S(1)}, bf16[1,1,104,768]{3,2,0,1:T(8,128)(2,1)S(1)}, u32[]{:S(2)}, u32[]{:S(2)}) collective-permute-start(bf16[1,1,104,768]{3,2,0,1:T(8,128)(2,1)S(1)} %maximum_bitcast_fusion.4), channel_id=1, source_target_pairs={{0,2},{1,3},{2,4},{3,5},{4,6},{5,7},{6,0},{7,1},{8,10},{9,11},{10,... | collective-permute-start | bytes 479240 | tf_op jit(solution)/shard_map/ppermute | solution.py:809
  18.6 218.2 %all-gather.15.cloned.1.call-start = ((), (), s32[]{:S(2)}) async-start(), calls=%async_computation.8 | async-start | bytes 5308416 | tf_op jit(solution)/shard_map/all_gather | solution.py:890
  79.8 33.7 %collective-permute-start.16 = (bf16[4,2,96,768]{3,2,1,0:T(8,128)(2,1)}, bf16[4,2,96,768]{3,2,1,0:T(8,128)(2,1)}, u32[]{:S(2)}, u32[]{:S(2)}) collective-permute-start(bf16[4,2,96,768]{3,2,1,0:T(8,128)(2,1)} %bitcast.371), channel_id=1, source_target_pairs={{0,1},{1,0},{2,3},{3,2},{4,5},{5,4},{6,7},{7,6},{8,9},{9,8},{10,11... | collective-permute-start | bytes 3538952 | tf_op jit(solution)/shard_map/ppermute | solution.py:809
  79.9 29.0 %collective-permute-start.13 = (bf16[4,2,96,768]{3,2,1,0:T(8,128)(2,1)}, bf16[4,2,96,768]{3,2,1,0:T(8,128)(2,1)S(1)}, u32[]{:S(2)}, u32[]{:S(2)}) collective-permute-start(bf16[4,2,96,768]{3,2,1,0:T(8,128)(2,1)} %bitcast.372), channel_id=1, source_target_pairs={{0,16},{8,24},{16,0},{24,8},{1,17},{9,25},{17,1},{25,9},{2,18},{10... | collective-permute-start | bytes 3538952 | tf_op jit(solution)/shard_map/ppermute | solution.py:809
  80.4 30.8 %collective-permute-start.12 = (bf16[4,2,96,768]{3,2,1,0:T(8,128)(2,1)}, bf16[4,2,96,768]{3,2,1,0:T(8,128)(2,1)}, u32[]{:S(2)}, u32[]{:S(2)}) collective-permute-start(bf16[4,2,96,768]{3,2,1,0:T(8,128)(2,1)} %bitcast.373), channel_id=1, source_target_pairs={{0,8},{8,0},{16,24},{24,16},{1,9},{9,1},{17,25},{25,17},{2,10},{10... | collective-permute-start | bytes 3538952 | tf_op jit(solution)/shard_map/ppermute | solution.py:809
  105.2 29.1 %collective-permute-start.22 = (bf16[4,2,96,768]{3,2,1,0:T(8,128)(2,1)S(1)}, bf16[4,2,96,768]{3,2,1,0:T(8,128)(2,1)S(1)}, u32[]{:S(2)}, u32[]{:S(2)}) collective-permute-start(bf16[4,2,96,768]{3,2,1,0:T(8,128)(2,1)S(1)} %bitcast.335), channel_id=1, source_target_pairs={{0,16},{8,24},{16,0},{24,8},{1,17},{9,25},{17,1},{25,9},{2,18},{10... | collective-permute-start | bytes 3538952 | tf_op jit(solution)/shard_map/ppermute | solution.py:809
  106.7 41.4 %collective-permute-start.21 = (bf16[4,2,96,768]{3,2,1,0:T(8,128)(2,1)S(1)}, bf16[4,2,96,768]{3,2,1,0:T(8,128)(2,1)}, u32[]{:S(2)}, u32[]{:S(2)}) collective-permute-start(bf16[4,2,96,768]{3,2,1,0:T(8,128)(2,1)S(1)} %bitcast.336), channel_id=1, source_target_pairs={{0,8},{8,0},{16,24},{24,16},{1,9},{9,1},{17,25},{25,17},{2,10},{10... | collective-permute-start | bytes 3538952 | tf_op jit(solution)/shard_map/ppermute | solution.py:809
  109.6 37.3 %collective-permute-start.14 = (bf16[2,2,96,768]{3,2,1,0:T(8,128)(2,1)S(1)}, bf16[2,2,96,768]{3,2,1,0:T(8,128)(2,1)}, u32[]{:S(2)}, u32[]{:S(2)}) collective-permute-start(bf16[2,2,96,768]{3,2,1,0:T(8,128)(2,1)S(1)} %slice_add_fusion.3), channel_id=1, source_target_pairs={{0,8},{8,0},{16,24},{24,16},{1,9},{9,1},{17,25},{25,17},{2,10},{10... | collective-permute-start | bytes 1769480 | tf_op jit(solution)/shard_map/ppermute | solution.py:809
  112.9 34.0 %collective-permute-start.15 = (bf16[2,2,96,768]{3,2,1,0:T(8,128)(2,1)S(1)}, bf16[2,2,96,768]{3,2,1,0:T(8,128)(2,1)}, u32[]{:S(2)}, u32[]{:S(2)}) collective-permute-start(bf16[2,2,96,768]{3,2,1,0:T(8,128)(2,1)S(1)} %slice_add_fusion.2), channel_id=1, source_target_pairs={{0,16},{8,24},{16,0},{24,8},{1,17},{9,25},{17,1},{25,9},{2,18},{10... | collective-permute-start | bytes 1769480 | tf_op jit(solution)/shard_map/ppermute | solution.py:809
  113.5 36.7 %collective-permute-start.18 = (bf16[4,2,96,768]{3,2,1,0:T(8,128)(2,1)S(1)}, bf16[4,2,96,768]{3,2,1,0:T(8,128)(2,1)}, u32[]{:S(2)}, u32[]{:S(2)}) collective-permute-start(bf16[4,2,96,768]{3,2,1,0:T(8,128)(2,1)S(1)} %collective-permute-done.13.refs_6_.refs_7_), channel_id=1, source_target_pairs={{0,1},{1,0},{2,3},{3,2},{4,5},{5,4},{6,7},{7,6},{8,9},{9,8},{10,11... | collective-permute-start | bytes 3538952 | tf_op jit(solution)/shard_map/ppermute | solution.py:809
  147.4 355.2 %reduce-scatter.3.cloned.1.call-start = ((), (), s32[]{:S(2)}) async-start(), calls=%async_computation.4 | async-start | bytes 2211840 | tf_op jit(solution)/shard_map/reduce_scatter | solution.py:995
  148.2 40.1 %collective-permute-start.25 = (bf16[4,2,96,768]{3,2,1,0:T(8,128)(2,1)S(1)}, bf16[4,2,96,768]{3,2,1,0:T(8,128)(2,1)}, u32[]{:S(2)}, u32[]{:S(2)}) collective-permute-start(bf16[4,2,96,768]{3,2,1,0:T(8,128)(2,1)S(1)} %bitcast.337), channel_id=1, source_target_pairs={{0,1},{1,0},{2,3},{3,2},{4,5},{5,4},{6,7},{7,6},{8,9},{9,8},{10,11... | collective-permute-start | bytes 3538952 | tf_op jit(solution)/shard_map/ppermute | solution.py:809
  149.2 39.0 %collective-permute-start.27 = (bf16[4,2,96,768]{3,2,1,0:T(8,128)(2,1)}, bf16[4,2,96,768]{3,2,1,0:T(8,128)(2,1)}, u32[]{:S(2)}, u32[]{:S(2)}) collective-permute-start(bf16[4,2,96,768]{3,2,1,0:T(8,128)(2,1)} %copy-done.31), channel_id=1, source_target_pairs={{0,1},{1,0},{2,3},{3,2},{4,5},{5,4},{6,7},{7,6},{8,9},{9,8},{10,11... | collective-permute-start | bytes 3538952 | tf_op jit(solution)/shard_map/ppermute | solution.py:809
  150.1 38.2 %collective-permute-start.26 = (bf16[4,2,96,768]{3,2,1,0:T(8,128)(2,1)}, bf16[4,2,96,768]{3,2,1,0:T(8,128)(2,1)}, u32[]{:S(2)}, u32[]{:S(2)}) collective-permute-start(bf16[4,2,96,768]{3,2,1,0:T(8,128)(2,1)} %collective-permute-done.21.refs_6_.refs_5_.refs_9_.refs_8_), channel_id=1, source_target_pairs={{0,1},{1,0},{2,3},{3,2},{4,5},{5,4},{6,7},{7,6},{8,9},{9,8},{10,11... | collective-permute-start | bytes 3538952 | tf_op jit(solution)/shard_map/ppermute | solution.py:809
  256.7 36.4 %collective-permute-start.33 = (bf16[4,4,96,768]{3,2,1,0:T(8,128)(2,1)}, bf16[4,4,96,768]{3,2,1,0:T(8,128)(2,1)}, u32[]{:S(2)}, u32[]{:S(2)}) collective-permute-start(bf16[4,4,96,768]{3,2,1,0:T(8,128)(2,1)} %get-tuple-element.94), channel_id=1, source_target_pairs={{0,1},{1,0},{2,3},{3,2},{4,5},{5,4},{6,7},{7,6},{8,9},{9,8},{10,11... | collective-permute-start | bytes 7077896 | tf_op jit(solution)/shard_map/ppermute | solution.py:809
  327.0 30.7 %collective-permute-start.40 = (bf16[4,4,96,768]{3,2,1,0:T(8,128)(2,1)}, bf16[4,4,96,768]{3,2,1,0:T(8,128)(2,1)}, u32[]{:S(2)}, u32[]{:S(2)}) collective-permute-start(bf16[4,4,96,768]{3,2,1,0:T(8,128)(2,1)} %get-tuple-element.106), channel_id=1, source_target_pairs={{0,1},{1,0},{2,3},{3,2},{4,5},{5,4},{6,7},{7,6},{8,9},{9,8},{10,11... | collective-permute-start | bytes 7077896 | tf_op jit(solution)/shard_map/ppermute | solution.py:809
  387.2 28.8 %collective-permute-start.46 = (bf16[4,4,96,768]{3,2,1,0:T(8,128)(2,1)}, bf16[4,4,96,768]{3,2,1,0:T(8,128)(2,1)}, u32[]{:S(2)}, u32[]{:S(2)}) collective-permute-start(bf16[4,4,96,768]{3,2,1,0:T(8,128)(2,1)} %get-tuple-element.116), channel_id=1, source_target_pairs={{0,1},{1,0},{2,3},{3,2},{4,5},{5,4},{6,7},{7,6},{8,9},{9,8},{10,11... | collective-permute-start | bytes 7077896 | tf_op jit(solution)/shard_map/ppermute | solution.py:809
  409.1 154.9 %reduce-scatter.5.cloned.1.call-start = ((), (), s32[]{:S(2)}) async-start(), calls=%async_computation.6 | async-start | bytes 1474560 | tf_op jit(solution)/shard_map/reduce_scatter | solution.py:995
  412.8 42.9 %collective-permute-start.47 = (bf16[2,2,96,768]{3,2,1,0:T(8,128)(2,1)}, bf16[2,2,96,768]{3,2,1,0:T(8,128)(2,1)S(1)}, u32[]{:S(2)}, u32[]{:S(2)}) collective-permute-start(bf16[2,2,96,768]{3,2,1,0:T(8,128)(2,1)} %pad_maximum_fusion.20.refs_19_), channel_id=1, source_target_pairs={{0,8},{8,0},{16,24},{24,16},{1,9},{9,1},{17,25},{25,17},{2,10},{10... | collective-permute-start | bytes 1769480 | tf_op jit(solution)/shard_map/ppermute | solution.py:809
  415.1 40.5 %collective-permute-start.49 = (bf16[2,2,96,768]{3,2,1,0:T(8,128)(2,1)}, bf16[2,2,96,768]{3,2,1,0:T(8,128)(2,1)S(1)}, u32[]{:S(2)}, u32[]{:S(2)}) collective-permute-start(bf16[2,2,96,768]{3,2,1,0:T(8,128)(2,1)} %pad_maximum_fusion.21.refs_20_), channel_id=1, source_target_pairs={{0,16},{8,24},{16,0},{24,8},{1,17},{9,25},{17,1},{25,9},{2,18},{10... | collective-permute-start | bytes 1769480 | tf_op jit(solution)/shard_map/ppermute | solution.py:809
  500.5 67.2 %all-gather.11.cloned.1.call-start = ((), (), s32[]{:S(2)}) async-start(), calls=%async_computation.5 | async-start | bytes 2211840 | tf_op jit(solution)/shard_map/all_gather | solution.py:999
  502.7 88.8 %all-gather.13.cloned.1.call-start = ((), (), s32[]{:S(2)}) async-start(), calls=%async_computation.7 | async-start | bytes 1474560 | tf_op jit(solution)/shard_map/all_gather | solution.py:999
  (113 other events, 1219.2 us)
Sparse Core Ops, SparseCore 0:
  11.6 36.1 all-gather.6
  49.9 32.1 all-gather.8
  409.2 38.8 reduce-scatter.2
  500.6 28.7 reduce-scatter.4
Sparse Core Ops, SparseCore 1:
  147.5 51.0 all-gather.14
  502.9 44.7 all-gather.10
  564.1 27.3 all-gather.12

commit v3 on v2

v3 whole, which is shorter than its diff:
```python
import functools

import jax
import jax.numpy as jnp
import numpy as np
from jax import lax
from jax.experimental import pallas as pl
from jax.experimental.pallas import tpu as pltpu
from jax.sharding import PartitionSpec as P

HEADS = 12
HD = 64
WINDOW = 14
SIDE = 64
LAYERS = 2
GRID = 5
RELS = 2 * WINDOW - 1
EPSILON = 1e-06
PITCH = 16
SPAN = WINDOW * PITCH
PAIRS = HEADS // 2
LANES = 2 * HD
F32 = jnp.float32
BF16 = jnp.bfloat16
CHUNK = 768
ROWS_STEP = 64
VMEM_LIMIT = 56 * 1024 * 1024
SLAB = 384
RIDERS = 8
LARGE = 256 * 1024


def dot_nn(a, b):
    return lax.dot_general(a, b, (((1,), (0,)), ((), ())), preferred_element_type=F32)


def dot_nt(a, b):
    return lax.dot_general(a, b, (((1,), (1,)), ((), ())), preferred_element_type=F32)


def dot_tn(a, b):
    return lax.dot_general(a, b, (((0,), (0,)), ((), ())), preferred_element_type=F32)


def norm_rows(values):
    centre = jnp.mean(values, -1, keepdims=True)
    centered = values - centre
    inverse = lax.rsqrt(jnp.mean(centered * centered, -1, keepdims=True) + EPSILON)
    return centered * inverse, inverse


def norm_back(grad, normed, inverse, gain):
    scaled = grad * gain
    return inverse * (
        scaled
        - jnp.mean(scaled, -1, keepdims=True)
        - normed * jnp.mean(scaled * normed, -1, keepdims=True)
    )


def each(count, step, body):
    def run(index, carry):
        body(pl.multiple_of(index * step, step))
        return carry

    lax.fori_loop(0, count, run, 0)


def each_index(count, body):
    def run(index, carry):
        body(index)
        return carry

    lax.fori_loop(0, count, run, 0)


def in_fours(count, body):
    def several(index):
        for i in range(4):
            body(4 * index + i)

    each_index(count // 4, several)


def half_lane():
    return lax.broadcasted_iota(jnp.int32, (SPAN, LANES), 1)


def split_heads(pair):
    lane = half_lane()
    zero = jnp.zeros_like(pair)
    return jnp.concatenate(
        [jnp.where(lane < HD, pair, zero), jnp.where(lane < HD, zero, pair)], axis=0
    )


def join_heads(stacked):
    return jnp.where(half_lane() < HD, stacked[:SPAN], stacked[SPAN:])


def shift_rows(table):
    by_row = jnp.concatenate(
        [
            pltpu.roll(table[i * PITCH : (i + 1) * PITCH], i, axis=1) if i else table[:PITCH]
            for i in range(WINDOW)
        ],
        axis=0,
    )
    by_col = pltpu.roll(
        table.reshape(WINDOW, PITCH, LANES), 0, axis=2, stride=1, stride_axis=1
    ).reshape(SPAN, LANES)
    return jnp.where(half_lane() < HD, by_row, by_col)


def key_tables():
    ahead = np.zeros((SPAN, LANES), np.float32)
    back = np.zeros((SPAN, LANES), np.float32)
    for k in range(WINDOW):
        for m in range(PITCH):
            row = k * PITCH + m
            ahead[row, WINDOW - 1 + k] = 1.0
            back[row, WINDOW - 1 - k] = 1.0
            if m < WINDOW:
                ahead[row, HD + WINDOW - 1 + m] = 1.0
                back[row, HD + WINDOW - 1 - m] = 1.0
            else:
                ahead[row, LANES - 1] = -1e30
    return jnp.asarray(ahead, BF16), jnp.asarray(back, BF16)


class Flow:
    def __init__(self, ins, in_sem, outs, out_sem):
        self.ins = {}
        for i, (given, taken) in enumerate(ins):
            copy = pltpu.make_async_copy(given, taken, in_sem.at[i])
            copy.start()
            self.ins[id(taken)] = copy
        self.outs = {
            id(made): pltpu.make_async_copy(made, given, out_sem.at[i])
            for i, (made, given) in enumerate(outs)
        }
        self.sent = []

    def need(self, *refs):
        for ref in refs:
            copy = self.ins.pop(id(ref), None)
            if copy is not None:
                copy.wait()

    def emit(self, *refs):
        for ref in refs:
            copy = self.outs.pop(id(ref), None)
            if copy is not None:
                copy.start()
                self.sent.append(copy)

    def finish(self):
        for copy in self.ins.values():
            copy.wait()
        for copy in self.outs.values():
            copy.start()
        for copy in (*self.outs.values(), *self.sent):
            copy.wait()


def attend_kernel(source, flow, *refs):
    (x_ref, live_ref, vec_ref, table_ref, keys_ref), refs = refs[:5], refs[5:]
    weight_refs, refs = refs[: source.count], refs[source.count :]
    (mid_ref, h1_ref, q_ref, k_ref, v_ref, p_ref, att_ref), refs = refs[:7], refs[7:]
    token_ref, w_ref, sem = refs
    token_ref[...] = jnp.zeros_like(token_ref)
    ready = source.load("attend", weight_refs, w_ref, sem)
    width = x_ref.shape[1]
    flow.need(x_ref)

    def first_norm(start):
        rows = pl.ds(start, ROWS_STEP)
        normed, _ = norm_rows(x_ref[rows, :].astype(F32))
        shaped = (normed * vec_ref[0:1, :] + vec_ref[1:2, :]) * live_ref[rows, :]
        h1_ref[rows, :] = shaped.astype(BF16)

    each(x_ref.shape[0] // ROWS_STEP, ROWS_STEP, first_norm)
    flow.emit(h1_ref)
    ready()
    for index, (out_ref, bias) in enumerate(((q_ref, 2), (k_ref, None), (v_ref, 3))):

        def project(start, index=index, out_ref=out_ref, bias=bias):
            cols = pl.ds(start, CHUNK)
            made = dot_nn(h1_ref[...], w_ref[index, :, cols])
            if bias is not None:
                made = made + vec_ref[bias : bias + 1, cols]
            out_ref[:, cols] = made.astype(BF16)

        each(width // CHUNK, CHUNK, project)
        flow.emit(out_ref)

    def attend(index):
        rows = pl.ds(pl.multiple_of(index // PAIRS * SPAN, SPAN), SPAN)
        cols = pl.ds(pl.multiple_of(index % PAIRS * LANES, LANES), LANES)
        queries = q_ref[rows, cols]
        offsets = dot_nn(queries, table_ref[...])
        lane = half_lane()
        sides = []
        for half in range(2):
            moved = shift_rows(offsets[:, half * LANES : (half + 1) * LANES])
            sides.append(jnp.where(lane == LANES - 1, 1.0, moved).astype(BF16))
        left = jnp.concatenate(
            [split_heads(queries) * HD ** (-0.5), jnp.concatenate(sides, axis=0)], axis=1
        )
        right = jnp.concatenate([k_ref[rows, cols], keys_ref[...]], axis=1)
        scores = dot_nt(left, right)
        shifted = jnp.exp(scores - jnp.max(scores, -1, keepdims=True))
        probs = shifted * (1.0 / jnp.sum(shifted, -1, keepdims=True))
        low = probs.astype(BF16)
        p_ref[index] = low
        att_ref[rows, cols] = join_heads(dot_nn(low, v_ref[rows, cols])).astype(BF16)

    in_fours(x_ref.shape[0] // SPAN * PAIRS, attend)
    flow.emit(p_ref, att_ref)

    def finish(start):
        cols = pl.ds(start, CHUNK)
        branch = dot_nn(att_ref[...], w_ref[3, :, cols]) + vec_ref[4:5, cols]
        mid_ref[:, cols] = x_ref[:, cols].astype(F32) + live_ref[...] * branch

    each(width // CHUNK, CHUNK, finish)


def mlp_kernel(plan, source, top, flow, *refs):
    (mid_ref, live_ref, vec_ref, bias_ref), refs = refs[:4], refs[4:]
    if top:
        (grad_ref,), refs = refs[:1], refs[1:]
    weight_refs, refs = refs[: source.count], refs[source.count :]
    if top:
        (h2_ref, act_ref, slope_ref, sums_ref), refs = refs[:4], refs[4:]
        sink_refs, refs = refs[: plan.sinks], refs[plan.sinks :]
        (w1_ref, dm_ref, sem), refs = refs[:3], refs[3:]
        sink = plan.sink(sink_refs, refs, False)
    else:
        out_ref, h2_ref, act_ref, slope_ref, w1_ref, w2_ref, sem, sem2 = refs
    ready1 = source.load("fc1", weight_refs, w1_ref, sem)
    if not top:
        ready2 = source.load("fc2", weight_refs, w2_ref, sem2)
    width = mid_ref.shape[1]
    hidden_width = act_ref.shape[1]
    flow.need(mid_ref)

    def second_norm(start):
        rows = pl.ds(start, ROWS_STEP)
        normed, _ = norm_rows(mid_ref[rows, :])
        h2_ref[rows, :] = (normed * vec_ref[5:6, :] + vec_ref[6:7, :]).astype(BF16)

    each(mid_ref.shape[0] // ROWS_STEP, ROWS_STEP, second_norm)
    flow.emit(h2_ref)
    ready1()

    def expand(index):
        start = pl.multiple_of(index * CHUNK, CHUNK)
        cols = pl.ds(start, CHUNK)
        inner = pl.ds(pl.multiple_of(start % width, CHUNK), CHUNK)
        hidden = dot_nn(h2_ref[...], w1_ref[start // width, :, inner]) + bias_ref[:, cols]
        below = 0.5 * (1.0 + lax.erf(hidden * (0.5**0.5)))
        bell = jnp.exp(-0.5 * hidden * hidden) * (0.5 / np.pi) ** 0.5
        act_ref[:, cols] = (hidden * below).astype(BF16)
        slope_ref[:, cols] = (below + hidden * bell).astype(BF16)

    each_index(hidden_width // CHUNK, expand)
    flow.emit(act_ref, slope_ref)
    if top:
        sums_ref[...] = jnp.zeros_like(sums_ref)
        flow.need(grad_ref)
        second_weight(grad_ref, live_ref, act_ref, dm_ref, sums_ref, sink)
        sink.wait()
    else:
        ready2()
        contract(act_ref, w2_ref, vec_ref, mid_ref, live_ref, out_ref)


def contract(act_ref, w2_ref, vec_ref, mid_ref, live_ref, out_ref):
    def run(start):
        cols = pl.ds(start, CHUNK)
        made = dot_nn(act_ref[...], w2_ref[:, cols]) + vec_ref[7:8, cols]
        out_ref[:, cols] = mid_ref[:, cols] + live_ref[...] * made

    each(out_ref.shape[1] // CHUNK, CHUNK, run)


def out_kernel(source, flow, act_ref, vec_ref, mid_ref, live_ref, *refs):
    weight_refs, (out_ref, w2_ref, sem) = refs[: source.count], refs[source.count :]
    source.load("fc2", weight_refs, w2_ref, sem)()
    flow.need(act_ref, mid_ref)
    contract(act_ref, w2_ref, vec_ref, mid_ref, live_ref, out_ref)


def second_weight(grad_ref, live_ref, act_ref, dm_ref, sums_ref, sink):
    dm_ref[...] = (live_ref[...] * grad_ref[...].astype(F32)).astype(BF16)
    sums_ref[7:8, :] = jnp.sum(dm_ref[...].astype(F32), 0, keepdims=True)

    def run(index):
        rows = pl.ds(pl.multiple_of(index * SLAB, SLAB), SLAB)
        sink.rows(index, dot_tn(act_ref[:, rows], dm_ref[...]).astype(BF16))

    each_index(act_ref.shape[1] // SLAB, run)
    sink.send_all()


def hidden_back(flow, ready, sink, h2_ref, slope_ref, dh_ref, hsum_ref, w2_ref, dm_ref):
    width = h2_ref.shape[1]
    hidden_width = slope_ref.shape[1]
    flow.need(slope_ref)
    ready()

    def inner_grad(start):
        cols = pl.ds(start, CHUNK)
        made = (dot_nt(dm_ref[...], w2_ref[cols, :]) * slope_ref[:, cols].astype(F32)).astype(BF16)
        dh_ref[:, cols] = made
        hsum_ref[:, cols] = jnp.sum(made.astype(F32), 0, keepdims=True)

    each(hidden_width // CHUNK, CHUNK, inner_grad)
    flow.emit(dh_ref)
    flow.need(h2_ref)
    for block in range(hidden_width // width):

        def first_weight(start, block=block):
            cols = pl.ds(start, CHUNK)
            outer = pl.ds(pl.multiple_of(block * width + start, CHUNK), CHUNK)
            sink.cols(block, cols, dot_tn(h2_ref[...], dh_ref[:, outer]).astype(BF16))

        each(width // CHUNK, CHUNK, first_weight)
        sink.send(block)


def hidden_back_kernel(plan, source, flow, *refs):
    (grad_ref, act_ref, live_ref, h2_ref, slope_ref), refs = refs[:5], refs[5:]
    weight_refs, refs = refs[: source.count], refs[source.count :]
    (dh_ref, sums_ref, hsum_ref), refs = refs[:3], refs[3:]
    sink_refs, (w2_ref, dm_ref, sem), refs = refs[:2], refs[2:5], refs[5:]
    more, sink = plan.two_sinks(sink_refs, refs, True)
    ready = source.load("fc2", weight_refs, w2_ref, sem)
    sums_ref[...] = jnp.zeros_like(sums_ref)
    flow.need(grad_ref, act_ref)
    second_weight(grad_ref, live_ref, act_ref, dm_ref, sums_ref, more)
    hidden_back(flow, ready, sink, h2_ref, slope_ref, dh_ref, hsum_ref, w2_ref, dm_ref)
    more.wait()
    sink.wait()


def middle_back_kernel(source, flow, *refs):
    (grad_ref, mid_ref, vec_ref, dh_ref), refs = refs[:4], refs[4:]
    weight_refs, refs = refs[: source.count], refs[source.count :]
    dmid_ref, sums_ref, w1_ref, ds_ref, sem = refs
    ready = source.load("fc1", weight_refs, w1_ref, sem)
    flow.need(dh_ref)
    sums_ref[...] = jnp.zeros_like(sums_ref)
    middle_back(
        flow, ready, grad_ref, mid_ref, vec_ref, dh_ref, dmid_ref, sums_ref, w1_ref, ds_ref
    )


def middle_back(
    flow, ready, grad_ref, mid_ref, vec_ref, dh_ref, dmid_ref, sums_ref, w1_ref, ds_ref
):
    width = mid_ref.shape[1]
    hidden_width = dh_ref.shape[1]
    ready()

    def back_in(start):
        rows = pl.ds(start, CHUNK)
        made = dot_nt(dh_ref[:, 0:width], w1_ref[0, rows, :])
        for block in range(1, hidden_width // width):
            made += dot_nt(
                dh_ref[:, block * width : (block + 1) * width], w1_ref[block, rows, :]
            )
        ds_ref[:, rows] = made

    each(width // CHUNK, CHUNK, back_in)
    flow.need(mid_ref, grad_ref)

    def back_norm(start):
        rows = pl.ds(start, ROWS_STEP)
        normed, inverse = norm_rows(mid_ref[rows, :])
        grad = ds_ref[rows, :]
        sums_ref[5:6, :] += jnp.sum(grad * normed, 0, keepdims=True)
        sums_ref[6:7, :] += jnp.sum(grad, 0, keepdims=True)
        dmid_ref[rows, :] = grad_ref[rows, :].astype(F32) + norm_back(
            grad, normed, inverse, vec_ref[5:6, :]
        )

    each(mid_ref.shape[0] // ROWS_STEP, ROWS_STEP, back_norm)


def top_back_kernel(plan, source, flow, *refs):
    (grad_ref, mid_ref, live_ref, vec_ref, h2_ref, slope_ref), refs = refs[:6], refs[6:]
    weight_refs, refs = refs[: source.count], refs[source.count :]
    (dmid_ref, sums_ref, hsum_ref), refs = refs[:3], refs[3:]
    sink_refs, refs = refs[: plan.sinks], refs[plan.sinks :]
    (w1_ref, w2_ref, dm_ref, dh_ref, ds_ref, sem, sem2), refs = refs[:7], refs[7:]
    sink = plan.sink(sink_refs, refs, False)
    ready2 = source.load("fc2", weight_refs, w2_ref, sem2)
    ready1 = source.load("fc1", weight_refs, w1_ref, sem)
    sums_ref[...] = jnp.zeros_like(sums_ref)
    flow.need(grad_ref)
    dm_ref[...] = (live_ref[...] * grad_ref[...].astype(F32)).astype(BF16)
    hidden_back(flow, ready2, sink, h2_ref, slope_ref, dh_ref, hsum_ref, w2_ref, dm_ref)
    middle_back(
        flow, ready1, grad_ref, mid_ref, vec_ref, dh_ref, dmid_ref, sums_ref, w1_ref, ds_ref
    )
    sink.wait()


def scores_back_kernel(source, flow, *refs):
    (
        dmid_ref, live_ref, table_ref, keys_ref, q_ref, k_ref, v_ref, p_ref,
    ), refs = refs[:8], refs[8:]
    weight_refs, refs = refs[: source.count], refs[source.count :]
    db_ref, dq_ref, dk_ref, dv_ref, sums_ref, rel_ref, w_ref, da_ref, sem = refs
    ready = source.load("proj", weight_refs, w_ref, sem)
    width = dmid_ref.shape[1]
    flow.need(dmid_ref)
    db_ref[...] = (live_ref[...] * dmid_ref[...]).astype(BF16)
    flow.emit(db_ref)
    sums_ref[...] = jnp.zeros_like(sums_ref)
    sums_ref[0:1, :] = jnp.sum(db_ref[...].astype(F32), 0, keepdims=True)
    rel_ref[...] = jnp.zeros_like(rel_ref)
    ready()

    def back_out(start):
        rows = pl.ds(start, CHUNK)
        da_ref[:, rows] = dot_nt(db_ref[...], w_ref[rows, :]).astype(BF16)

    each(width // CHUNK, CHUNK, back_out)
    flow.need(v_ref, p_ref, k_ref, q_ref)

    def attend(index):
        rows = pl.ds(pl.multiple_of(index // PAIRS * SPAN, SPAN), SPAN)
        cols = pl.ds(pl.multiple_of(index % PAIRS * LANES, LANES), LANES)
        low = p_ref[index]
        probs = low.astype(F32)
        outer = split_heads(da_ref[rows, cols])
        queries = split_heads(q_ref[rows, cols])
        d_probs = dot_nt(outer, v_ref[rows, cols])
        dv_ref[rows, cols] = dot_tn(low, outer).astype(BF16)
        mean = jnp.sum(d_probs * probs, -1, keepdims=True)
        d_scores = (probs * (d_probs - mean)).astype(BF16)
        both = dot_nn(d_scores, jnp.concatenate([k_ref[rows, cols], keys_ref[...]], axis=1))
        moved = [
            shift_rows(both[half * SPAN : (half + 1) * SPAN, LANES:]).astype(BF16)
            for half in range(2)
        ]
        rel_part = dot_nt(jnp.concatenate(moved, axis=1), table_ref[...])
        direct = join_heads(both[:, :LANES]) * HD ** (-0.5)
        dq_ref[rows, cols] = (direct + rel_part).astype(BF16)
        dk_ref[rows, cols] = (dot_tn(d_scores, queries) * HD ** (-0.5)).astype(BF16)
        rel_ref[...] += dot_tn(jnp.concatenate(moved, axis=0), queries)

    in_fours(dmid_ref.shape[0] // SPAN * PAIRS, attend)
    flow.emit(dq_ref, dk_ref, dv_ref)
    sums_ref[1:2, :] = jnp.sum(dq_ref[...].astype(F32), 0, keepdims=True)
    sums_ref[2:3, :] = jnp.sum(dv_ref[...].astype(F32), 0, keepdims=True)


def first_weights(flow, sink, h1_ref, att_ref, db_ref, dq_ref, dk_ref, dv_ref):
    pairs = ((h1_ref, dq_ref), (h1_ref, dk_ref), (h1_ref, dv_ref), (att_ref, db_ref))
    for index, (left_ref, right_ref) in enumerate(pairs):
        flow.need(left_ref, right_ref)

        def weight(start, index=index, left_ref=left_ref, right_ref=right_ref):
            cols = pl.ds(start, CHUNK)
            sink.cols(index, cols, dot_tn(left_ref[...], right_ref[:, cols]).astype(BF16))

        each(h1_ref.shape[1] // CHUNK, CHUNK, weight)
        sink.send(index)


def first_weights_kernel(plan, flow, *refs):
    sink = plan.sink(refs[6 : 6 + plan.sinks], refs[6 + plan.sinks :], True)
    first_weights(flow, sink, *refs[:6])
    sink.wait()


def first_back(
    flow, ready, dmid_ref, x_ref, live_ref, vec_ref, dq_ref, dk_ref, dv_ref, next_ref, sums_ref,
    w_ref, dh_ref,
):
    width = x_ref.shape[1]
    flow.need(dq_ref, dk_ref, dv_ref)
    ready()

    def back_in(start):
        rows = pl.ds(start, CHUNK)
        made = dot_nt(dq_ref[...], w_ref[0, rows, :])
        made += dot_nt(dk_ref[...], w_ref[1, rows, :])
        made += dot_nt(dv_ref[...], w_ref[2, rows, :])
        dh_ref[:, rows] = made * live_ref[...]

    each(width // CHUNK, CHUNK, back_in)
    flow.need(x_ref, dmid_ref)
    sums_ref[...] = jnp.zeros_like(sums_ref)

    def back_norm(start):
        rows = pl.ds(start, ROWS_STEP)
        normed, inverse = norm_rows(x_ref[rows, :].astype(F32))
        grad = dh_ref[rows, :]
        sums_ref[3:4, :] += jnp.sum(grad * normed, 0, keepdims=True)
        sums_ref[4:5, :] += jnp.sum(grad, 0, keepdims=True)
        next_ref[rows, :] = dmid_ref[rows, :] + norm_back(grad, normed, inverse, vec_ref[0:1, :])

    each(x_ref.shape[0] // ROWS_STEP, ROWS_STEP, back_norm)


def first_back_kernel(source, flow, *refs):
    ins, refs = refs[:7], refs[7:]
    weight_refs, refs = refs[: source.count], refs[source.count :]
    next_ref, sums_ref, w_ref, dh_ref, sem = refs
    ready = source.load("attend", weight_refs, w_ref, sem)
    first_back(flow, ready, *ins, next_ref, sums_ref, w_ref, dh_ref)


def first_all_kernel(plan, source, flow, *refs):
    (dmid_ref, x_ref, live_ref, vec_ref, h1_ref, att_ref, db_ref), refs = refs[:7], refs[7:]
    (dq_ref, dk_ref, dv_ref), refs = refs[:3], refs[3:]
    weight_refs, refs = refs[: source.count], refs[source.count :]
    (next_ref, sums_ref), refs = refs[:2], refs[2:]
    sink_refs, refs = refs[: plan.sinks], refs[plan.sinks :]
    (w_ref, dh_ref, sem), refs = refs[:3], refs[3:]
    sink = plan.sink(sink_refs, refs, True)
    ready = source.load("attend", weight_refs, w_ref, sem)
    first_weights(flow, sink, h1_ref, att_ref, db_ref, dq_ref, dk_ref, dv_ref)
    first_back(
        flow, ready, dmid_ref, x_ref, live_ref, vec_ref, dq_ref, dk_ref, dv_ref, next_ref,
        sums_ref, w_ref, dh_ref,
    )
    sink.wait()


VM = pl.BlockSpec(memory_space=pltpu.VMEM)
ANY = pl.BlockSpec(memory_space=pltpu.HBM)


def shape(dims, kind):
    return jax.ShapeDtypeStruct(tuple(dims), kind)


class Source:
    def __init__(self, **parts):
        self.parts = parts
        self.arrays = []
        self.places = {}
        for name, (arrays, _, _) in parts.items():
            found = []
            for array in arrays:
                known = [i for i, other in enumerate(self.arrays) if other is array]
                if not known:
                    known = [len(self.arrays)]
                    self.arrays.append(array)
                found.append(known[0])
            self.places[name] = found
        self.count = len(self.arrays)

    def semaphores(self, name):
        whole = self.parts[name][1] is None
        return pltpu.SemaphoreType.DMA((4 if whole else 8 if name == "proj" else 32,))

    def load(self, name, refs, target, sem):
        arrays, offset, rotated = self.parts[name]
        refs = [refs[i] for i in self.places[name]]
        if offset is not None and name == "proj":
            return load_proj(refs, target, offset, rotated, sem)
        if offset is None:
            pairs = whole_pairs(name, refs, target)
        else:
            pairs = [pair for _, _, pair in piece_pairs(name, refs, target, offset, rotated)]
        copies = [
            pltpu.make_async_copy(given, taken, sem.at[i])
            for i, (given, taken) in enumerate(pairs)
        ]
        for copy in copies:
            copy.start()

        def ready():
            for copy in copies:
                copy.wait()

        return ready


def whole_pairs(name, refs, target):
    if name == "fc2":
        return [(refs[0], target)]
    if name == "proj":
        return [(refs[1], target)]
    width = target.shape[1]
    pairs = []
    for ref in refs:
        for start in range(0, ref.shape[1], width):
            pairs.append((ref.at[:, pl.ds(start, width)], target.at[len(pairs)]))
    return pairs


def position():
    shard = lax.axis_index("fsdp")
    return lax.axis_index("rep"), shard >> 1, shard & 1


def piece_pairs(name, refs, target, offset, rotated):
    rep, level, core = position()
    pairs = []
    rows = target.shape[-2] // 8
    span = rows // 4 if name == "fc2" else rows
    for parity in range(2):
        for part, (away, levels) in enumerate(
            ((0, range(4)), (1, range(4)), (2, range(4)), (3, range(2)), (3, range(2, 4)))
        ):
            ref = refs[parity * 5 + part]
            for place, step in enumerate(levels):
                source_level = (level - step) & 3 if rotated else step
                shard = source_level * 2 + (core ^ parity)
                kind = rep ^ away
                if name == "fc2":
                    start = pl.multiple_of(shard * rows + kind * span, 16)
                    taken = target.at[pl.ds(start, span), :]
                else:
                    start = pl.multiple_of(shard * span, 16)
                    whole = target if name == "proj" else target.at[kind]
                    taken = whole.at[pl.ds(start, span), :]
                given = ref.at[place, pl.ds(offset, span), :]
                pairs.append((away, parity * 4 + step, (given, taken)))
    return pairs


def load_proj(refs, target, offset, rotated, sem):
    rep = lax.axis_index("rep")
    pairs = piece_pairs("proj", refs, target, offset, rotated)
    for away in range(4):

        @pl.when((rep ^ away) == 3)
        def _(away=away):
            for other, slot, pair in pairs:
                if other == away:
                    pltpu.make_async_copy(*pair, sem.at[slot]).start()

    def ready():
        for away, slot, pair in pairs:
            if away == 0:
                pltpu.make_async_copy(*pair, sem.at[slot]).wait()

    return ready


class WholeSink:
    def __init__(self, refs, scratch):
        self.ref = refs[0]
        self.held, self.sem = scratch[:2]
        self.sent = []

    def rows(self, index, value):
        self.held[pl.ds(pl.multiple_of(index * SLAB, SLAB), SLAB), :] = value

    def cols(self, block, cols, value):
        self.held[block, :, cols] = value

    def copy(self, given, taken):
        copy = pltpu.make_async_copy(given, taken, self.sem.at[len(self.sent)])
        copy.start()
        self.sent.append(copy)

    def send(self, block):
        self.copy(self.held.at[block], self.ref.at[block])

    def send_all(self):
        self.copy(self.held, self.ref)

    def wait(self):
        for copy in self.sent:
            copy.wait()


class PieceSink:
    def __init__(self, refs, scratch, rotated, offset=0):
        self.refs, self.rotated, self.offset = refs, rotated, offset
        self.held, self.sem = scratch[:2]
        self.position = position()
        self.sent = []

    def rows(self, index, value):
        span = self.held.shape[3]
        for block in range(4):
            self.held[index & 1, block, index >> 1] = value[block * span : (block + 1) * span]

    def cols(self, block, cols, value):
        span = self.held.shape[3]
        for shard in range(8):
            self.held[shard & 1, block, shard >> 1, :, cols] = value[
                shard * span : (shard + 1) * span
            ]

    def send(self, block):
        rep, level, core = self.position
        for parity in range(2):
            given = self.held.at[core ^ parity, block]
            span = self.held.shape[3]
            taken = self.refs[parity].at[rep ^ block, :, pl.ds(self.offset, span)]
            moves = [(given, taken)]
            if self.rotated:
                moves = [(given.at[(level + step) & 3], taken.at[step]) for step in range(4)]
            for move in moves:
                copy = pltpu.make_async_copy(*move, self.sem.at[len(self.sent)])
                copy.start()
                self.sent.append(copy)

    def send_all(self):
        for block in range(4):
            self.send(block)

    def wait(self):
        for copy in self.sent:
            copy.wait()


class WholePlan:
    sinks = 1

    def sink(self, refs, scratch, rotated=False):
        return WholeSink(refs, scratch)

    def sink_outs(self, dims):
        return [shape(dims, BF16)], [ANY], [pltpu.VMEM(dims, BF16), pltpu.SemaphoreType.DMA((4,))]

    def two_sinks(self, refs, scratch, rotated):
        return WholeSink(refs[:1], scratch), WholeSink(refs[1:], scratch[2:])

    def two_outs(self, hidden, width):
        one = self.sink_outs((hidden, width))
        two = self.sink_outs((hidden // width, width, width))
        return one[0] + two[0], one[1] + two[1], one[2] + two[2]


class PiecePlan:
    sinks = 2

    def sink(self, refs, scratch, rotated=False):
        return PieceSink(refs, scratch, rotated)

    def sink_outs(self, dims):
        width = dims[-1]
        span = int(np.prod(dims)) // width // 32
        outs = [shape((4, 4, span, width), BF16)] * 2
        scratch = [pltpu.VMEM((2, 4, 4, span, width), BF16), pltpu.SemaphoreType.DMA((32,))]
        return outs, [ANY] * 2, scratch

    def two_sinks(self, refs, scratch, rotated):
        span = scratch[0].shape[3]
        return PieceSink(refs, scratch, rotated), PieceSink(refs, scratch[2:], rotated, span)

    def two_outs(self, hidden, width):
        span = hidden // 32
        outs = [shape((4, 4, 2 * span, width), BF16)] * 2
        scratch = [pltpu.VMEM((2, 4, 4, span, width), BF16), pltpu.SemaphoreType.DMA((32,))] * 2
        return outs, [ANY] * 2, scratch


def large(array):
    return int(np.prod(array.shape)) * np.dtype(array.dtype).itemsize >= LARGE


def call(kernel, resident, source, outs, scratch, micros, sinks=(), after=()):
    sink_outs, sink_specs, sink_scratch = [], [], []
    for more_outs, more_specs, more_scratch in sinks:
        sink_outs += more_outs
        sink_specs += more_specs
        sink_scratch += more_scratch
    in_moves = [i for i, a in enumerate(resident) if large(a)]
    out_moves = [i for i, a in enumerate(outs) if large(a)]
    buffers = [pltpu.VMEM(resident[i].shape, resident[i].dtype) for i in in_moves]
    buffers += [pltpu.VMEM(outs[i].shape, outs[i].dtype) for i in out_moves]
    semaphores = [
        pltpu.SemaphoreType.DMA((max(len(moves), 1),)) for moves in (in_moves, out_moves)
    ]
    count = len(resident)
    first = count + source.count

    def body(*refs):
        ins, weights = list(refs[:count]), refs[count:first]
        refs = refs[first + len(after) :]
        made, refs = list(refs[: len(outs)]), refs[len(outs) :]
        sunk, refs = refs[: len(sink_outs)], refs[len(sink_outs) :]
        held, refs = refs[: len(buffers)], refs[len(buffers) :]
        in_sem, out_sem, *rest = refs
        in_held, out_held = held[: len(in_moves)], held[len(in_moves) :]
        flow = Flow(
            [(ins[i], ref) for i, ref in zip(in_moves, in_held)],
            in_sem,
            [(ref, made[i]) for i, ref in zip(out_moves, out_held)],
            out_sem,
        )
        for i, ref in zip(in_moves, in_held):
            ins[i] = ref
        for i, ref in zip(out_moves, out_held):
            made[i] = ref
        kernel(flow, *ins, *weights, *made, *sunk, *rest)
        flow.finish()

    run = pl.pallas_call(
        body,
        out_shape=tuple([*outs, *sink_outs]),
        in_specs=[ANY if large(a) else VM for a in resident]
        + [ANY] * (source.count + len(after)),
        out_specs=tuple([*[ANY if large(a) else VM for a in outs], *sink_specs]),
        scratch_shapes=[*buffers, *semaphores, *scratch, *sink_scratch],
        compiler_params=pltpu.CompilerParams(vmem_limit_bytes=VMEM_LIMIT),
        cost_estimate=pl.CostEstimate(
            flops=int(micros * 1e9), bytes_accessed=1 << 20, transcendentals=0
        ),
    )
    return run(*resident, *source.arrays, *after)


def attend_forward(x, live, vec, table, keys, source, after):
    rows, width = x.shape
    outs = (
        shape((rows, width), F32),
        *[shape((rows, width), BF16)] * 4,
        shape((rows // SPAN * PAIRS, 2 * SPAN, SPAN), BF16),
        shape((rows, width), BF16),
        shape((8, LANES), F32),
    )
    scratch = [pltpu.VMEM((4, width, width), BF16), source.semaphores("attend")]
    return call(
        functools.partial(attend_kernel, source),
        (x, live, vec, table, keys), source, outs, scratch, 20, (), after,
    )


def mlp_forward(plan, top, mid, live, vec, bias, grad, source, after):
    rows, width = mid.shape
    hidden = bias.shape[1]
    outs = [
        shape((rows, width), BF16), shape((rows, hidden), BF16), shape((rows, hidden), BF16),
    ]
    scratch = [pltpu.VMEM((hidden // width, width, width), BF16)]
    resident = [mid, live, vec, bias]
    sinks = []
    if top:
        resident.append(grad)
        outs.append(shape((8, width), F32))
        scratch += [pltpu.VMEM((rows, width), BF16), source.semaphores("fc1")]
        sinks.append(plan.sink_outs((hidden, width)))
    else:
        outs.insert(0, shape((rows, width), F32))
        scratch += [
            pltpu.VMEM((hidden, width), BF16), source.semaphores("fc1"),
            source.semaphores("fc2"),
        ]
    return call(
        functools.partial(mlp_kernel, plan, source, top),
        resident, source, outs, scratch, 16, sinks, after,
    )


def mlp_output(act, vec, mid, live, source, after):
    hidden, width = act.shape[1], mid.shape[1]
    scratch = [pltpu.VMEM((hidden, width), BF16), source.semaphores("fc2")]
    return call(
        functools.partial(out_kernel, source), (act, vec, mid, live), source,
        [shape(mid.shape, F32)], scratch, 5, (), after,
    )[0]


def hidden_backward(plan, grad, act, live, h2, slope, source, after):
    rows, width = h2.shape
    hidden = slope.shape[1]
    outs = [shape((rows, hidden), BF16), shape((8, width), F32), shape((1, hidden), F32)]
    scratch = [
        pltpu.VMEM((hidden, width), BF16), pltpu.VMEM((rows, width), BF16),
        source.semaphores("fc2"),
    ]
    return call(
        functools.partial(hidden_back_kernel, plan, source),
        (grad, act, live, h2, slope), source, outs, scratch, 18,
        [plan.two_outs(hidden, width)], after,
    )


def top_backward(plan, grad, mid, live, vec, h2, slope, source, after):
    rows, width = mid.shape
    hidden = slope.shape[1]
    outs = [shape((rows, width), F32), shape((8, width), F32), shape((1, hidden), F32)]
    scratch = [
        pltpu.VMEM((hidden // width, width, width), BF16), pltpu.VMEM((hidden, width), BF16),
        pltpu.VMEM((rows, width), BF16), pltpu.VMEM((rows, hidden), BF16),
        pltpu.VMEM((rows, width), F32), source.semaphores("fc1"), source.semaphores("fc2"),
    ]
    return call(
        functools.partial(top_back_kernel, plan, source),
        (grad, mid, live, vec, h2, slope), source, outs, scratch, 19,
        [plan.sink_outs((hidden // width, width, width))], after,
    )


def middle_backward(grad, mid, vec, dh, source, after):
    rows, width = mid.shape
    hidden = dh.shape[1]
    outs = [shape((rows, width), F32), shape((8, width), F32)]
    scratch = [
        pltpu.VMEM((hidden // width, width, width), BF16), pltpu.VMEM((rows, width), F32),
        source.semaphores("fc1"),
    ]
    return call(
        functools.partial(middle_back_kernel, source),
        (grad, mid, vec, dh), source, outs, scratch, 10, (), after,
    )


def scores_backward(dmid, live, table, keys, q, k, v, p, source, after):
    rows, width = dmid.shape
    outs = [*[shape((rows, width), BF16)] * 4, shape((8, width), F32), shape((LANES, LANES), F32)]
    scratch = [
        pltpu.VMEM((width, width), BF16), pltpu.VMEM((rows, width), BF16),
        source.semaphores("proj"),
    ]
    return call(
        functools.partial(scores_back_kernel, source),
        (dmid, live, table, keys, q, k, v, p), source, outs, scratch, 15, (), after,
    )


def weights_backward(plan, h1, att, db, dq, dk, dv, after):
    width = h1.shape[1]
    return call(
        functools.partial(first_weights_kernel, plan), (h1, att, db, dq, dk, dv),
        Source(), [], [], 8, [plan.sink_outs((4, width, width))], after,
    )


def first_backward(dmid, x, live, vec, dq, dk, dv, source, after):
    rows, width = x.shape
    outs = [shape((rows, width), F32), shape((8, width), F32)]
    scratch = [
        pltpu.VMEM((4, width, width), BF16), pltpu.VMEM((rows, width), F32),
        source.semaphores("attend"),
    ]
    return call(
        functools.partial(first_back_kernel, source),
        (dmid, x, live, vec, dq, dk, dv), source, outs, scratch, 10, (), after,
    )


def first_all_backward(plan, dmid, x, live, vec, h1, att, db, dq, dk, dv, source, after):
    rows, width = x.shape
    outs = [shape((rows, width), F32), shape((8, width), F32)]
    scratch = [
        pltpu.VMEM((4, width, width), BF16), pltpu.VMEM((rows, width), F32),
        source.semaphores("attend"),
    ]
    return call(
        functools.partial(first_all_kernel, plan, source),
        (dmid, x, live, vec, h1, att, db, dq, dk, dv), source, outs, scratch, 14,
        [plan.sink_outs((4, width, width))], after,
    )


def live_rows(slot_table):
    places = jnp.arange(PITCH, dtype=jnp.int32)
    rows_inside = slot_table[:, None] // GRID * WINDOW + places[None, :WINDOW] < SIDE
    cols_inside = slot_table[:, None] % GRID * WINDOW + places[None, :] < SIDE
    cols_inside = cols_inside & (places < WINDOW)[None, :]
    both_inside = rows_inside[:, :, None] & cols_inside[:, None, :]
    return both_inside.astype(F32).reshape(slot_table.shape[0] * SPAN, 1)


def spread(values):
    width = values.shape[1]
    grid = values.reshape(-1, WINDOW, width)
    return jnp.pad(grid, ((0, 0), (0, PITCH - WINDOW), (0, 0))).reshape(-1, width)


def gather_back(values):
    width = values.shape[1]
    return values.reshape(-1, PITCH, width)[:, :WINDOW].reshape(-1, width)


def relative_tables(rel_height, rel_width):
    stacked = jnp.stack([rel_height, rel_width], 1).reshape(LAYERS, 2, RELS, HD)

    def spread_table(rows):
        padded = jnp.pad(rows, ((0, 0), (0, 0), (0, HD - RELS), (0, 0)))
        one = padded.reshape(LAYERS, LANES, HD).transpose(0, 2, 1)
        none = jnp.zeros_like(one)
        return jnp.concatenate(
            [jnp.concatenate([one, none], 2), jnp.concatenate([none, one], 2)], 1
        )

    return spread_table(stacked[:, :, ::-1]), spread_table(stacked)


def whole_weights(weights):
    qkv, proj, fc1, fc2 = weights
    layers = []
    for layer in range(LAYERS):
        q, p, a, b = (
            lax.all_gather(w[layer], "fsdp", axis=0, tiled=True) for w in (qkv, proj, fc1, fc2)
        )
        layers.append(
            dict(attend=((q, p), None, False), proj=((q, p), None, False), fc1=((a,), None, False), fc2=((b,), None, False))
        )
    return layers


def whole_small(parts):
    packed = jnp.concatenate(parts, axis=1)
    return lax.all_gather(packed, "fsdp", axis=0, tiled=False)


def whole_reduce(value, axis):
    return lax.psum(lax.psum_scatter(value, "fsdp", scatter_dimension=axis, tiled=True), "rep")


def whole_sums(grads):
    (g,), (g2, g1) = grads
    return whole_reduce(g, 1), whole_reduce(g1, 1), whole_reduce(g2, 0)


def named(g, g1, g2):
    return jnp.concatenate([g[0], g[1], g[2]], 1), g[3], jnp.concatenate(list(g1), 1), g2


def permute(value, axis, move):
    return lax.ppermute(value, axis, [(i, move(i)) for i in range({"rep": 4, "fsdp": 8}[axis])])


def to_x(value):
    return permute(value, "rep", lambda i: i ^ 1)


def to_y(value):
    return permute(value, "rep", lambda i: i ^ 2)


def to_xy(value):
    return permute(value, "rep", lambda i: i ^ 3)


def to_core(value):
    return permute(value, "fsdp", lambda i: i ^ 1)


def to_level(value, step):
    return permute(value, "fsdp", lambda i: (i + 2 * step) % 8)


LEVELS = [[0, 2, 4, 6], [1, 3, 5, 7]]


def nothing(value):
    return jnp.minimum(jnp.abs(value), 0)


def swap(value, flag, axis):
    first = lax.slice_in_dim(value, 0, 1, axis=axis)
    second = lax.slice_in_dim(value, 1, 2, axis=axis)
    return jnp.where(flag == 1, jnp.concatenate([second, first], axis), value)


def by_replica(value, rep):
    rest = value.shape[1:]
    value = value.reshape(2, 2, *rest)
    value = swap(swap(value, rep & 1, 1), rep >> 1, 0)
    return value.reshape(4, *rest)


def turn(value, start, axis):
    size = value.shape[axis]
    return lax.dynamic_slice_in_dim(
        jnp.concatenate([value, value], axis), start, size, axis
    )


def own_blocks(weights, layer, rep):
    qkv, proj, fc1, fc2 = (w[layer] for w in weights)
    width = proj.shape[1]
    span = proj.shape[0]
    first = lax.dynamic_slice_in_dim(jnp.concatenate([qkv, proj], 1), rep * width, width, 1)
    second = lax.dynamic_slice_in_dim(fc1, rep * width, width, 1)
    third = lax.dynamic_slice_in_dim(fc2, rep * span, span, 0)
    return first, second, third


class Across:
    def __init__(self, held):
        self.held = held
        self.x, self.y = to_x(held), to_y(held)

    def cross(self, token=None):
        low, high = self.y[:2], self.x[2:]
        if token is not None:
            low, high = low + token, high + token
        self.low, self.high = to_x(low), to_y(high)
        return low, high

    def finish(self, token=None):
        low, high = self.low, self.high
        if token is not None:
            low, high = low + token, high + token
        pieces = (self.held, self.x, self.y, low, high)
        return pieces + tuple(to_core(piece) for piece in pieces)


class PieceWeights:
    def __init__(self, weights, small):
        rep, level, core = position()
        blocks = [own_blocks(weights, layer, rep) for layer in range(LAYERS)]
        span, width = blocks[0][0].shape
        size = small.shape[0] // 4
        rider = lax.dynamic_slice_in_dim(small, rep * size, size, 0)
        rider = jnp.pad(rider, (0, RIDERS * width - size)).reshape(RIDERS, width)
        first = jnp.concatenate([*blocks[0][:2], rider], 0)[None]
        self.span = span
        held = jnp.concatenate([first] + [to_level(first, step) for step in (1, 2, 3)], 0)
        self.rest = lax.all_gather(
            jnp.concatenate([blocks[0][2], blocks[1][0]], 0) + nothing(held[3, 0, 0]), "fsdp",
            axis=0, tiled=True, axis_index_groups=LEVELS,
        ).reshape(4, 2 * span, width)
        self.fc1 = lax.all_gather(
            weights[2][1] + nothing(self.rest[0, 0, 0]), "fsdp", axis=0, tiled=True
        )
        self.fc2 = lax.all_gather(
            weights[3][1] + nothing(self.fc1[0, 0]), "fsdp", axis=0, tiled=True
        )
        one = Across(held)
        one.cross()
        self.one = one.finish()
        riders = jnp.stack(
            [
                jnp.concatenate([t[:, 2 * span :] for t in self.one[5 * p : 5 * p + 5]], 0).reshape(
                    4, 4, RIDERS * width
                )[:, :, :size]
                for p in range(2)
            ]
        )
        riders = by_replica(swap(riders, core, 0).transpose(1, 0, 2, 3), rep)
        turned = jnp.concatenate([riders[:, :, i : i + 1] for i in (3, 2, 1, 0)], 2)
        riders = turn(turned, 3 - level, 2)
        self.small = riders.transpose(2, 1, 0, 3).reshape(8, LAYERS, -1)

    def before(self, name):
        if name == "attend_0":
            self.next = Across(self.rest)
            return (self.rest,)
        if name == "mlp_0":
            self.two = self.next.finish()
        return ()

    def passed(self, name, token):
        if name == "attend_0":
            self.next.cross(token[0, 0].astype(BF16))

    def source(self, layer, *names):
        if layer == 0:
            parts = dict(
                attend=lambda: (self.one, 0, True),
                proj=lambda: (self.one, 0, True),
                fc1=lambda: (self.one, self.span, True),
                fc2=lambda: (self.two, 0, False),
            )
        else:
            parts = dict(
                attend=lambda: (self.two, self.span, False),
                proj=lambda: (self.two, self.span, False),
                fc1=lambda: ((self.fc1,), None, False),
                fc2=lambda: ((self.fc2,), None, False),
            )
        return Source(**{name: parts[name]() for name in names})


class WholeWeights:
    def __init__(self, weights, small):
        self.small = whole_small(small)
        self.layers = whole_weights(weights)

    def before(self, name):
        return ()

    def passed(self, name, token):
        pass

    def source(self, layer, *names):
        return Source(**{name: self.layers[layer][name] for name in names})


class ReplicaSum:
    def __init__(self, *pairs):
        self.pairs = [(keep, to_core(send)) for keep, send in pairs]
        self.step = 0

    def both(self, away, part):
        sums = [
            keep[away, part].astype(F32) + got[away, part].astype(F32) for keep, got in self.pairs
        ]
        return sums[0] if len(sums) == 1 else jnp.concatenate(sums, -2)

    def advance(self):
        low, high = slice(0, 2), slice(2, 4)
        self.step += 1
        if self.step == 1:
            send_x = self.both(slice(1, 4, 2), low).astype(BF16)
            send_y = self.both(slice(2, 4), high).astype(BF16)
            self.x, self.y = to_x(send_x), to_y(send_y)
            return [send_x, send_y]
        if self.step == 2:
            send_y = (self.both(2, low) + self.x[1].astype(F32)).astype(BF16)
            send_x = (self.both(1, high) + self.y[1].astype(F32)).astype(BF16)
            self.last_y, self.last_x = to_y(send_y), to_x(send_x)
            return [send_x, send_y]
        if self.step == 4:
            low, high = self.result
            sends = (low[1], high[0], high[1])
            self.levels = [to_level(send, step + 1) for step, send in enumerate(sends)]
            return list(sends)
        if self.step == 5:
            total = self.result[0][0].astype(F32)
            for got in self.levels:
                total = total + got.astype(F32)
            self.total = total.astype(BF16)
            return [self.total]
        self.result = [
            (self.both(0, low) + self.x[0].astype(F32) + self.last_y.astype(F32)).astype(BF16),
            (self.both(0, high) + self.y[0].astype(F32) + self.last_x.astype(F32)).astype(BF16),
        ]
        return self.result


class PieceSums:
    def __init__(self, plan):
        self.plan = plan
        self.sums = {}

    def add(self, name, pair):
        self.sums[name] = ReplicaSum(pair)

    def advance(self, *names):
        found = []
        for name in names:
            found += self.sums[name].advance()
        return found

    def finish(self, sums, top):
        last = self.sums["attend"]
        riders = ReplicaSum(pack_riders(self.plan, sums))
        span, width = last.pairs[0][0].shape[2:]
        last.advance()
        for _ in range(3):
            riders.advance()
        self.advance("mlp", "mlp", "mlp")
        last.advance()
        last.advance()
        first = last.result[0][0, 0, 0]
        last.result = [jnp.concatenate(pair, 1) for pair in zip(last.result, riders.result)]
        last.advance()
        late = to_replicas(self.sums["mlp"].total + nothing(first))
        last.advance()
        self.token = first
        g, g1, g2 = top
        big = assemble_late(g1, g2, late)
        return assemble_last(to_replicas(last.total), g), big


def to_replicas(value):
    return value, to_x(value), to_y(value), to_xy(value)


def load_replicas(refs, held, sem):
    rep = lax.axis_index("rep")
    copies = [
        pltpu.make_async_copy(ref, held.at[rep ^ away], sem.at[away])
        for away, ref in enumerate(refs)
    ]
    for copy in copies:
        copy.start()
    return copies


def late_kernel(flow, g1_ref, g2_ref, *refs):
    held, sem = refs[6:]
    fc1_ref, fc2_ref = refs[4:6]
    copies = load_replicas(refs[:4], held, sem)
    width = fc2_ref.shape[2]
    span = g1_ref.shape[1]
    flow.need(g1_ref, g2_ref)
    fc2_ref[1] = g2_ref[...].astype(F32)
    for block in range(4):
        fc1_ref[1, :, block * width : (block + 1) * width] = g1_ref[block].astype(F32)
    for copy in copies:
        copy.wait()
    for block in range(4):
        fc1_ref[0, :, block * width : (block + 1) * width] = held[block, span:].astype(F32)
        fc2_ref[0, block * span : (block + 1) * span, :] = held[block, :span].astype(F32)


def assemble_late(g1, g2, late):
    _, span, width = g1.shape
    return call(
        late_kernel, (g1, g2), Pieces(late),
        [shape((LAYERS, span, 4 * width), F32), shape((LAYERS, 4 * span, width), F32)],
        [pltpu.VMEM((4, *late[0].shape), BF16), pltpu.SemaphoreType.DMA((4,))], 4,
    )


class Pieces:
    def __init__(self, arrays):
        self.arrays, self.count = arrays, len(arrays)


def last_kernel(flow, g_ref, *refs):
    last_refs, refs = refs[:4], refs[4:]
    (qkv_ref, proj_ref), refs = refs[:2], refs[2:]
    small_refs, (held, sem) = refs[:10], refs[10:]
    copies = load_replicas(last_refs, held, sem)
    width = proj_ref.shape[2]
    span = g_ref.shape[1]
    flow.need(g_ref)

    def put(layer, source):
        for block in range(3):
            qkv_ref[layer, :, block * width : (block + 1) * width] = source[
                block, :span
            ].astype(F32)
        proj_ref[layer] = source[3, :span].astype(F32)

    put(1, g_ref)
    for copy in copies:
        copy.wait()
    put(0, held)
    unit = width // 8
    heads = held[0, span:].astype(F32)
    others = held[1, span:].astype(F32)
    rel = held[2, span:].astype(F32)
    qv, pb, n1g, n1b, n2g, n2b, f1b, f2b, rh, rw = small_refs
    size = rh.shape[1]
    for layer in range(LAYERS):
        for ref, row in ((pb, 0), (n1g, 3), (n1b, 4), (n2g, 5), (n2b, 6), (f2b, 7)):
            ref[layer : layer + 1, :] = heads[row : row + 1, layer * unit : (layer + 1) * unit]
        qv[layer : layer + 1, :] = others[layer : layer + 1, : 2 * unit]
        f1b[layer : layer + 1, :] = others[layer : layer + 1, 2 * unit : 6 * unit]
        rh[layer : layer + 1, :] = rel[2 * layer : 2 * layer + 1, :size]
        rw[layer : layer + 1, :] = rel[2 * layer + 1 : 2 * layer + 2, :size]


def assemble_last(last, g):
    _, span, width = g.shape
    unit = width // 8
    sizes = (2 * unit, *[unit] * 5, 4 * unit, unit, RELS * HD // 8, RELS * HD // 8)
    outs = [shape((LAYERS, span, 3 * width), F32), shape((LAYERS, span, width), F32)]
    outs += [shape((LAYERS, size), F32) for size in sizes]
    return call(
        last_kernel, (g,), Pieces(last), outs,
        [pltpu.VMEM((4, *last[0].shape), BF16), pltpu.SemaphoreType.DMA((4,))], 4,
    )


def pack_kernel(plan, flow, *refs):
    (
        (heads_ref, hidden_ref, rel_ref), (heads1_ref, hidden1_ref, rel1_ref)
    ), refs = (refs[:3], refs[3:6]), refs[6:]
    sink = plan.sink(refs[: plan.sinks], refs[plan.sinks :], True)
    held = sink.held
    held[...] = jnp.zeros_like(held)
    layers = ((heads_ref, hidden_ref, rel_ref), (heads1_ref, hidden1_ref, rel1_ref))
    span = heads_ref.shape[1] // 8
    for layer, (heads, hidden, rel) in enumerate(layers):
        for shard in range(8):
            core, level = shard & 1, shard >> 1
            cut = heads[:, shard * span : (shard + 1) * span]
            held[core, 0, level, :, layer * span : (layer + 1) * span] = cut.astype(BF16)
            first = shard % 4 * 2 * span
            row = 1 if shard < 4 else 2
            pair = heads[row : row + 1, first : first + 2 * span]
            held[core, 1, level, layer : layer + 1, 0 : 2 * span] = pair.astype(BF16)
            start = shard * 4 * span
            held[core, 1, level, layer : layer + 1, 2 * span : 6 * span] = hidden[
                :, start : start + 4 * span
            ].astype(BF16)
            held[core, 2, level, 2 * layer : 2 * layer + 2, 0 : rel.shape[2]] = rel[
                shard
            ].astype(BF16)
    sink.send_all()
    sink.wait()


def pack_riders(plan, sums):
    resident = []
    width = sums[0][0].shape[1]
    for heads, hidden, rel in sums:
        resident += [heads, hidden, rel]
    return call(
        functools.partial(pack_kernel, plan), resident, Source(), [], [], 3,
        [plan.sink_outs((32, RIDERS, width))],
    )


class WholeSums:
    def __init__(self, plan):
        self.pairs = {}

    def add(self, name, pair):
        self.pairs[name] = pair

    def advance(self, *names):
        return ()

    def finish(self, sums, top):
        self.token = sums[0][0]
        big = [named(*whole_sums((self.pairs["attend"], self.pairs["mlp"]))), named(*top)]
        shards = lax.axis_size("fsdp")
        parts = []
        for heads, hidden, rel in sums:
            rel = rel.transpose(1, 0, 2).reshape(2, -1)
            rows = (
                jnp.concatenate([heads[1], heads[2]]), heads[0], heads[3], heads[4], heads[5],
                heads[6], hidden[0], heads[7], rel[0], rel[1],
            )
            parts.append([row.reshape(shards, -1) for row in rows])
        cuts = np.cumsum([0] + [part.shape[1] for part in parts[0]])
        small = jnp.stack([jnp.concatenate(rows, 1) for rows in parts])
        mine = whole_reduce(small.astype(BF16), 1).astype(F32)[:, 0]
        stacked = [
            jnp.stack([big[layer][i] for layer in range(LAYERS)]).astype(F32) for i in range(4)
        ]
        small = [mine[:, a:b] for a, b in zip(cuts, cuts[1:])]
        return (*stacked[:2], *small), stacked[2:]


def on_device(
    ring, windows, slot_table, cotangent, qkv_weight, qv_bias, proj_weight, proj_bias,
    norm1_gain, norm1_bias, norm2_gain, norm2_bias, fc1_weight, fc1_bias, fc2_weight, fc2_bias,
    rel_height, rel_width,
):
    width = windows.shape[1]
    weights = (qkv_weight, proj_weight, fc1_weight, fc2_weight)
    parts = (
        qv_bias, proj_bias, norm1_gain, norm1_bias, norm2_gain, norm2_bias, fc1_bias, fc2_bias,
        rel_height, rel_width,
    )
    cuts = np.cumsum([0] + [part.shape[1] for part in parts])
    if ring:
        plan = PiecePlan()
        pending = PieceSums(plan)
        held = PieceWeights(weights, jnp.concatenate(parts, 1).reshape(-1))
    else:
        plan = WholePlan()
        pending = WholeSums(plan)
        held = WholeWeights(weights, parts)
    small = held.small
    (
        qv_bias_w, proj_bias_w, norm1_gain_w, norm1_bias_w, norm2_gain_w, norm2_bias_w,
        fc1_bias_w, fc2_bias_w, rel_height_w, rel_width_w,
    ) = [
        small[:, :, a:b].transpose(1, 0, 2).reshape(LAYERS, -1) for a, b in zip(cuts, cuts[1:])
    ]
    vec = jnp.stack(
        [norm1_gain_w, norm1_bias_w, qv_bias_w[:, :width], qv_bias_w[:, width:], proj_bias_w,
         norm2_gain_w, norm2_bias_w, fc2_bias_w], 1
    ).astype(F32)
    hidden_bias = fc1_bias_w.astype(F32)[:, None, :]
    ahead, back = relative_tables(rel_height_w, rel_width_w)
    keys_ahead, keys_back = key_tables()
    live = live_rows(slot_table)
    current = spread(windows)
    grad = spread(cotangent)
    whole = WholePlan()
    kept = []
    for layer in range(LAYERS):
        top = layer == LAYERS - 1
        after = held.before(f"attend_{layer}")
        if layer == 0:
            after = (*after, back)
        mid, h1, q, k, v, p, att, token = attend_forward(
            current, live, vec[layer], ahead[layer], keys_ahead, held.source(layer, "attend"),
            after,
        )
        held.passed(f"attend_{layer}", token)
        used = ("fc1",) if top else ("fc1", "fc2")
        after = held.before(f"mlp_{layer}")
        made = mlp_forward(
            whole, top, mid, live, vec[layer], hidden_bias[layer], grad,
            held.source(layer, *used), after,
        )
        following = None
        if top:
            h2, act, slope, top_sums, top_g2 = made
        else:
            following, h2, act, slope = made
        kept.append((current, mid, h1, q, k, v, p, att, h2, act, slope))
        current = following
    sums = [None] * LAYERS
    steps = {"scores_0": ("mlp",), "first_0": ("mlp",)}

    def ahead_of(name):
        return pending.advance(*steps.get(name, ()))

    for layer in reversed(range(LAYERS)):
        top = layer == LAYERS - 1
        x, mid, h1, q, k, v, p, att, h2, act, slope = kept[layer]
        if top:
            dmid, sums2, hsum, top_g1 = top_backward(
                whole, grad, mid, live, vec[layer], h2, slope, held.source(layer, "fc1", "fc2"),
                (),
            )
            sums3 = top_sums
        else:
            dh, sums3, hsum, *pair = hidden_backward(
                plan, grad, act, live, h2, slope, held.source(layer, "fc2"), ()
            )
            pending.add("mlp", pair)
            dmid, sums2 = middle_backward(
                grad, mid, vec[layer], dh, held.source(layer, "fc1"), ()
            )
        db, dq, dk, dv, sums1, rel = scores_backward(
            dmid, live, back[layer], keys_back, q, k, v, p, held.source(layer, "proj"),
            ahead_of(f"scores_{layer}"),
        )
        if top:
            grad, sums4, top_g = first_all_backward(
                whole, dmid, x, live, vec[layer], h1, att, db, dq, dk, dv,
                held.source(layer, "attend"), (),
            )
            top_sum = whole_sums(((top_g,), (top_g2, top_g1)))
        else:
            pair = weights_backward(plan, h1, att, db, dq, dk, dv, ())
            pending.add("attend", pair)
            grad, sums4 = first_backward(
                dmid, x, live, vec[layer], dq, dk, dv, held.source(layer, "attend"),
                ahead_of("first_0"),
            )
        rel = rel[:, :HD] + rel[:, HD:]
        rel = jnp.stack([rel[:RELS].reshape(8, -1), rel[HD : HD + RELS].reshape(8, -1)], 1)
        sums[layer] = (sums1 + sums2 + sums3 + sums4, hsum, rel)
    input_grad = gather_back(grad).astype(BF16)
    (qkv_grad, proj_grad, *small), (fc1_grad, fc2_grad) = pending.finish(sums, top_sum)
    output = gather_back(
        mlp_output(
            kept[-1][9], vec[-1], kept[-1][1], live, held.source(LAYERS - 1, "fc2"),
            (pending.token.reshape(1, -1),),
        )
    ).astype(BF16)
    qv, pb, n1g, n1b, n2g, n2b, f1b, f2b, rh, rw = small
    return (
        output, input_grad, qkv_grad, qv, proj_grad, pb, n1g, n1b, n2g, n2b, fc1_grad, f1b,
        fc2_grad, f2b, rh, rw,
    )


def solution(mesh):
    rows = P(("rep", "fsdp"), None)
    cube = P(None, "fsdp", None)
    flat = P(None, "fsdp")
    ring = mesh.shape["rep"] == 4 and mesh.shape["fsdp"] == 8
    return jax.shard_map(
        functools.partial(on_device, ring),
        mesh=mesh,
        in_specs=(
            rows, P(("rep", "fsdp")), rows, cube, flat, cube, flat, flat, flat, flat, flat, cube,
            flat, cube, flat, flat, flat,
        ),
        out_specs=(
            rows, rows, cube, flat, cube, flat, flat, flat, flat, flat, cube, flat, cube, flat,
            flat, flat,
        ),
        check_vma=False,
    )
```

time: 616 us -> 489 us (0.79)
  other arithmetic: 82.3 us -> 33.4 us
  Pallas kernels: 227 us -> 198 us
  local copies, waits for them, and re-layouts: 58.4 us -> 32.6 us
  starting transfers between devices: 56.9 us -> 44.1 us
  waiting for transfers between devices: 163 us -> 155 us
    another operation x49 -> x5, other arithmetic: 41.5 us -> 3.47 us
    pallas_call x15 -> x16, Pallas kernels: 227 us -> 198 us  [call(): return run(*resident, *source.arrays, *after)]
    psum x0 -> x1, waiting for transfers between devices: none -> 18.5 us  [whole_reduce(): lax.psum(lax.psum_scatter(value, 'fsdp', scatter_dimension=axis, tiled=Tr...]
    ppermute x66 -> x48, waiting for transfers between devices: 152 us -> 136 us  [permute(): lax.ppermute(value, axis, [(i, move(i)) for i in range({'rep': 4, 'fsdp':...]
    ppermute x66 -> x48, starting transfers between devices: 56.6 us -> 43.4 us  [permute(): lax.ppermute(value, axis, [(i, move(i)) for i in range({'rep': 4, 'fsdp':...]
    convert_element_type x3 -> x8, other arithmetic: 2.11 us -> 14.3 us  [the longest x2 4.54 us: advance(): send_y = self.both(slice(2, 4), high).astype(BF16)]
    slice x27 -> x11, local copies, waits for them, and re-layouts: 18.2 us -> 6.74 us  [the longest x2 2.23 us: cross(): low, high = (self.y[:2], self.x[2:])]
    all_gather x5 -> x3, waiting for transfers between devices: 10.3 us -> 0.02 us  [the longest x1 0.02 us: __init__(): lax.all_gather(weights[3][1] + nothing(self.fc1[0, 0]), 'fsdp', axis=0, t...]
  transfers between devices with their start and end apart: 73 -> 55, of which waited for: 29 -> 22; matrix products, arithmetic and copies ran while one was open for 20% -> 12% of each run, Pallas kernels for 33% -> 40%
where the time goes in v3:
time: 489 us; the launch traced here: 481 us
  Pallas kernels  198 us (40%)
  waiting for transfers between devices  155 us (32%)
  starting transfers between devices  44.1 us (9%)
  other arithmetic  33.4 us (7%)
  local copies, waits for them, and re-layouts  32.6 us (7%)
  between operations  18.3 us (4%)
    pallas_call x16, Pallas kernels, call(): return run(*resident, *source.arrays, *after)  198 us
    ppermute x48, waiting for transfers between devices, permute(): lax.ppermute(value, axis, [(i, move(i)) for i in range({'rep': 4, 'fsdp':...  136 us
    ppermute x48, starting transfers between devices, permute(): lax.ppermute(value, axis, [(i, move(i)) for i in range({'rep': 4, 'fsdp':...  43.4 us
    psum x1, waiting for transfers between devices, whole_reduce(): lax.psum(lax.psum_scatter(value, 'fsdp', scatter_dimension=axis, tiled=Tr...  18.5 us
  transfers between devices with their start and end apart: 55, of which 22 were waited for; matrix products, arithmetic and copies ran while one was open for 12% of the time, Pallas kernels for 40%

profile of v3, /device:TPU:8, one launch (start us, length us, event | category | flops | bytes accessed | tf_op | source)
XLA Modules:
  0.0 481.2 jit_solution(16446153183240340428)
XLA Ops:
  11.7 8.0 %collective-permute-done.2 = bf16[1,200,768]{2,1,0:T(8,128)(2,1)S(1)} collective-permute-done((bf16[1,200,768]{2,1,0:T(8,128)(2,1)S(1)}, bf16[1,200,768]{2,1,0:T(8,128)(2,1)S(1)}, u32[]{:S(2)}, u32[]{:S(2)}) %collective-permute-start.2) | collective-permute-done | bytes 307232 | tf_op jit(solution)/shard_map/ppermute | solution.py:1028
  26.2 16.9 %collective-permute-done.1 = bf16[1,200,768]{2,1,0:T(8,128)(2,1)S(1)} collective-permute-done((bf16[1,200,768]{2,1,0:T(8,128)(2,1)S(1)}, bf16[1,200,768]{2,1,0:T(8,128)(2,1)S(1)}, u32[]{:S(2)}, u32[]{:S(2)}) %collective-permute-start.1) | collective-permute-done | bytes 307232 | tf_op jit(solution)/shard_map/ppermute | solution.py:1028
  43.1 18.6 %collective-permute-done = bf16[1,200,768]{2,1,0:T(8,128)(2,1)S(1)} collective-permute-done((bf16[1,200,768]{2,1,0:T(8,128)(2,1)S(1)}, bf16[1,200,768]{2,1,0:T(8,128)(2,1)S(1)}, u32[]{:S(2)}, u32[]{:S(2)}) %collective-permute-start) | collective-permute-done | bytes 307232 | tf_op jit(solution)/shard_map/ppermute | solution.py:1028
  71.0 21.6 %collective-permute-done.4.refs_6_.refs_5_.refs_9_.refs_8_ = bf16[4,200,768]{2,1,0:T(8,128)(2,1)} collective-permute-done((bf16[4,200,768]{2,1,0:T(8,128)(2,1)S(1)}, bf16[4,200,768]{2,1,0:T(8,128)(2,1)}, u32[]{:S(2)}, u32[]{:S(2)}) %collective-permute-start.4) | collective-permute-done | bytes 1228832 | tf_op jit(solution)/shard_map/ppermute | solution.py:1028
  100.0 10.1 %collective-permute-done.8.refs_8_.refs_7_.refs_11_.refs_10_ = bf16[2,200,768]{2,1,0:T(8,128)(2,1)S(1)} collective-permute-done((bf16[2,200,768]{2,1,0:T(8,128)(2,1)S(1)}, bf16[2,200,768]{2,1,0:T(8,128)(2,1)S(1)}, u32[]{:S(2)}, u32[]{:S(2)}) %collective-permute-start.8) | collective-permute-done | bytes 614432 | tf_op jit(solution)/shard_map/ppermute | solution.py:1028
  124.9 17.4 %shard_map.306 = (f32[448,768]{1,0:T(8,128)}, bf16[448,768]{1,0:T(8,128)(2,1)}, bf16[448,768]{1,0:T(8,128)(2,1)}, bf16[448,768]{1,0:T(8,128)(2,1)}, bf16[448,768...) custom-call(bf16[448,768]{1,0:T(8,128)(2,1)} %bitcast.152, ...), custom_call_target="tpu_custom_call" | custom-call | flops 20000000000 | bytes 1048576 | tf_op jit(solution)/shard_map/pallas_call | solution.py:815
  148.5 11.2 %collective-permute-done.14.refs_17_.refs_8_.refs_11_.refs_13_ = bf16[2,192,768]{2,1,0:T(8,128)(2,1)S(1)} collective-permute-done((bf16[2,192,768]{2,1,0:T(8,128)(2,1)S(1)}, bf16[2,192,768]{2,1,0:T(8,128)(2,1)S(1)}, u32[]{:S(2)}, u32[]{:S(2)}) %collective-permute-start.14) | collective-permute-done | bytes 589856 | tf_op jit(solution)/shard_map/ppermute | solution.py:1028
  165.1 14.8 %shard_map.307 = (f32[448,768]{1,0:T(8,128)}, bf16[448,768]{1,0:T(8,128)(2,1)}, bf16[448,3072]{1,0:T(8,128)(2,1)}, bf16[448,3072]{1,0:T(8,128)(2,1)}) custom-call(f32[448,768]{1,0:T(8,128)} %get-tuple-element.86.refs_0_.refs_1_, f32[448,1]{1,0:T(8,128)} %reshape.318.refs_1_.refs_2_.refs_3_, f32[8,768]{1,0:T(8,128)} %get-tuple-element.208.refs_2_.refs_3_, ...), custom_call_target="tpu_custom_call" | custom-call | flops 16000000000 | bytes 1048576 | tf_op jit(solution)/shard_map/pallas_call | solution.py:815
  179.9 17.8 %shard_map.308 = (f32[448,768]{1,0:T(8,128)}, bf16[448,768]{1,0:T(8,128)(2,1)}, bf16[448,768]{1,0:T(8,128)(2,1)}, bf16[448,768]{1,0:T(8,128)(2,1)}, bf16[448,768...) custom-call(f32[448,768]{1,0:T(8,128)} %get-tuple-element.88.refs_0_.refs_1_, ...), custom_call_target="tpu_custom_call" | custom-call | flops 20000000000 | bytes 1048576 | tf_op jit(solution)/shard_map/pallas_call | solution.py:815
  197.8 16.0 %shard_map.309 = (bf16[448,768]{1,0:T(8,128)(2,1)}, bf16[448,3072]{1,0:T(8,128)(2,1)}, bf16[448,3072]{1,0:T(8,128)(2,1)}, f32[8,768]{1,0:T(8,128)}, bf16[3072,768]{1,0:T(8,128)(2,1)}) custom-call(f32[448,768]{1,0:T(8,128)} %get-tuple-element.89.refs_0_.refs_1_.refs_2_, f32[448,1]{1,0:T(8,128)} %reshape.318.refs_1_.refs_2_.refs_3_, ...), custom_call_target="tpu_custom_call" | custom-call | flops 16000000000 | bytes 1048576 | tf_op jit(solution)/shard_map/pallas_call | solution.py:815
  213.9 19.5 %shard_map.310 = (f32[448,768]{1,0:T(8,128)}, f32[8,768]{1,0:T(8,128)}, f32[1,3072]{1,0:T(1,128)}, bf16[4,768,768]{2,1,0:T(8,128)(2,1)}) custom-call(bf16[448,768]{1,0:T(8,128)(2,1)} %bitcast.155, f32[448,768]{1,0:T(8,128)} %get-tuple-element.89.refs_0_.refs_1_.refs_2_, f32[448,1]{1,0:T(8,128)} %reshape.318.refs_1_.refs_2_.refs_3_, ...), custom_call_target="tpu_custom_call" | custom-call | flops 19000000512 | bytes 1048576 | tf_op jit(solution)/shard_map/pallas_call | solution.py:815
  235.0 15.5 %shard_map.311 = (bf16[448,768]{1,0:T(8,128)(2,1)}, bf16[448,768]{1,0:T(8,128)(2,1)}, bf16[448,768]{1,0:T(8,128)(2,1)}, bf16[448,768]{1,0:T(8,128)(2,1)}, f32[8,768]{1,0:T(8,128)}, /*index=5*/f32[128,128]{1,0:T(8,128)}) custom-call(f32[448,768]{1,0:T(8,128)} %get-tuple-element.95.refs_0_, f32[448,1]{1,0:T(8,128)} %reshape.318.refs_1_.refs_2_.refs_3_, ...), custom_call_target="tpu_custom_call" | custom-call | flops 15000000512 | bytes 1048576 | tf_op jit(solution)/shard_map/pallas_call | solution.py:815
  250.5 15.7 %shard_map.312 = (f32[448,768]{1,0:T(8,128)}, f32[8,768]{1,0:T(8,128)}, bf16[4,768,768]{2,1,0:T(8,128)(2,1)}) custom-call(f32[448,768]{1,0:T(8,128)} %get-tuple-element.95.refs_0_, f32[448,768]{1,0:T(8,128)} %get-tuple-element.88.refs_0_.refs_1_, f32[448,1]{1,0:T(8,128)} %reshape.318.refs_1_.refs_2_.refs_3_, ...), custom_call_target="tpu_custom_call" | custom-call | flops 14000000000 | bytes 1048576 | tf_op jit(solution)/shard_map/pallas_call | solution.py:815
  266.3 17.7 %shard_map.313 = (bf16[448,3072]{1,0:T(8,128)(2,1)}, f32[8,768]{1,0:T(8,128)}, f32[1,3072]{1,0:T(1,128)}, bf16[4,4,192,768]{3,2,1,0:T(8,128)(2,1)}, bf16[4,4,192,768]{3,2,1,0:T(8,128)(2,1)}) custom-call(f32[448,768]{1,0:T(8,128)} %get-tuple-element.106.refs_0_, bf16[448,3072]{1,0:T(8,128)(2,1)} %get-tuple-element.107.refs_1_, ...), custom_call_target="tpu_custom_call" | custom-call | flops 17999998976 | bytes 1048576 | tf_op jit(solution)/shard_map/pallas_call | solution.py:815
  286.6 12.0 %shard_map.314 = (f32[448,768]{1,0:T(8,128)}, f32[8,768]{1,0:T(8,128)}) custom-call(f32[448,768]{1,0:T(8,128)} %get-tuple-element.106.refs_0_, f32[448,768]{1,0:T(8,128)} %get-tuple-element.86.refs_0_.refs_1_, f32[8,768]{1,0:T(8,128)} %get-tuple-element.208.refs_2_.refs_3_, bf16[448,3072]{1,0:T(8,128)(2,1)} %get-tuple-element.110.refs_3_, ...), custom_call_target="tpu_custom_call" | custom-call | flops 10000000000 | bytes 1048576 | tf_op jit(solution)/shard_map/pallas_call | solution.py:815
  302.9 15.4 %shard_map.315 = (bf16[448,768]{1,0:T(8,128)(2,1)}, bf16[448,768]{1,0:T(8,128)(2,1)}, bf16[448,768]{1,0:T(8,128)(2,1)}, bf16[448,768]{1,0:T(8,128)(2,1)}, f32[8,768]{1,0:T(8,128)}, /*index=5*/f32[128,128]{1,0:T(8,128)}) custom-call(f32[448,768]{1,0:T(8,128)} %get-tuple-element.111.refs_0_, f32[448,1]{1,0:T(8,128)} %reshape.318.refs_1_.refs_2_.refs_3_, ...), custom_call_target="tpu_custom_call" | custom-call | flops 15000000512 | bytes 1048576 | tf_op jit(solution)/shard_map/pallas_call | solution.py:815
  322.0 7.2 %shard_map.316 = (bf16[4,4,96,768]{3,2,1,0:T(8,128)(2,1)}, bf16[4,4,96,768]{3,2,1,0:T(8,128)(2,1)}) custom-call(bf16[448,768]{1,0:T(8,128)(2,1)} %get-tuple-element.91.refs_0_, bf16[448,768]{1,0:T(8,128)(2,1)} %get-tuple-element.92.refs_1_, bf16[448,768]{1,0:T(8,128)(2,1)} %get-tuple-element.118.refs_2_, ...), custom_call_target="tpu_custom_call" | custom-call | flops 8000000000 | bytes 1048576 | tf_op jit(solution)/shard_map/pallas_call | solution.py:815
  334.3 10.9 %shard_map.318 = (f32[448,768]{1,0:T(8,128)}, f32[8,768]{1,0:T(8,128)}) custom-call(f32[448,768]{1,0:T(8,128)} %get-tuple-element.111.refs_0_, bf16[448,768]{1,0:T(8,128)(2,1)} %bitcast.153, f32[448,1]{1,0:T(8,128)} %reshape.318.refs_1_.refs_2_.refs_3_, f32[8,768]{1,0:T(8,128)} %get-tuple-element.208.refs_2_.refs_3_, ...), custom_call_target="tpu_custom_call" | custom-call | flops 10000000000 | bytes 1048576 | tf_op jit(solution)/shard_map/pallas_call | solution.py:815
  362.6 8.0 %collective-permute-done.29 = bf16[2,8,768]{2,1,0:T(8,128)(2,1)S(1)} collective-permute-done((bf16[2,8,768]{2,1,0:T(8,128)(2,1)S(1)}, bf16[2,8,768]{2,1,0:T(8,128)(2,1)S(1)}, u32[]{:S(2)}, u32[]{:S(2)}) %collective-permute-start.29) | collective-permute-done | bytes 24608 | tf_op jit(solution)/shard_map/ppermute | solution.py:1028
  377.0 5.1 %collective-permute-done.31 = bf16[2,2,96,768]{3,2,1,0:T(8,128)(2,1)} collective-permute-done((bf16[2,2,96,768]{3,2,1,0:T(8,128)(2,1)}, bf16[2,2,96,768]{3,2,1,0:T(8,128)(2,1)}, u32[]{:S(2)}, u32[]{:S(2)}) %collective-permute-start.31) | collective-permute-done | bytes 589856 | tf_op jit(solution)/shard_map/ppermute | solution.py:1028
  402.5 15.5 %collective-permute-done.41 = bf16[192,768]{1,0:T(8,128)(2,1)S(1)} collective-permute-done((bf16[192,768]{1,0:T(8,128)(2,1)S(1)}, bf16[192,768]{1,0:T(8,128)(2,1)S(1)}, u32[]{:S(2)}, u32[]{:S(2)}) %collective-permute-start.41) | collective-permute-done | bytes 294944 | tf_op jit(solution)/shard_map/ppermute | solution.py:1028
  418.0 6.3 %collective-permute-done.43 = bf16[192,768]{1,0:T(8,128)(2,1)S(1)} collective-permute-done((bf16[192,768]{1,0:T(8,128)(2,1)S(1)}, bf16[192,768]{1,0:T(8,128)(2,1)S(1)}, u32[]{:S(2)}, u32[]{:S(2)}) %collective-permute-start.43) | collective-permute-done | bytes 294944 | tf_op jit(solution)/shard_map/ppermute | solution.py:1028
  432.4 9.0 %shard_map.317 = f32[448,768]{1,0:T(8,128)} custom-call(bf16[448,3072]{1,0:T(8,128)(2,1)} %get-tuple-element.90.refs_0_, f32[8,768]{1,0:T(8,128)} %get-tuple-element.207.refs_2_.refs_3_.refs_1_, f32[448,768]{1,0:T(8,128)} %get-tuple-element.89.refs_0_.refs_1_.refs_2_, f32[448,1]{1,0:T(8,128)} %reshape.318.refs_1_.refs_2_.refs_3_, ...), custom_call_target="tpu_custom_call" | custom-call | flops 5000000000 | bytes 1048576 | tf_op jit(solution)/shard_map/pallas_call | solution.py:815
  447.2 18.5 %all-reduce.12.cloned.1.call-done = (bf16[4,96,768]{2,1,0:T(8,128)(2,1)}, bf16[4,96,768]{2,1,0:T(8,128)(2,1)}, bf16[384,768]{1,0:T(8,128)(2,1)}) async-done(((bf16[4,96,768]{2,1,0:T(8,128)(2,1)}, bf16[4,96,768]{2,1,0:T(8,128)(2,1)}, bf16[384,768]{1,0:T(8,128)(2,1)}), (bf16[4,96,768]{2,1,0:T(8,128)(2,1)}, bf16[4,96,768]{2,1,0:T(8,128)(2,1)}, bf16[384,768]{1,0:T(8,128)(2,1)})) %all-reduce.12.cloned.1.call-update) | async-done | bytes 1769488 | tf_op jit(solution)/shard_map/psum | solution.py:1015
  (344 shorter events, 134.2 us)
Async XLA Ops:
  7.2 58.8 %all-gather.6.cloned.1.call-start = ((), (), s32[]{:S(2)}) async-start(), calls=%async_computation.3 | async-start | bytes 1474560 | tf_op jit(solution)/shard_map/all_gather | solution.py:1119
  21.7 100.2 %all-gather.8.cloned.1.call-start = ((), (), s32[]{:S(2)}) async-start(), calls=%async_computation.7 | async-start | bytes 5308416 | tf_op jit(solution)/shard_map/all_gather | solution.py:1123
  26.2 35.5 %collective-permute-start = (bf16[1,200,768]{2,1,0:T(8,128)(2,1)S(1)}, bf16[1,200,768]{2,1,0:T(8,128)(2,1)S(1)}, u32[]{:S(2)}, u32[]{:S(2)}) collective-permute-start(bf16[1,200,768]{2,1,0:T(8,128)(2,1)S(1)} %maximum_bitcast_fusion), channel_id=1, source_target_pairs={{0,2},{1,3},{2,4},{3,5},{4,6},{5,7},{6,0},{7,1},{8,10},{9,11},{10,... | collective-permute-start | bytes 921608 | tf_op jit(solution)/shard_map/ppermute | solution.py:1028
  62.9 29.8 %collective-permute-start.6 = (bf16[4,200,768]{2,1,0:T(8,128)(2,1)S(1)}, bf16[4,200,768]{2,1,0:T(8,128)(2,1)}, u32[]{:S(2)}, u32[]{:S(2)}) collective-permute-start(bf16[4,200,768]{2,1,0:T(8,128)(2,1)S(1)} %pad_maximum_fusion.refs_5_.refs_4_.refs_8_.refs_7_), channel_id=1, source_target_pairs={{0,16},{8,24},{16,0},{24,8},{1,17},{9,25},{17,1},{25,9},{2,18},{10... | collective-permute-start | bytes 3686408 | tf_op jit(solution)/shard_map/ppermute | solution.py:1028
  64.5 28.1 %collective-permute-start.4 = (bf16[4,200,768]{2,1,0:T(8,128)(2,1)S(1)}, bf16[4,200,768]{2,1,0:T(8,128)(2,1)}, u32[]{:S(2)}, u32[]{:S(2)}) collective-permute-start(bf16[4,200,768]{2,1,0:T(8,128)(2,1)S(1)} %pad_maximum_fusion.refs_5_.refs_4_.refs_8_.refs_7_), channel_id=1, source_target_pairs={{0,8},{8,0},{16,24},{24,16},{1,9},{9,1},{17,25},{25,17},{2,10},{10... | collective-permute-start | bytes 3686408 | tf_op jit(solution)/shard_map/ppermute | solution.py:1028
  68.7 145.2 %all-gather.10.cloned.1.call-start = ((), (), s32[]{:S(2)}) async-start(), calls=%async_computation.8 | async-start | bytes 5308416 | tf_op jit(solution)/shard_map/all_gather | solution.py:1126
  68.9 29.7 %collective-permute-start.3 = (bf16[4,200,768]{2,1,0:T(8,128)(2,1)S(1)}, bf16[4,200,768]{2,1,0:T(8,128)(2,1)}, u32[]{:S(2)}, u32[]{:S(2)}) collective-permute-start(bf16[4,200,768]{2,1,0:T(8,128)(2,1)S(1)} %pad_maximum_fusion.refs_5_.refs_4_.refs_8_.refs_7_), channel_id=1, source_target_pairs={{0,1},{1,0},{2,3},{3,2},{4,5},{5,4},{6,7},{7,6},{8,9},{9,8},{10,11... | collective-permute-start | bytes 3686408 | tf_op jit(solution)/shard_map/ppermute | solution.py:1028
  99.5 65.1 %collective-permute-start.16 = (bf16[4,192,768]{2,1,0:T(8,128)(2,1)}, bf16[4,192,768]{2,1,0:T(8,128)(2,1)}, u32[]{:S(2)}, u32[]{:S(2)}) collective-permute-start(bf16[4,192,768]{2,1,0:T(8,128)(2,1)} %bitcast.27.refs_15_.refs_14_.refs_5_.refs_8_.refs_10_), channel_id=1, source_target_pairs={{0,1},{1,0},{2,3},{3,2},{4,5},{5,4},{6,7},{7,6},{8,9},{9,8},{10,11... | collective-permute-start | bytes 3538952 | tf_op jit(solution)/shard_map/ppermute | solution.py:1028
  110.1 33.5 %collective-permute-start.13 = (bf16[4,192,768]{2,1,0:T(8,128)(2,1)}, bf16[4,192,768]{2,1,0:T(8,128)(2,1)S(1)}, u32[]{:S(2)}, u32[]{:S(2)}) collective-permute-start(bf16[4,192,768]{2,1,0:T(8,128)(2,1)} %bitcast.27.refs_15_.refs_14_.refs_5_.refs_8_.refs_10_), channel_id=1, source_target_pairs={{0,16},{8,24},{16,0},{24,8},{1,17},{9,25},{17,1},{25,9},{2,18},{10... | collective-permute-start | bytes 3538952 | tf_op jit(solution)/shard_map/ppermute | solution.py:1028
  114.4 31.3 %collective-permute-start.12 = (bf16[4,192,768]{2,1,0:T(8,128)(2,1)}, bf16[4,192,768]{2,1,0:T(8,128)(2,1)}, u32[]{:S(2)}, u32[]{:S(2)}) collective-permute-start(bf16[4,192,768]{2,1,0:T(8,128)(2,1)} %bitcast.27.refs_15_.refs_14_.refs_5_.refs_8_.refs_10_), channel_id=1, source_target_pairs={{0,8},{8,0},{16,24},{24,16},{1,9},{9,1},{17,25},{25,17},{2,10},{10... | collective-permute-start | bytes 3538952 | tf_op jit(solution)/shard_map/ppermute | solution.py:1028
  124.6 263.9 %reduce-scatter.8.cloned.1.call-start = ((), (), s32[]{:S(2)}) async-start(), calls=%async_computation.6 | async-start | bytes 5308416 | tf_op jit(solution)/shard_map/reduce_scatter | solution.py:1015
  213.8 174.7 %reduce-scatter.6.cloned.1.call-start = ((), (), s32[]{:S(2)}) async-start(), calls=%async_computation.5 | async-start | bytes 5308416 | tf_op jit(solution)/shard_map/reduce_scatter | solution.py:1015
  233.5 155.1 %reduce-scatter.4.cloned.1.call-start = ((), (), s32[]{:S(2)}) async-start(), calls=%async_computation.4 | async-start | bytes 5308416 | tf_op jit(solution)/shard_map/reduce_scatter | solution.py:1015
  284.2 181.5 %all-reduce.12.cloned.1.call-start = ((), (), s32[]{:S(2)}) async-start(), calls=%async_computation.9 | async-start | bytes 3538944 | tf_op jit(solution)/shard_map/psum | solution.py:1015
  301.8 28.4 %collective-permute-start.25 = (bf16[2,2,192,768]{3,2,1,0:T(8,128)(2,1)}, bf16[2,2,192,768]{3,2,1,0:T(8,128)(2,1)S(1)}, u32[]{:S(2)}, u32[]{:S(2)}) collective-permute-start(bf16[2,2,192,768]{3,2,1,0:T(8,128)(2,1)} %get-tuple-element.165.refs_19_), channel_id=1, source_target_pairs={{0,16},{8,24},{16,0},{24,8},{1,17},{9,25},{17,1},{25,9},{2,18},{10... | collective-permute-start | bytes 3538952 | tf_op jit(solution)/shard_map/ppermute | solution.py:1028
  301.9 28.4 %collective-permute-start.26 = (bf16[2,2,192,768]{3,2,1,0:T(8,128)(2,1)S(1)}, bf16[2,2,192,768]{3,2,1,0:T(8,128)(2,1)S(1)}, u32[]{:S(2)}, u32[]{:S(2)}) collective-permute-start(bf16[2,2,192,768]{3,2,1,0:T(8,128)(2,1)S(1)} %get-tuple-element.166.refs_18_), channel_id=1, source_target_pairs={{0,8},{8,0},{16,24},{24,16},{1,9},{9,1},{17,25},{25,17},{2,10},{10... | collective-permute-start | bytes 3538952 | tf_op jit(solution)/shard_map/ppermute | solution.py:1028
  329.2 30.8 %collective-permute-start.22 = (bf16[4,4,96,768]{3,2,1,0:T(8,128)(2,1)}, bf16[4,4,96,768]{3,2,1,0:T(8,128)(2,1)S(1)}, u32[]{:S(2)}, u32[]{:S(2)}) collective-permute-start(bf16[4,4,96,768]{3,2,1,0:T(8,128)(2,1)} %get-tuple-element.123), channel_id=1, source_target_pairs={{0,1},{1,0},{2,3},{3,2},{4,5},{5,4},{6,7},{7,6},{8,9},{9,8},{10,11... | collective-permute-start | bytes 7077896 | tf_op jit(solution)/shard_map/ppermute | solution.py:1028
  388.6 29.4 %collective-permute-start.41 = (bf16[192,768]{1,0:T(8,128)(2,1)S(1)}, bf16[192,768]{1,0:T(8,128)(2,1)S(1)}, u32[]{:S(2)}, u32[]{:S(2)}) collective-permute-start(bf16[192,768]{1,0:T(8,128)(2,1)S(1)} %slice_bitcast_fusion.4), channel_id=1, source_target_pairs={{0,2},{1,3},{2,4},{3,5},{4,6},{5,7},{6,0},{7,1},{8,10},{9,11},{10,... | collective-permute-start | bytes 884744 | tf_op jit(solution)/shard_map/ppermute | solution.py:1028
  392.7 31.7 %collective-permute-start.43 = (bf16[192,768]{1,0:T(8,128)(2,1)S(1)}, bf16[192,768]{1,0:T(8,128)(2,1)S(1)}, u32[]{:S(2)}, u32[]{:S(2)}) collective-permute-start(bf16[192,768]{1,0:T(8,128)(2,1)S(1)} %get-tuple-element.175), channel_id=1, source_target_pairs={{0,4},{1,5},{2,6},{3,7},{4,0},{5,1},{6,2},{7,3},{8,12},{9,13},{10,... | collective-permute-start | bytes 884744 | tf_op jit(solution)/shard_map/ppermute | solution.py:1028
  392.8 31.6 %collective-permute-start.44 = (bf16[192,768]{1,0:T(8,128)(2,1)S(1)}, bf16[192,768]{1,0:T(8,128)(2,1)S(1)}, u32[]{:S(2)}, u32[]{:S(2)}) collective-permute-start(bf16[192,768]{1,0:T(8,128)(2,1)S(1)} %get-tuple-element.176), channel_id=1, source_target_pairs={{0,6},{1,7},{2,0},{3,1},{4,2},{5,3},{6,4},{7,5},{8,14},{9,15},{10,... | collective-permute-start | bytes 884744 | tf_op jit(solution)/shard_map/ppermute | solution.py:1028
  398.1 29.0 %collective-permute-start.30 = (bf16[104,768]{1,0:T(8,128)(2,1)S(1)}, bf16[104,768]{1,0:T(8,128)(2,1)S(1)}, u32[]{:S(2)}, u32[]{:S(2)}) collective-permute-start(bf16[104,768]{1,0:T(8,128)(2,1)S(1)} %fusion.24), channel_id=1, source_target_pairs={{0,2},{1,3},{2,4},{3,5},{4,6},{5,7},{6,0},{7,1},{8,10},{9,11},{10,... | collective-permute-start | bytes 479240 | tf_op jit(solution)/shard_map/ppermute | solution.py:1028
  401.4 27.4 %collective-permute-start.35 = (bf16[104,768]{1,0:T(8,128)(2,1)S(1)}, bf16[104,768]{1,0:T(8,128)(2,1)S(1)}, u32[]{:S(2)}, u32[]{:S(2)}) collective-permute-start(bf16[104,768]{1,0:T(8,128)(2,1)S(1)} %get-tuple-element.183), channel_id=1, source_target_pairs={{0,4},{1,5},{2,6},{3,7},{4,0},{5,1},{6,2},{7,3},{8,12},{9,13},{10,... | collective-permute-start | bytes 479240 | tf_op jit(solution)/shard_map/ppermute | solution.py:1028
  424.5 44.6 %collective-permute-start.47 = (bf16[192,768]{1,0:T(8,128)(2,1)S(1)}, bf16[192,768]{1,0:T(8,128)(2,1)S(1)}, u32[]{:S(2)}, u32[]{:S(2)}) collective-permute-start(bf16[192,768]{1,0:T(8,128)(2,1)S(1)} %fusion.14.refs_2_), channel_id=1, source_target_pairs={{0,24},{8,16},{16,8},{24,0},{1,25},{9,17},{17,9},{25,1},{2,26},{10... | collective-permute-start | bytes 884744 | tf_op jit(solution)/shard_map/ppermute | solution.py:1028
  425.0 44.1 %collective-permute-start.46 = (bf16[192,768]{1,0:T(8,128)(2,1)S(1)}, bf16[192,768]{1,0:T(8,128)(2,1)S(1)}, u32[]{:S(2)}, u32[]{:S(2)}) collective-permute-start(bf16[192,768]{1,0:T(8,128)(2,1)S(1)} %fusion.14.refs_2_), channel_id=1, source_target_pairs={{0,16},{8,24},{16,0},{24,8},{1,17},{9,25},{17,1},{25,9},{2,18},{10... | collective-permute-start | bytes 884744 | tf_op jit(solution)/shard_map/ppermute | solution.py:1028
  (76 other events, 785.6 us)
Sparse Core Ops, SparseCore 0:
  21.8 42.2 all-gather.5
  68.9 49.3 all-gather.7
  124.8 50.8 all-gather.9
  214.0 51.7 reduce-scatter.7
  267.9 53.2 reduce-scatter.5
  323.4 53.3 reduce-scatter.3
  388.7 76.9 all-reduce.11

commit v4 on v3

--- a/solution.py
+++ b/solution.py
@@ -809,7 +809,7 @@
         scratch_shapes=[*buffers, *semaphores, *scratch, *sink_scratch],
         compiler_params=pltpu.CompilerParams(vmem_limit_bytes=VMEM_LIMIT),
         cost_estimate=pl.CostEstimate(
-            flops=int(micros * 1e9), bytes_accessed=1 << 20, transcendentals=0
+            flops=int(micros * 1e10), bytes_accessed=1 << 20, transcendentals=0
         ),
     )
     return run(*resident, *source.arrays, *after)
@@ -1117,15 +1117,13 @@
         self.span = span
         held = jnp.concatenate([first] + [to_level(first, step) for step in (1, 2, 3)], 0)
         self.rest = lax.all_gather(
-            jnp.concatenate([blocks[0][2], blocks[1][0]], 0) + nothing(held[3, 0, 0]), "fsdp",
+            jnp.concatenate([blocks[0][2], blocks[1][0]], 0) + nothing(jnp.max(jnp.abs(held[1:, 0, 0]))), "fsdp",
             axis=0, tiled=True, axis_index_groups=LEVELS,
         ).reshape(4, 2 * span, width)
         self.fc1 = lax.all_gather(
             weights[2][1] + nothing(self.rest[0, 0, 0]), "fsdp", axis=0, tiled=True
         )
-        self.fc2 = lax.all_gather(
-            weights[3][1] + nothing(self.fc1[0, 0]), "fsdp", axis=0, tiled=True
-        )
+        self.top = weights[3][1]
         one = Across(held)
         one.cross()
         self.one = one.finish()
@@ -1152,7 +1150,9 @@
 
     def passed(self, name, token):
         if name == "attend_0":
-            self.next.cross(token[0, 0].astype(BF16))
+            token = token[0, 0].astype(BF16)
+            self.next.cross(token)
+            self.fc2 = lax.all_gather(self.top + token, "fsdp", axis=0, tiled=True)
 
     def source(self, layer, *names):
         if layer == 0:
@@ -1198,17 +1198,17 @@
         ]
         return sums[0] if len(sums) == 1 else jnp.concatenate(sums, -2)
 
-    def advance(self):
+    def advance(self, hold=0):
         low, high = slice(0, 2), slice(2, 4)
         self.step += 1
         if self.step == 1:
-            send_x = self.both(slice(1, 4, 2), low).astype(BF16)
-            send_y = self.both(slice(2, 4), high).astype(BF16)
+            send_x = (self.both(slice(1, 4, 2), low) + hold).astype(BF16)
+            send_y = (self.both(slice(2, 4), high) + hold).astype(BF16)
             self.x, self.y = to_x(send_x), to_y(send_y)
             return [send_x, send_y]
         if self.step == 2:
-            send_y = (self.both(2, low) + self.x[1].astype(F32)).astype(BF16)
-            send_x = (self.both(1, high) + self.y[1].astype(F32)).astype(BF16)
+            send_y = (self.both(2, low) + self.x[1].astype(F32) + hold).astype(BF16)
+            send_x = (self.both(1, high) + self.y[1].astype(F32) + hold).astype(BF16)
             self.last_y, self.last_x = to_y(send_y), to_x(send_x)
             return [send_x, send_y]
         if self.step == 4:
@@ -1229,6 +1229,28 @@
         return self.result
 
 
+class ReplicaAll:
+    def __init__(self, *parts):
+        self.parts = list(parts)
+        self.moves = [to_x, to_y]
+        self.got = None
+
+    def advance(self, hold=0):
+        if self.got is not None:
+            self.add(hold)
+        else:
+            self.parts = [part + jnp.asarray(hold, BF16) for part in self.parts]
+        self.got = [move(part) for move, part in zip(self.moves, self.parts)]
+        return self.parts
+
+    def add(self, hold=0):
+        self.moves = self.moves[::-1]
+        self.parts = [
+            (part.astype(F32) + got.astype(F32) + hold).astype(BF16)
+            for part, got in zip(self.parts, self.got)
+        ]
+
+
 class PieceSums:
     def __init__(self, plan):
         self.plan = plan
@@ -1237,31 +1259,44 @@
     def add(self, name, pair):
         self.sums[name] = ReplicaSum(pair)
 
-    def advance(self, *names):
+    def add_top(self, g2, g1, g):
+        g2 = lax.psum_scatter(g2, "fsdp", scatter_dimension=0, tiled=True)
+        g1 = lax.psum_scatter(g1, "fsdp", scatter_dimension=1, tiled=True)
+        g = lax.psum_scatter(g, "fsdp", scatter_dimension=1, tiled=True)
+        half = g2.shape[0] // 2
+        self.sums["top"] = ReplicaAll(g2[:half], g2[half:])
+        self.sums["next"] = ReplicaAll(g1, g)
+
+    def advance(self, hold, *names):
         found = []
         for name in names:
-            found += self.sums[name].advance()
+            found += self.sums[name].advance(hold)
         return found
 
-    def finish(self, sums, top):
-        last = self.sums["attend"]
-        riders = ReplicaSum(pack_riders(self.plan, sums))
-        span, width = last.pairs[0][0].shape[2:]
+    def finish(self, sums):
+        last, mlp, top, following = (
+            self.sums[name] for name in ("attend", "mlp", "top", "next")
+        )
+        riders = ReplicaSum(pack_riders(self.plan, sums, mlp.advance()))
         last.advance()
         for _ in range(3):
             riders.advance()
-        self.advance("mlp", "mlp", "mlp")
-        last.advance()
+        mlp.advance()
+        mlp.advance()
+        crossed = last.advance()[0]
         last.advance()
         first = last.result[0][0, 0, 0]
         last.result = [jnp.concatenate(pair, 1) for pair in zip(last.result, riders.result)]
         last.advance()
-        late = to_replicas(self.sums["mlp"].total + nothing(first))
+        following.advance(nothing(crossed[0, 0, 0]))
+        late = to_replicas(mlp.total + nothing(first))
         last.advance()
-        self.token = first
-        g, g1, g2 = top
-        big = assemble_late(g1, g2, late)
-        return assemble_last(to_replicas(last.total), g), big
+        self.token = last.total[:1]
+        following.advance()
+        following.add()
+        top.add()
+        big = assemble_late((*top.parts, following.parts[0]), late)
+        return assemble_last(to_replicas(last.total), following.parts[1:]), big
 
 
 def to_replicas(value):
@@ -1279,14 +1314,16 @@
     return copies
 
 
-def late_kernel(flow, g1_ref, g2_ref, *refs):
+def late_kernel(flow, low_ref, high_ref, g1_ref, *refs):
     held, sem = refs[6:]
     fc1_ref, fc2_ref = refs[4:6]
     copies = load_replicas(refs[:4], held, sem)
     width = fc2_ref.shape[2]
     span = g1_ref.shape[1]
-    flow.need(g1_ref, g2_ref)
-    fc2_ref[1] = g2_ref[...].astype(F32)
+    flow.need(low_ref, high_ref, g1_ref)
+    half = low_ref.shape[0]
+    fc2_ref[1, :half] = low_ref[...].astype(F32)
+    fc2_ref[1, half:] = high_ref[...].astype(F32)
     for block in range(4):
         fc1_ref[1, :, block * width : (block + 1) * width] = g1_ref[block].astype(F32)
     for copy in copies:
@@ -1296,10 +1333,10 @@
         fc2_ref[0, block * span : (block + 1) * span, :] = held[block, :span].astype(F32)
 
 
-def assemble_late(g1, g2, late):
-    _, span, width = g1.shape
+def assemble_late(top, late):
+    _, span, width = top[2].shape
     return call(
-        late_kernel, (g1, g2), Pieces(late),
+        late_kernel, top, Pieces(late),
         [shape((LAYERS, span, 4 * width), F32), shape((LAYERS, 4 * span, width), F32)],
         [pltpu.VMEM((4, *late[0].shape), BF16), pltpu.SemaphoreType.DMA((4,))], 4,
     )
@@ -1319,17 +1356,15 @@
     span = g_ref.shape[1]
     flow.need(g_ref)
 
-    def put(layer, source):
-        for block in range(3):
-            qkv_ref[layer, :, block * width : (block + 1) * width] = source[
-                block, :span
-            ].astype(F32)
-        proj_ref[layer] = source[3, :span].astype(F32)
-
-    put(1, g_ref)
+    def put(layer, blocks):
+        for i, block in enumerate(blocks[:3]):
+            qkv_ref[layer, :, i * width : (i + 1) * width] = block.astype(F32)
+        proj_ref[layer] = blocks[3].astype(F32)
+
+    put(1, [g_ref[i] for i in range(4)])
     for copy in copies:
         copy.wait()
-    put(0, held)
+    put(0, [held[i, :span] for i in range(4)])
     unit = width // 8
     heads = held[0, span:].astype(F32)
     others = held[1, span:].astype(F32)
@@ -1345,14 +1380,14 @@
         rw[layer : layer + 1, :] = rel[2 * layer + 1 : 2 * layer + 2, :size]
 
 
-def assemble_last(last, g):
-    _, span, width = g.shape
+def assemble_last(last, parts):
+    _, span, width = parts[0].shape
     unit = width // 8
     sizes = (2 * unit, *[unit] * 5, 4 * unit, unit, RELS * HD // 8, RELS * HD // 8)
     outs = [shape((LAYERS, span, 3 * width), F32), shape((LAYERS, span, width), F32)]
     outs += [shape((LAYERS, size), F32) for size in sizes]
     return call(
-        last_kernel, (g,), Pieces(last), outs,
+        last_kernel, parts, Pieces(last), outs,
         [pltpu.VMEM((4, *last[0].shape), BF16), pltpu.SemaphoreType.DMA((4,))], 4,
     )
 
@@ -1386,14 +1421,14 @@
     sink.wait()
 
 
-def pack_riders(plan, sums):
+def pack_riders(plan, sums, after):
     resident = []
     width = sums[0][0].shape[1]
     for heads, hidden, rel in sums:
         resident += [heads, hidden, rel]
     return call(
         functools.partial(pack_kernel, plan), resident, Source(), [], [], 3,
-        [plan.sink_outs((32, RIDERS, width))],
+        [plan.sink_outs((32, RIDERS, width))], after,
     )
 
 
@@ -1404,12 +1439,17 @@
     def add(self, name, pair):
         self.pairs[name] = pair
 
-    def advance(self, *names):
+    def add_top(self, g2, g1, g):
+        self.top = whole_reduce(g, 1), whole_reduce(g1, 1), whole_reduce(g2, 0)
+
+    def advance(self, hold, *names):
         return ()
 
-    def finish(self, sums, top):
-        self.token = sums[0][0]
-        big = [named(*whole_sums((self.pairs["attend"], self.pairs["mlp"]))), named(*top)]
+    def finish(self, sums):
+        self.token = sums[0][0][:1]
+        big = [
+            named(*whole_sums((self.pairs["attend"], self.pairs["mlp"]))), named(*self.top)
+        ]
         shards = lax.axis_size("fsdp")
         parts = []
         for heads, hidden, rel in sums:
@@ -1492,10 +1532,10 @@
         kept.append((current, mid, h1, q, k, v, p, att, h2, act, slope))
         current = following
     sums = [None] * LAYERS
-    steps = {"scores_0": ("mlp",), "first_0": ("mlp",)}
-
-    def ahead_of(name):
-        return pending.advance(*steps.get(name, ()))
+    steps = {"middle_0": ("top",), "scores_0": ("top", "mlp"), "first_0": ("mlp",)}
+
+    def ahead_of(name, past):
+        return pending.advance(nothing(past.astype(F32)), *steps.get(name, ()))
 
     for layer in reversed(range(LAYERS)):
         top = layer == LAYERS - 1
@@ -1512,34 +1552,34 @@
             )
             pending.add("mlp", pair)
             dmid, sums2 = middle_backward(
-                grad, mid, vec[layer], dh, held.source(layer, "fc1"), ()
+                grad, mid, vec[layer], dh, held.source(layer, "fc1"), ahead_of("middle_0", sums3[0, 0])
             )
         db, dq, dk, dv, sums1, rel = scores_backward(
             dmid, live, back[layer], keys_back, q, k, v, p, held.source(layer, "proj"),
-            ahead_of(f"scores_{layer}"),
+            ahead_of(f"scores_{layer}", sums2[0, 0]),
         )
         if top:
             grad, sums4, top_g = first_all_backward(
                 whole, dmid, x, live, vec[layer], h1, att, db, dq, dk, dv,
                 held.source(layer, "attend"), (),
             )
-            top_sum = whole_sums(((top_g,), (top_g2, top_g1)))
+            pending.add_top(top_g2, top_g1, top_g)
         else:
             pair = weights_backward(plan, h1, att, db, dq, dk, dv, ())
             pending.add("attend", pair)
             grad, sums4 = first_backward(
                 dmid, x, live, vec[layer], dq, dk, dv, held.source(layer, "attend"),
-                ahead_of("first_0"),
+                ahead_of("first_0", pair[0][(0,) * pair[0].ndim]),
             )
         rel = rel[:, :HD] + rel[:, HD:]
         rel = jnp.stack([rel[:RELS].reshape(8, -1), rel[HD : HD + RELS].reshape(8, -1)], 1)
         sums[layer] = (sums1 + sums2 + sums3 + sums4, hsum, rel)
     input_grad = gather_back(grad).astype(BF16)
-    (qkv_grad, proj_grad, *small), (fc1_grad, fc2_grad) = pending.finish(sums, top_sum)
+    (qkv_grad, proj_grad, *small), (fc1_grad, fc2_grad) = pending.finish(sums)
     output = gather_back(
         mlp_output(
             kept[-1][9], vec[-1], kept[-1][1], live, held.source(LAYERS - 1, "fc2"),
-            (pending.token.reshape(1, -1),),
+            (pending.token,),
         )
     ).astype(BF16)
     qv, pb, n1g, n1b, n2g, n2b, f1b, f2b, rh, rw = small

time: 489 us -> 464 us (0.949)
  waiting for transfers between devices: 155 us -> 94.3 us
  other arithmetic: 33.4 us -> 48 us
  starting transfers between devices: 44.1 us -> 57 us
  local copies, waits for them, and re-layouts: 32.6 us -> 37.7 us
    ppermute x48 -> x56, waiting for transfers between devices: 136 us -> 94.2 us  [permute(): lax.ppermute(value, axis, [(i, move(i)) for i in range({'rep': 4, 'fsdp':...]
    psum x1 -> x0, waiting for transfers between devices: 18.5 us -> none  [whole_reduce(): lax.psum(lax.psum_scatter(value, 'fsdp', scatter_dimension=axis, tiled=Tr...]
    ppermute x48 -> x56, starting transfers between devices: 43.4 us -> 56.1 us  [permute(): lax.ppermute(value, axis, [(i, move(i)) for i in range({'rep': 4, 'fsdp':...]
    add x3 -> x7, other arithmetic: 1.8 us -> 10.3 us  [the longest x3 4.19 us: advance(): self.parts = [part + jnp.asarray(hold, BF16) for part in self.parts]]
    convert_element_type x6 -> x13, other arithmetic: 12.4 us -> 16.4 us  [the longest x8 8.63 us: add(): (part.astype(F32) + got.astype(F32) + hold).astype(BF16)]
  transfers between devices with their start and end apart: 55 -> 62, of which waited for: 22 -> 20; matrix products, arithmetic and copies ran while one was open for 12% -> 17% of each run, Pallas kernels for 40% -> 43%
where the time goes in v4:
time: 464 us; the launch traced here: 455 us
  Pallas kernels  197 us (42%)
  waiting for transfers between devices  94.3 us (20%)
  starting transfers between devices  57 us (12%)
  other arithmetic  48 us (10%)
  local copies, waits for them, and re-layouts  37.7 us (8%)
  between operations  20.4 us (4%)
    pallas_call x16, Pallas kernels, call(): return run(*resident, *source.arrays, *after)  197 us
    ppermute x56, waiting for transfers between devices, permute(): lax.ppermute(value, axis, [(i, move(i)) for i in range({'rep': 4, 'fsdp':...  94.2 us
    ppermute x56, starting transfers between devices, permute(): lax.ppermute(value, axis, [(i, move(i)) for i in range({'rep': 4, 'fsdp':...  56.1 us
    unnamed x118, local copies, waits for them, and re-layouts  9.29 us
  transfers between devices with their start and end apart: 62, of which 20 were waited for; matrix products, arithmetic and copies ran while one was open for 17% of the time, Pallas kernels for 43%

profile of v4, /device:TPU:8, one launch (start us, length us, event | category | flops | bytes accessed | tf_op | source)
XLA Modules:
  0.0 454.7 jit_solution(13045635963600640923)
XLA Ops:
  17.0 17.1 %collective-permute-done.2 = bf16[1,200,768]{2,1,0:T(8,128)(2,1)S(1)} collective-permute-done((bf16[1,200,768]{2,1,0:T(8,128)(2,1)S(1)}, bf16[1,200,768]{2,1,0:T(8,128)(2,1)S(1)}, u32[]{:S(2)}, u32[]{:S(2)}) %collective-permute-start.2) | collective-permute-done | bytes 307232 | tf_op jit(solution)/shard_map/ppermute | solution.py:1028
  34.1 5.7 %collective-permute-done = bf16[1,200,768]{2,1,0:T(8,128)(2,1)S(1)} collective-permute-done((bf16[1,200,768]{2,1,0:T(8,128)(2,1)S(1)}, bf16[1,200,768]{2,1,0:T(8,128)(2,1)S(1)}, u32[]{:S(2)}, u32[]{:S(2)}) %collective-permute-start) | collective-permute-done | bytes 307232 | tf_op jit(solution)/shard_map/ppermute | solution.py:1028
  47.5 20.9 %collective-permute-done.6.refs_7_.refs_6_.refs_10_.refs_9_ = bf16[4,200,768]{2,1,0:T(8,128)(2,1)} collective-permute-done((bf16[4,200,768]{2,1,0:T(8,128)(2,1)S(1)}, bf16[4,200,768]{2,1,0:T(8,128)(2,1)}, u32[]{:S(2)}, u32[]{:S(2)}) %collective-permute-start.6) | collective-permute-done | bytes 1228832 | tf_op jit(solution)/shard_map/ppermute | solution.py:1028
  80.7 3.9 collective-permute-done.8.refs_8_.refs_7_.refs_11_.refs_10_
  98.5 17.4 %shard_map.306 = (f32[448,768]{1,0:T(8,128)}, bf16[448,768]{1,0:T(8,128)(2,1)}, bf16[448,768]{1,0:T(8,128)(2,1)}, bf16[448,768]{1,0:T(8,128)(2,1)}, bf16[448,768...) custom-call(bf16[448,768]{1,0:T(8,128)(2,1)} %bitcast.153, ...), custom_call_target="tpu_custom_call" | custom-call | flops 199999995904 | bytes 1048576 | tf_op jit(solution)/shard_map/pallas_call | solution.py:815
  127.5 7.2 %collective-permute-done.14.refs_17_.refs_8_.refs_11_.refs_13_ = bf16[2,192,768]{2,1,0:T(8,128)(2,1)} collective-permute-done((bf16[2,192,768]{2,1,0:T(8,128)(2,1)S(1)}, bf16[2,192,768]{2,1,0:T(8,128)(2,1)}, u32[]{:S(2)}, u32[]{:S(2)}) %collective-permute-start.14) | collective-permute-done | bytes 589856 | tf_op jit(solution)/shard_map/ppermute | solution.py:1028
  141.2 15.1 %shard_map.307 = (f32[448,768]{1,0:T(8,128)}, bf16[448,768]{1,0:T(8,128)(2,1)}, bf16[448,3072]{1,0:T(8,128)(2,1)}, bf16[448,3072]{1,0:T(8,128)(2,1)}) custom-call(f32[448,768]{1,0:T(8,128)} %get-tuple-element.86.refs_0_.refs_1_, f32[448,1]{1,0:T(8,128)} %reshape.331.refs_1_.refs_2_.refs_3_, f32[8,768]{1,0:T(8,128)} %get-tuple-element.207.refs_2_.refs_3_, ...), custom_call_target="tpu_custom_call" | custom-call | flops 160000000000 | bytes 1048576 | tf_op jit(solution)/shard_map/pallas_call | solution.py:815
  156.2 17.7 %shard_map.308 = (f32[448,768]{1,0:T(8,128)}, bf16[448,768]{1,0:T(8,128)(2,1)}, bf16[448,768]{1,0:T(8,128)(2,1)}, bf16[448,768]{1,0:T(8,128)(2,1)}, bf16[448,768...) custom-call(f32[448,768]{1,0:T(8,128)} %get-tuple-element.88.refs_0_.refs_1_, ...), custom_call_target="tpu_custom_call" | custom-call | flops 199999995904 | bytes 1048576 | tf_op jit(solution)/shard_map/pallas_call | solution.py:815
  173.9 15.9 %shard_map.309 = (bf16[448,768]{1,0:T(8,128)(2,1)}, bf16[448,3072]{1,0:T(8,128)(2,1)}, bf16[448,3072]{1,0:T(8,128)(2,1)}, f32[8,768]{1,0:T(8,128)}, bf16[3072,768]{1,0:T(8,128)(2,1)}) custom-call(f32[448,768]{1,0:T(8,128)} %get-tuple-element.89.refs_0_.refs_1_.refs_2_, f32[448,1]{1,0:T(8,128)} %reshape.331.refs_1_.refs_2_.refs_3_, ...), custom_call_target="tpu_custom_call" | custom-call | flops 160000000000 | bytes 1048576 | tf_op jit(solution)/shard_map/pallas_call | solution.py:815
  190.4 19.6 %shard_map.310 = (f32[448,768]{1,0:T(8,128)}, f32[8,768]{1,0:T(8,128)}, f32[1,3072]{1,0:T(1,128)}, bf16[4,768,768]{2,1,0:T(8,128)(2,1)}) custom-call(bf16[448,768]{1,0:T(8,128)(2,1)} %bitcast.156, f32[448,768]{1,0:T(8,128)} %get-tuple-element.89.refs_0_.refs_1_.refs_2_, f32[448,1]{1,0:T(8,128)} %reshape.331.refs_1_.refs_2_.refs_3_, ...), custom_call_target="tpu_custom_call" | custom-call | flops 190000005120 | bytes 1048576 | tf_op jit(solution)/shard_map/pallas_call | solution.py:815
  210.0 15.4 %shard_map.311 = (bf16[448,768]{1,0:T(8,128)(2,1)}, bf16[448,768]{1,0:T(8,128)(2,1)}, bf16[448,768]{1,0:T(8,128)(2,1)}, bf16[448,768]{1,0:T(8,128)(2,1)}, f32[8,768]{1,0:T(8,128)}, /*index=5*/f32[128,128]{1,0:T(8,128)}) custom-call(f32[448,768]{1,0:T(8,128)} %get-tuple-element.95.refs_0_, f32[448,1]{1,0:T(8,128)} %reshape.331.refs_1_.refs_2_.refs_3_, ...), custom_call_target="tpu_custom_call" | custom-call | flops 149999992832 | bytes 1048576 | tf_op jit(solution)/shard_map/pallas_call | solution.py:815
  227.9 15.9 %shard_map.312 = (f32[448,768]{1,0:T(8,128)}, f32[8,768]{1,0:T(8,128)}, bf16[4,768,768]{2,1,0:T(8,128)(2,1)}) custom-call(f32[448,768]{1,0:T(8,128)} %get-tuple-element.95.refs_0_, f32[448,768]{1,0:T(8,128)} %get-tuple-element.88.refs_0_.refs_1_, f32[448,1]{1,0:T(8,128)} %reshape.331.refs_1_.refs_2_.refs_3_, ...), custom_call_target="tpu_custom_call" | custom-call | flops 140000002048 | bytes 1048576 | tf_op jit(solution)/shard_map/pallas_call | solution.py:815
  243.8 17.6 %shard_map.313 = (bf16[448,3072]{1,0:T(8,128)(2,1)}, f32[8,768]{1,0:T(8,128)}, f32[1,3072]{1,0:T(1,128)}, bf16[4,4,192,768]{3,2,1,0:T(8,128)(2,1)}, bf16[4,4,192,768]{3,2,1,0:T(8,128)(2,1)}) custom-call(f32[448,768]{1,0:T(8,128)} %get-tuple-element.106.refs_0_, bf16[448,3072]{1,0:T(8,128)(2,1)} %get-tuple-element.107.refs_1_, ...), custom_call_target="tpu_custom_call" | custom-call | flops 179999997952 | bytes 1048576 | tf_op jit(solution)/shard_map/pallas_call | solution.py:815
  269.1 12.1 %shard_map.314 = (f32[448,768]{1,0:T(8,128)}, f32[8,768]{1,0:T(8,128)}) custom-call(f32[448,768]{1,0:T(8,128)} %get-tuple-element.106.refs_0_, f32[448,768]{1,0:T(8,128)} %get-tuple-element.86.refs_0_.refs_1_, f32[8,768]{1,0:T(8,128)} %get-tuple-element.207.refs_2_.refs_3_, bf16[448,3072]{1,0:T(8,128)(2,1)} %get-tuple-element.110.refs_3_, ...), custom_call_target="tpu_custom_call" | custom-call | flops 99999997952 | bytes 1048576 | tf_op jit(solution)/shard_map/pallas_call | solution.py:815
  283.1 3.8 add_convert_fusion
  292.7 15.4 %shard_map.315 = (bf16[448,768]{1,0:T(8,128)(2,1)}, bf16[448,768]{1,0:T(8,128)(2,1)}, bf16[448,768]{1,0:T(8,128)(2,1)}, bf16[448,768]{1,0:T(8,128)(2,1)}, f32[8,768]{1,0:T(8,128)}, /*index=5*/f32[128,128]{1,0:T(8,128)}) custom-call(f32[448,768]{1,0:T(8,128)} %get-tuple-element.113.refs_0_, f32[448,1]{1,0:T(8,128)} %reshape.331.refs_1_.refs_2_.refs_3_, ...), custom_call_target="tpu_custom_call" | custom-call | flops 149999992832 | bytes 1048576 | tf_op jit(solution)/shard_map/pallas_call | solution.py:815
  308.1 7.3 %shard_map.316 = (bf16[4,4,96,768]{3,2,1,0:T(8,128)(2,1)}, bf16[4,4,96,768]{3,2,1,0:T(8,128)(2,1)}) custom-call(bf16[448,768]{1,0:T(8,128)(2,1)} %get-tuple-element.91.refs_0_, bf16[448,768]{1,0:T(8,128)(2,1)} %get-tuple-element.92.refs_1_, bf16[448,768]{1,0:T(8,128)(2,1)} %get-tuple-element.121.refs_2_, ...), custom_call_target="tpu_custom_call" | custom-call | flops 80000000000 | bytes 1048576 | tf_op jit(solution)/shard_map/pallas_call | solution.py:815
  329.8 10.6 %shard_map.317 = (f32[448,768]{1,0:T(8,128)}, f32[8,768]{1,0:T(8,128)}) custom-call(f32[448,768]{1,0:T(8,128)} %get-tuple-element.113.refs_0_, bf16[448,768]{1,0:T(8,128)(2,1)} %bitcast.154, f32[448,1]{1,0:T(8,128)} %reshape.331.refs_1_.refs_2_.refs_3_, f32[8,768]{1,0:T(8,128)} %get-tuple-element.207.refs_2_.refs_3_, ...), custom_call_target="tpu_custom_call" | custom-call | flops 99999997952 | bytes 1048576 | tf_op jit(solution)/shard_map/pallas_call | solution.py:815
  361.8 9.0 %collective-permute-done.33 = bf16[2,8,768]{2,1,0:T(8,128)(2,1)S(1)} collective-permute-done((bf16[2,8,768]{2,1,0:T(8,128)(2,1)S(1)}, bf16[2,8,768]{2,1,0:T(8,128)(2,1)S(1)}, u32[]{:S(2)}, u32[]{:S(2)}) %collective-permute-start.33) | collective-permute-done | bytes 24608 | tf_op jit(solution)/shard_map/ppermute | solution.py:1028
  370.8 3.6 collective-permute-start.52
  397.5 4.1 collective-permute-done.34
  409.2 8.0 %shard_map.319 = f32[448,768]{1,0:T(8,128)} custom-call(bf16[448,3072]{1,0:T(8,128)(2,1)} %get-tuple-element.90.refs_0_, f32[8,768]{1,0:T(8,128)} %get-tuple-element.206.refs_2_.refs_3_.refs_1_, f32[448,768]{1,0:T(8,128)} %get-tuple-element.89.refs_0_.refs_1_.refs_2_, f32[448,1]{1,0:T(8,128)} %reshape.331.refs_1_.refs_2_.refs_3_, ...), custom_call_target="tpu_custom_call" | custom-call | flops 49999998976 | bytes 1048576 | tf_op jit(solution)/shard_map/pallas_call | solution.py:815
  436.0 5.0 %collective-permute-done.49 = bf16[4,96,768]{2,1,0:T(8,128)(2,1)S(1)} collective-permute-done((bf16[4,96,768]{2,1,0:T(8,128)(2,1)S(1)}, bf16[4,96,768]{2,1,0:T(8,128)(2,1)S(1)}, u32[]{:S(2)}, u32[]{:S(2)}) %collective-permute-start.49) | collective-permute-done | bytes 589856 | tf_op jit(solution)/shard_map/ppermute | solution.py:1028
  443.5 3.9 shard_map.321
  (386 shorter events, 162.1 us)
Async XLA Ops:
  7.2 70.2 %all-gather.6.cloned.1.call-start = ((), (), s32[]{:S(2)}) async-start(), calls=%async_computation.3 | async-start | bytes 1474560 | tf_op jit(solution)/shard_map/all_gather | solution.py:1119
  10.7 23.4 %collective-permute-start.2 = (bf16[1,200,768]{2,1,0:T(8,128)(2,1)S(1)}, bf16[1,200,768]{2,1,0:T(8,128)(2,1)S(1)}, u32[]{:S(2)}, u32[]{:S(2)}) collective-permute-start(bf16[1,200,768]{2,1,0:T(8,128)(2,1)S(1)} %maximum_bitcast_fusion), channel_id=1, source_target_pairs={{0,6},{1,7},{2,0},{3,1},{4,2},{5,3},{6,4},{7,5},{8,14},{9,15},{10,... | collective-permute-start | bytes 921608 | tf_op jit(solution)/shard_map/ppermute | solution.py:1028
  10.7 23.4 %collective-permute-start.1 = (bf16[1,200,768]{2,1,0:T(8,128)(2,1)S(1)}, bf16[1,200,768]{2,1,0:T(8,128)(2,1)S(1)}, u32[]{:S(2)}, u32[]{:S(2)}) collective-permute-start(bf16[1,200,768]{2,1,0:T(8,128)(2,1)S(1)} %maximum_bitcast_fusion), channel_id=1, source_target_pairs={{0,4},{1,5},{2,6},{3,7},{4,0},{5,1},{6,2},{7,3},{8,12},{9,13},{10,... | collective-permute-start | bytes 921608 | tf_op jit(solution)/shard_map/ppermute | solution.py:1028
  13.8 26.0 %collective-permute-start = (bf16[1,200,768]{2,1,0:T(8,128)(2,1)S(1)}, bf16[1,200,768]{2,1,0:T(8,128)(2,1)S(1)}, u32[]{:S(2)}, u32[]{:S(2)}) collective-permute-start(bf16[1,200,768]{2,1,0:T(8,128)(2,1)S(1)} %maximum_bitcast_fusion), channel_id=1, source_target_pairs={{0,2},{1,3},{2,4},{3,5},{4,6},{5,7},{6,0},{7,1},{8,10},{9,11},{10,... | collective-permute-start | bytes 921608 | tf_op jit(solution)/shard_map/ppermute | solution.py:1028
  40.0 28.3 %collective-permute-start.6 = (bf16[4,200,768]{2,1,0:T(8,128)(2,1)S(1)}, bf16[4,200,768]{2,1,0:T(8,128)(2,1)}, u32[]{:S(2)}, u32[]{:S(2)}) collective-permute-start(bf16[4,200,768]{2,1,0:T(8,128)(2,1)S(1)} %pad_maximum_fusion.refs_5_.refs_4_.refs_8_.refs_7_), channel_id=1, source_target_pairs={{0,16},{8,24},{16,0},{24,8},{1,17},{9,25},{17,1},{25,9},{2,18},{10... | collective-permute-start | bytes 3686408 | tf_op jit(solution)/shard_map/ppermute | solution.py:1028
  41.6 30.2 %collective-permute-start.4 = (bf16[4,200,768]{2,1,0:T(8,128)(2,1)S(1)}, bf16[4,200,768]{2,1,0:T(8,128)(2,1)}, u32[]{:S(2)}, u32[]{:S(2)}) collective-permute-start(bf16[4,200,768]{2,1,0:T(8,128)(2,1)S(1)} %pad_maximum_fusion.refs_5_.refs_4_.refs_8_.refs_7_), channel_id=1, source_target_pairs={{0,8},{8,0},{16,24},{24,16},{1,9},{9,1},{17,25},{25,17},{2,10},{10... | collective-permute-start | bytes 3686408 | tf_op jit(solution)/shard_map/ppermute | solution.py:1028
  45.1 128.8 %all-gather.8.cloned.1.call-start = ((), (), s32[]{:S(2)}) async-start(), calls=%async_computation.7 | async-start | bytes 5308416 | tf_op jit(solution)/shard_map/all_gather | solution.py:1123
  45.3 31.3 %collective-permute-start.3 = (bf16[4,200,768]{2,1,0:T(8,128)(2,1)S(1)}, bf16[4,200,768]{2,1,0:T(8,128)(2,1)}, u32[]{:S(2)}, u32[]{:S(2)}) collective-permute-start(bf16[4,200,768]{2,1,0:T(8,128)(2,1)S(1)} %pad_maximum_fusion.refs_5_.refs_4_.refs_8_.refs_7_), channel_id=1, source_target_pairs={{0,1},{1,0},{2,3},{3,2},{4,5},{5,4},{6,7},{7,6},{8,9},{9,8},{10,11... | collective-permute-start | bytes 3686408 | tf_op jit(solution)/shard_map/ppermute | solution.py:1028
  78.6 38.5 %collective-permute-start.13 = (bf16[4,192,768]{2,1,0:T(8,128)(2,1)}, bf16[4,192,768]{2,1,0:T(8,128)(2,1)}, u32[]{:S(2)}, u32[]{:S(2)}) collective-permute-start(bf16[4,192,768]{2,1,0:T(8,128)(2,1)} %bitcast.26.refs_15_.refs_14_.refs_5_.refs_8_.refs_10_), channel_id=1, source_target_pairs={{0,16},{8,24},{16,0},{24,8},{1,17},{9,25},{17,1},{25,9},{2,18},{10... | collective-permute-start | bytes 3538952 | tf_op jit(solution)/shard_map/ppermute | solution.py:1028
  80.7 109.7 %all-gather.10.cloned.1.call-start = ((), (), s32[]{:S(2)}) async-start(), calls=%async_computation.8 | async-start | bytes 5308416 | tf_op jit(solution)/shard_map/all_gather | solution.py:1155
  84.6 35.3 %collective-permute-start.12 = (bf16[4,192,768]{2,1,0:T(8,128)(2,1)}, bf16[4,192,768]{2,1,0:T(8,128)(2,1)}, u32[]{:S(2)}, u32[]{:S(2)}) collective-permute-start(bf16[4,192,768]{2,1,0:T(8,128)(2,1)} %bitcast.26.refs_15_.refs_14_.refs_5_.refs_8_.refs_10_), channel_id=1, source_target_pairs={{0,8},{8,0},{16,24},{24,16},{1,9},{9,1},{17,25},{25,17},{2,10},{10... | collective-permute-start | bytes 3538952 | tf_op jit(solution)/shard_map/ppermute | solution.py:1028
  127.3 138.5 %reduce-scatter.4.cloned.1.call-start = ((), (), s32[]{:S(2)}) async-start(), calls=%async_computation.4 | async-start | bytes 5308416 | tf_op jit(solution)/shard_map/reduce_scatter | solution.py:1263
  189.9 191.9 %reduce-scatter.8.cloned.1.call-start = ((), (), s32[]{:S(2)}) async-start(), calls=%async_computation.6 | async-start | bytes 5308416 | tf_op jit(solution)/shard_map/reduce_scatter | solution.py:1264
  227.8 156.0 %reduce-scatter.6.cloned.1.call-start = ((), (), s32[]{:S(2)}) async-start(), calls=%async_computation.5 | async-start | bytes 5308416 | tf_op jit(solution)/shard_map/reduce_scatter | solution.py:1265
  287.0 38.1 %collective-permute-start.27 = (bf16[2,2,192,768]{3,2,1,0:T(8,128)(2,1)}, bf16[2,2,192,768]{3,2,1,0:T(8,128)(2,1)}, u32[]{:S(2)}, u32[]{:S(2)}) collective-permute-start(bf16[2,2,192,768]{3,2,1,0:T(8,128)(2,1)} %get-tuple-element.162.refs_21_), channel_id=1, source_target_pairs={{0,16},{8,24},{16,0},{24,8},{1,17},{9,25},{17,1},{25,9},{2,18},{10... | collective-permute-start | bytes 3538952 | tf_op jit(solution)/shard_map/ppermute | solution.py:1028
  287.5 37.6 %collective-permute-start.28 = (bf16[2,2,192,768]{3,2,1,0:T(8,128)(2,1)}, bf16[2,2,192,768]{3,2,1,0:T(8,128)(2,1)}, u32[]{:S(2)}, u32[]{:S(2)}) collective-permute-start(bf16[2,2,192,768]{3,2,1,0:T(8,128)(2,1)} %get-tuple-element.163.refs_20_), channel_id=1, source_target_pairs={{0,8},{8,0},{16,24},{24,16},{1,9},{9,1},{17,25},{25,17},{2,10},{10... | collective-permute-start | bytes 3538952 | tf_op jit(solution)/shard_map/ppermute | solution.py:1028
  289.6 31.8 %collective-permute-start.47 = (bf16[192,768]{1,0:T(8,128)(2,1)}, bf16[192,768]{1,0:T(8,128)(2,1)}, u32[]{:S(2)}, u32[]{:S(2)}) collective-permute-start(bf16[192,768]{1,0:T(8,128)(2,1)} %add_convert_fusion.14.refs_19_), channel_id=1, source_target_pairs={{0,8},{8,0},{16,24},{24,16},{1,9},{9,1},{17,25},{25,17},{2,10},{10... | collective-permute-start | bytes 884744 | tf_op jit(solution)/shard_map/ppermute | solution.py:1028
  291.1 32.1 %collective-permute-start.46 = (bf16[192,768]{1,0:T(8,128)(2,1)}, bf16[192,768]{1,0:T(8,128)(2,1)}, u32[]{:S(2)}, u32[]{:S(2)}) collective-permute-start(bf16[192,768]{1,0:T(8,128)(2,1)} %add_convert_fusion.15.refs_18_), channel_id=1, source_target_pairs={{0,16},{8,24},{16,0},{24,8},{1,17},{9,25},{17,1},{25,9},{2,18},{10... | collective-permute-start | bytes 884744 | tf_op jit(solution)/shard_map/ppermute | solution.py:1028
  315.7 37.3 %collective-permute-start.24 = (bf16[4,4,96,768]{3,2,1,0:T(8,128)(2,1)}, bf16[4,4,96,768]{3,2,1,0:T(8,128)(2,1)}, u32[]{:S(2)}, u32[]{:S(2)}) collective-permute-start(bf16[4,4,96,768]{3,2,1,0:T(8,128)(2,1)} %get-tuple-element.126), channel_id=1, source_target_pairs={{0,1},{1,0},{2,3},{3,2},{4,5},{5,4},{6,7},{7,6},{8,9},{9,8},{10,11... | collective-permute-start | bytes 7077896 | tf_op jit(solution)/shard_map/ppermute | solution.py:1028
  359.5 33.2 %collective-permute-start.50 = (bf16[192,768]{1,0:T(8,128)(2,1)}, bf16[192,768]{1,0:T(8,128)(2,1)}, u32[]{:S(2)}, u32[]{:S(2)}) collective-permute-start(bf16[192,768]{1,0:T(8,128)(2,1)} %slice_bitcast_fusion.4), channel_id=1, source_target_pairs={{0,2},{1,3},{2,4},{3,5},{4,6},{5,7},{6,0},{7,1},{8,10},{9,11},{10,... | collective-permute-start | bytes 884744 | tf_op jit(solution)/shard_map/ppermute | solution.py:1028
  370.8 25.1 %collective-permute-start.52 = (bf16[192,768]{1,0:T(8,128)(2,1)}, bf16[192,768]{1,0:T(8,128)(2,1)}, u32[]{:S(2)}, u32[]{:S(2)}) collective-permute-start(bf16[192,768]{1,0:T(8,128)(2,1)} %get-tuple-element.173), channel_id=1, source_target_pairs={{0,6},{1,7},{2,0},{3,1},{4,2},{5,3},{6,4},{7,5},{8,14},{9,15},{10,... | collective-permute-start | bytes 884744 | tf_op jit(solution)/shard_map/ppermute | solution.py:1028
  389.4 30.2 %collective-permute-start.48 = (bf16[4,96,768]{2,1,0:T(8,128)(2,1)}, bf16[4,96,768]{2,1,0:T(8,128)(2,1)}, u32[]{:S(2)}, u32[]{:S(2)}) collective-permute-start(bf16[4,96,768]{2,1,0:T(8,128)(2,1)} %broadcast_add_fusion), channel_id=1, source_target_pairs={{0,8},{8,0},{16,24},{24,16},{1,9},{9,1},{17,25},{25,17},{2,10},{10... | collective-permute-start | bytes 1769480 | tf_op jit(solution)/shard_map/ppermute | solution.py:1028
  401.6 40.3 %collective-permute-start.55 = (bf16[192,768]{1,0:T(8,128)(2,1)S(1)}, bf16[192,768]{1,0:T(8,128)(2,1)S(1)}, u32[]{:S(2)}, u32[]{:S(2)}) collective-permute-start(bf16[192,768]{1,0:T(8,128)(2,1)S(1)} %fusion.14.refs_3_), channel_id=1, source_target_pairs={{0,24},{8,16},{16,8},{24,0},{1,25},{9,17},{17,9},{25,1},{2,26},{10... | collective-permute-start | bytes 884744 | tf_op jit(solution)/shard_map/ppermute | solution.py:1028
  403.3 38.6 %collective-permute-start.54 = (bf16[192,768]{1,0:T(8,128)(2,1)S(1)}, bf16[192,768]{1,0:T(8,128)(2,1)S(1)}, u32[]{:S(2)}, u32[]{:S(2)}) collective-permute-start(bf16[192,768]{1,0:T(8,128)(2,1)S(1)} %fusion.14.refs_3_), channel_id=1, source_target_pairs={{0,16},{8,24},{16,0},{24,8},{1,17},{9,25},{17,1},{25,9},{2,18},{10... | collective-permute-start | bytes 884744 | tf_op jit(solution)/shard_map/ppermute | solution.py:1028
  (90 other events, 838.7 us)
Sparse Core Ops, SparseCore 0:
  45.3 29.0 all-gather.5
  80.8 50.2 all-gather.7
  133.3 50.5 all-gather.9
  190.0 52.4 reduce-scatter.3
  244.7 53.0 reduce-scatter.7
  300.0 53.6 reduce-scatter.5
